TPU v7x, 32 devices: a whole 2x2x4 slice. The times are simulated.
32 devices in a mesh: fsdp: 8 (over y, x, core), tp: 4 (over z).
Axes of the slice: x: 2, y: 2, z: 4, core: 2. Of those that a mesh axis runs over, the one named last changes fastest.
Arguments:
- inputs: bfloat16 [8192, 2048], P(('fsdp', 'tp')), may hold values from -6 to 6
- query_weight: bfloat16 [2048, 2048], P('fsdp', 'tp'), may hold values from -0.125 to 0.125
- query_bias: float32 [2048], P('tp'), may hold values from -3 to 3
- key_weight: bfloat16 [2048, 2048], P('fsdp', 'tp'), may hold values from -0.125 to 0.125
- value_weight: bfloat16 [2048, 2048], P('fsdp', 'tp'), may hold values from -0.125 to 0.125
- value_bias: float32 [2048], P('tp'), may hold values from -3 to 3
- output_weight: bfloat16 [2048, 2048], P('tp', 'fsdp'), may hold values from -0.75 to 0.75
- output_bias: float32 [2048], replicated, may hold values from -3 to 3
- first_gain: float32 [2048], replicated, may hold values from 0.5 to 1.5
- first_shift: float32 [2048], replicated, may hold values from -3 to 3
- up_weight: bfloat16 [2048, 8192], P('fsdp', 'tp'), may hold values from -0.125 to 0.125
- up_bias: float32 [8192], P('tp'), may hold values from -3 to 3
- down_weight: bfloat16 [8192, 2048], P('tp', 'fsdp'), may hold values from -0.125 to 0.125
- down_bias: float32 [2048], replicated, may hold values from -3 to 3
- second_gain: float32 [2048], replicated, may hold values from 0.5 to 1.5
- second_shift: float32 [2048], replicated, may hold values from -3 to 3
- segments: int32 [8, 1024], P('fsdp'), may hold values from 0 to 7, never falling along the last dimension, each value on 1 to 512 neighbouring positions
- cotangent: bfloat16 [8192, 2048], P(('fsdp', 'tp')), may hold values from -6 to 6
Outputs:
- layer_out: bfloat16 [8192, 2048], P(('fsdp', 'tp'))
- input_grad: bfloat16 [8192, 2048], P(('fsdp', 'tp'))
- query_weight_grad: float32 [2048, 2048], P('fsdp', 'tp')
- query_bias_grad: float32 [4, 512], P('tp', 'fsdp')
- key_weight_grad: float32 [2048, 2048], P('fsdp', 'tp')
- value_weight_grad: float32 [2048, 2048], P('fsdp', 'tp')
- value_bias_grad: float32 [4, 512], P('tp', 'fsdp')
- output_weight_grad: float32 [2048, 2048], P('tp', 'fsdp')
- output_bias_grad: float32 [2048], P(('fsdp', 'tp'))
- first_gain_grad: float32 [2048], P(('fsdp', 'tp'))
- first_shift_grad: float32 [2048], P(('fsdp', 'tp'))
- up_weight_grad: float32 [2048, 8192], P('fsdp', 'tp')
- up_bias_grad: float32 [4, 2048], P('tp', 'fsdp')
- down_weight_grad: float32 [8192, 2048], P('tp', 'fsdp')
- down_bias_grad: float32 [2048], P(('fsdp', 'tp'))
- second_gain_grad: float32 [2048], P(('fsdp', 'tp'))
- second_shift_grad: float32 [2048], P(('fsdp', 'tp'))
Inputs may be any that keep to these rules, and one draw needn't show every extreme that they name: `segments`: within a sequence the numbers never fall; one number marks one document of 1 to 512 tokens, and one document of each sequence has exactly 512.
All inputs are finite; a program needn't handle non-finite values.
Results may differ from a plain program's by a relative error of at most 0.019.
Values may be sent and summed in bfloat16 or wider, within the bound.
A program may use at most 192 MiB of HBM per device.

v0:
```python
import jax
import jax.numpy as jnp
from jax import lax
from jax.sharding import PartitionSpec as P

HD = 128


EPS = 1e-06
NEG = -1000000000.0


def project(left, right):
    return jnp.dot(left, right, preferred_element_type=jnp.float32)


def against(left, right):
    return lax.dot_general(
        left, right, (((1,), (1,)), ((), ())), preferred_element_type=jnp.float32
    )


def across(left, right):
    return lax.dot_general(
        left, right, (((0,), (0,)), ((), ())), preferred_element_type=jnp.float32
    )


def normalize(total, gain, shift):
    center = total - jnp.mean(total, axis=-1, keepdims=True)
    spread = jnp.mean(center * center, axis=-1, keepdims=True)
    scale_inv = lax.rsqrt(spread + EPS)
    normed = center * scale_inv
    return (normed * gain + shift, normed, scale_inv)


def norm_back(grad, normed, scale_inv, gain):
    scaled = grad * gain
    inner = (
        scaled
        - jnp.mean(scaled, axis=-1, keepdims=True)
        - normed * jnp.mean(scaled * normed, axis=-1, keepdims=True)
    )
    return (scale_inv * inner, jnp.sum(grad * normed, axis=0), jnp.sum(grad, axis=0))


def gelu_tanh(values):
    return jax.nn.gelu(values, approximate=True)


def scores_of(queries, keys, labels):
    scores = jnp.einsum("qhd,khd->hqk", queries, keys, preferred_element_type=jnp.float32) * HD ** (
        -0.5
    )
    same = labels[:, None] == labels[None, :]
    return jnp.where(same[None], scores, NEG)


def attend(pieces):
    queries, keys, values, labels = pieces
    scores = scores_of(queries, keys, labels)
    top = jnp.max(scores, axis=-1, keepdims=True)
    weights = jnp.exp(scores - top)
    total = jnp.sum(weights, axis=-1, keepdims=True)
    probs = (weights / total).astype(jnp.bfloat16)
    context = jnp.einsum("hqk,khd->qhd", probs, values, preferred_element_type=jnp.float32).astype(
        jnp.bfloat16
    )
    return (context, top[..., 0] + jnp.log(total[..., 0]))


def attend_back(pieces):
    queries, keys, values, d_context, log_total, labels = pieces
    probs = jnp.exp(scores_of(queries, keys, labels) - log_total[..., None])
    probs_low = probs.astype(jnp.bfloat16)
    d_value = jnp.einsum(
        "hqk,qhd->khd", probs_low, d_context, preferred_element_type=jnp.float32
    ).astype(jnp.bfloat16)
    d_probs = jnp.einsum("qhd,khd->hqk", d_context, values, preferred_element_type=jnp.float32)
    d_scores = (probs * (d_probs - jnp.sum(probs * d_probs, axis=-1, keepdims=True))).astype(
        jnp.bfloat16
    )
    d_query = (
        jnp.einsum("hqk,khd->qhd", d_scores, keys, preferred_element_type=jnp.float32)
        * HD ** (-0.5)
    ).astype(jnp.bfloat16)
    d_key = (
        jnp.einsum("hqk,qhd->khd", d_scores, queries, preferred_element_type=jnp.float32)
        * HD ** (-0.5)
    ).astype(jnp.bfloat16)
    return (d_query, d_key, d_value)


def collect_inner(query_weight, key_weight, value_weight, up_weight):
    return (
        lax.all_gather(query_weight, "fsdp", axis=0, tiled=True),
        lax.all_gather(key_weight, "fsdp", axis=0, tiled=True),
        lax.all_gather(value_weight, "fsdp", axis=0, tiled=True),
        lax.all_gather(up_weight, "fsdp", axis=0, tiled=True),
    )


def collect_outer(output_weight, down_weight):
    return (
        lax.all_gather(output_weight, "fsdp", axis=1, tiled=True),
        lax.all_gather(down_weight, "fsdp", axis=1, tiled=True),
    )


def shards(
    inputs,
    query_weight,
    query_bias,
    key_weight,
    value_weight,
    value_bias,
    output_weight,
    output_bias,
    first_gain,
    first_shift,
    up_weight,
    up_bias,
    down_weight,
    down_bias,
    second_gain,
    second_shift,
    segments,
    cotangent,
):
    number, length = segments.shape
    local = query_weight.shape[1] // HD

    def heads(table):
        return table.reshape(number, length, local, HD)

    rows_all = lax.all_gather(inputs, "tp", axis=0, tiled=True)
    inner = collect_inner(query_weight, key_weight, value_weight, up_weight)
    outer = collect_outer(output_weight, down_weight)
    query = (project(rows_all, inner[0]) + query_bias).astype(jnp.bfloat16)
    keys = project(rows_all, inner[1]).astype(jnp.bfloat16)
    value = (project(rows_all, inner[2]) + value_bias).astype(jnp.bfloat16)
    context, log_total = lax.map(attend, (heads(query), heads(keys), heads(value), segments))
    context = context.reshape(rows_all.shape[0], local * HD)
    attn = lax.psum_scatter(project(context, outer[0]), "tp", scatter_dimension=0, tiled=True)
    first_sum = inputs.astype(jnp.float32) + attn + output_bias
    first_out, first_normed, first_inv = normalize(first_sum, first_gain, first_shift)
    mid_all = lax.all_gather(first_out.astype(jnp.bfloat16), "tp", axis=0, tiled=True)
    pre = project(mid_all, inner[3]) + up_bias
    active, gelu_back = jax.vjp(gelu_tanh, pre)
    hidden = active.astype(jnp.bfloat16)
    ffn = lax.psum_scatter(project(hidden, outer[1]), "tp", scatter_dimension=0, tiled=True)
    second_sum = first_out + ffn + down_bias
    final, second_normed, second_inv = normalize(second_sum, second_gain, second_shift)
    layer_out = final.astype(jnp.bfloat16)
    fresh = lax.optimization_barrier(
        (query_weight, key_weight, value_weight, up_weight, output_weight, down_weight, layer_out)
    )
    query_full, key_full, value_full, up_full = collect_inner(
        fresh[0], fresh[1], fresh[2], fresh[3]
    )
    output_full, down_full = collect_outer(fresh[4], fresh[5])
    d_second, second_gain_term, second_shift_term = norm_back(
        cotangent.astype(jnp.float32), second_normed, second_inv, second_gain
    )
    down_bias_term = jnp.sum(d_second, axis=0)
    d_branch_all = lax.all_gather(d_second.astype(jnp.bfloat16), "tp", axis=0, tiled=True)
    down_term = across(hidden, d_branch_all)
    d_hidden = against(d_branch_all, down_full)
    d_pre = gelu_back(d_hidden)[0].astype(jnp.bfloat16)
    up_bias_term = jnp.sum(d_pre.astype(jnp.float32), axis=0)
    up_term = across(mid_all, d_pre)
    d_mid = lax.psum_scatter(against(d_pre, up_full), "tp", scatter_dimension=0, tiled=True)
    d_first = d_mid + d_second
    d_first_sum, first_gain_term, first_shift_term = norm_back(
        d_first, first_normed, first_inv, first_gain
    )
    output_bias_term = jnp.sum(d_first_sum, axis=0)
    d_attn_all = lax.all_gather(d_first_sum.astype(jnp.bfloat16), "tp", axis=0, tiled=True)
    output_term = across(context, d_attn_all)
    d_context = against(d_attn_all, output_full).astype(jnp.bfloat16)
    d_query, d_key, d_value = lax.map(
        attend_back,
        (heads(query), heads(keys), heads(value), heads(d_context), log_total, segments),
    )
    d_query = d_query.reshape(rows_all.shape[0], local * HD)
    d_key = d_key.reshape(rows_all.shape[0], local * HD)
    d_value = d_value.reshape(rows_all.shape[0], local * HD)
    query_bias_term = jnp.sum(d_query.astype(jnp.float32), axis=0)
    value_bias_term = jnp.sum(d_value.astype(jnp.float32), axis=0)
    back_rows = (
        against(d_query, query_full) + against(d_key, key_full) + against(d_value, value_full)
    )
    d_rows = lax.psum_scatter(
        back_rows.astype(jnp.bfloat16), "tp", scatter_dimension=0, tiled=True
    ).astype(jnp.float32)
    input_grad = (d_rows + d_first_sum).astype(jnp.bfloat16)
    first_grads = (
        lax.psum_scatter(
            across(rows_all, d_query).astype(jnp.bfloat16), "fsdp", scatter_dimension=0, tiled=True
        ).astype(jnp.float32),
        lax.psum_scatter(
            across(rows_all, d_key).astype(jnp.bfloat16), "fsdp", scatter_dimension=0, tiled=True
        ).astype(jnp.float32),
        lax.psum_scatter(
            across(rows_all, d_value).astype(jnp.bfloat16), "fsdp", scatter_dimension=0, tiled=True
        ).astype(jnp.float32),
        lax.psum_scatter(
            up_term.astype(jnp.bfloat16), "fsdp", scatter_dimension=0, tiled=True
        ).astype(jnp.float32),
    )
    second_grads = (
        lax.psum_scatter(
            output_term.astype(jnp.bfloat16), "fsdp", scatter_dimension=1, tiled=True
        ).astype(jnp.float32),
        lax.psum_scatter(
            down_term.astype(jnp.bfloat16), "fsdp", scatter_dimension=1, tiled=True
        ).astype(jnp.float32),
        lax.psum_scatter(
            query_bias_term[None].astype(jnp.bfloat16), "fsdp", scatter_dimension=1, tiled=True
        ).astype(jnp.float32),
        lax.psum_scatter(
            value_bias_term[None].astype(jnp.bfloat16), "fsdp", scatter_dimension=1, tiled=True
        ).astype(jnp.float32),
        lax.psum_scatter(
            up_bias_term[None].astype(jnp.bfloat16), "fsdp", scatter_dimension=1, tiled=True
        ).astype(jnp.float32),
    )
    small = (
        lax.psum_scatter(output_bias_term, ("fsdp", "tp"), scatter_dimension=0, tiled=True),
        lax.psum_scatter(first_gain_term, ("fsdp", "tp"), scatter_dimension=0, tiled=True),
        lax.psum_scatter(first_shift_term, ("fsdp", "tp"), scatter_dimension=0, tiled=True),
        lax.psum_scatter(down_bias_term, ("fsdp", "tp"), scatter_dimension=0, tiled=True),
        lax.psum_scatter(second_gain_term, ("fsdp", "tp"), scatter_dimension=0, tiled=True),
        lax.psum_scatter(second_shift_term, ("fsdp", "tp"), scatter_dimension=0, tiled=True),
    )
    return (
        layer_out,
        input_grad,
        first_grads[0],
        second_grads[2],
        first_grads[1],
        first_grads[2],
        second_grads[3],
        second_grads[0],
        small[0],
        small[1],
        small[2],
        first_grads[3],
        second_grads[4],
        second_grads[1],
        small[3],
        small[4],
        small[5],
    )


def solution(mesh):
    placed = (
        P(("fsdp", "tp"), None),
        P("fsdp", "tp"),
        P("tp"),
        P("fsdp", "tp"),
        P("fsdp", "tp"),
        P("tp"),
        P("tp", "fsdp"),
        P(),
        P(),
        P(),
        P("fsdp", "tp"),
        P("tp"),
        P("tp", "fsdp"),
        P(),
        P(),
        P(),
        P("fsdp", None),
        P(("fsdp", "tp"), None),
    )
    return jax.shard_map(
        shards,
        mesh=mesh,
        in_specs=placed,
        out_specs=(
            P(("fsdp", "tp"), None),
            P(("fsdp", "tp"), None),
            P("fsdp", "tp"),
            P("tp", "fsdp"),
            P("fsdp", "tp"),
            P("fsdp", "tp"),
            P("tp", "fsdp"),
            P("tp", "fsdp"),
            P(("fsdp", "tp")),
            P(("fsdp", "tp")),
            P(("fsdp", "tp")),
            P("fsdp", "tp"),
            P("tp", "fsdp"),
            P("tp", "fsdp"),
            P(("fsdp", "tp")),
            P(("fsdp", "tp")),
            P(("fsdp", "tp")),
        ),
        check_vma=False,
    )
```

profile of v0, /device:TPU:1, one launch (start us, length us, event | category | flops | bytes accessed | tf_op | source)
XLA Modules:
  0.0 1813.3 jit_solution(9502454436063739699)
XLA Ops:
  12.0 28.3 %all-gather.23.cloned.1.call-done = bf16[2048,512]{1,0:T(8,128)(2,1)} async-done(((bf16[256,512]{1,0:T(8,128)(2,1)}), bf16[2048,512]{1,0:T(8,128)(2,1)}) %all-gather.23.cloned.1.call-update) | async-done | bytes 2097168 | tf_op jit(solution)/shard_map/all_gather | solution.py:97
  40.3 81.9 %all-gather.17.cloned.1.call-done = bf16[1024,2048]{1,0:T(8,128)(2,1)} async-done(((bf16[256,2048]{1,0:T(8,128)(2,1)}), bf16[1024,2048]{1,0:T(8,128)(2,1)}) %all-gather.17.cloned.1.call-update) | async-done | bytes 4194320 | tf_op jit(solution)/shard_map/all_gather | solution.py:136
  127.5 23.5 %all-gather.21.cloned.1.call-done = bf16[2048,512]{1,0:T(8,128)(2,1)} async-done(((bf16[256,512]{1,0:T(8,128)(2,1)}), bf16[2048,512]{1,0:T(8,128)(2,1)}) %all-gather.21.cloned.1.call-update) | async-done | bytes 2097168 | tf_op jit(solution)/shard_map/all_gather | solution.py:96
  151.1 5.2 add_convert_fusion.3
  157.3 7.7 fusion.36
  165.0 15.8 all-gather.19.cloned.1.call-done
  180.7 5.2 add_convert_fusion.4
  186.0 8.6 fusion
  195.2 7.6 fusion.24
  202.8 7.9 all-gather.25.cloned.1.call-done
  210.7 7.2 fusion.37
  218.7 143.2 %reduce-scatter.20.cloned.1.call-done = f32[256,2048]{1,0:T(8,128)} async-done(((f32[1024,2048]{1,0:T(8,128)}), f32[256,2048]{1,0:T(8,128)}) %reduce-scatter.20.cloned.1.call-update) | async-done | bytes 2097168 | tf_op jit(solution)/shard_map/reduce_scatter | solution.py:144
  366.6 53.0 %all-gather.29.cloned.1.call-done = bf16[2048,2048]{1,0:T(8,128)(2,1)} async-done(((bf16[256,2048]{1,0:T(8,128)(2,1)}), bf16[2048,2048]{1,0:T(8,128)(2,1)}) %all-gather.29.cloned.1.call-update) | async-done | bytes 8388624 | tf_op jit(solution)/shard_map/all_gather | solution.py:99
  419.6 82.5 %all-gather.27.cloned.1.call-done = bf16[1024,2048]{1,0:T(8,128)(2,1)} async-done(((bf16[256,2048]{1,0:T(8,128)(2,1)}), bf16[1024,2048]{1,0:T(8,128)(2,1)}) %all-gather.27.cloned.1.call-update) | async-done | bytes 4194320 | tf_op jit(solution)/shard_map/all_gather | solution.py:147
  502.1 14.7 fusion.38
  516.9 42.1 %all-gather.31.cloned.1.call-done = bf16[2048,2048]{1,0:T(8,128)(2,1)} async-done(((bf16[2048,256]{1,0:T(8,128)(2,1)}), bf16[2048,2048]{1,0:T(8,128)(2,1)}) %all-gather.31.cloned.1.call-update) | async-done | bytes 8388624 | tf_op jit(solution)/shard_map/all_gather | solution.py:106
  558.9 17.6 fusion.28
  576.6 144.0 %reduce-scatter.22.cloned.1.call-done = f32[256,2048]{1,0:T(8,128)} async-done(((f32[1024,2048]{1,0:T(8,128)}), f32[256,2048]{1,0:T(8,128)}) %reduce-scatter.22.cloned.1.call-update) | async-done | bytes 2097168 | tf_op jit(solution)/shard_map/reduce_scatter | solution.py:151
  731.1 80.4 %all-gather.33.cloned.1.call-done = bf16[1024,2048]{1,0:T(8,128)(2,1)} async-done(((bf16[256,2048]{1,0:T(8,128)(2,1)}), bf16[1024,2048]{1,0:T(8,128)(2,1)}) %all-gather.33.cloned.1.call-update) | async-done | bytes 4194320 | tf_op jit(solution)/shard_map/all_gather | solution.py:166
  811.5 56.7 %all-gather.35.cloned.1.call-done = bf16[2048,2048]{1,0:T(8,128)(2,1)} async-done(((bf16[2048,256]{1,0:T(8,128)(2,1)}), bf16[2048,2048]{1,0:T(8,128)(2,1)}) %all-gather.35.cloned.1.call-update) | async-done | bytes 8388624 | tf_op jit(solution)/shard_map/all_gather | solution.py:106
  868.2 20.3 %fusion.29 = (bf16[2048]{0:T(1024)(128)(2,1)S(1)}, bf16[1024,2048]{1,0:T(8,128)(2,1)}) fusion(f32[1024,2048]{1,0:T(8,128)} %fusion.38, f32[2048]{0:T(1024)S(1)} %copy-done.32, bf16[1024,2048]{1,0:T(8,128)(2,1)} %all-gather.33.cloned.1.call-done, bf16[2048,2048]{1,0:T(8,128)(2,1)} %all-gather.35.cloned.1.call-done), kind=kOutput, calls=%fused_computation.81 | convolution fusion | flops 8636069888 | bytes 25178112 | tf_op jit(solution)/shard_map/dot_general | solution.py:18
  888.5 36.0 %all-gather.37.cloned.1.call-done = bf16[2048,2048]{1,0:T(8,128)(2,1)} async-done(((bf16[256,2048]{1,0:T(8,128)(2,1)}), bf16[2048,2048]{1,0:T(8,128)(2,1)}) %all-gather.37.cloned.1.call-update) | async-done | bytes 8388624 | tf_op jit(solution)/shard_map/all_gather | solution.py:99
  924.5 14.7 fusion.39
  939.8 143.4 %reduce-scatter.24.cloned.1.call-done = f32[256,2048]{1,0:T(8,128)} async-done(((f32[1024,2048]{1,0:T(8,128)}), f32[256,2048]{1,0:T(8,128)}) %reduce-scatter.24.cloned.1.call-update) | async-done | bytes 2097168 | tf_op jit(solution)/shard_map/reduce_scatter | solution.py:172
  1094.1 16.0 convolution_convert_fusion
  1110.1 14.1 convolution_convert_fusion.1
  1125.0 71.9 %all-gather.39.cloned.1.call-done = bf16[1024,2048]{1,0:T(8,128)(2,1)} async-done(((bf16[256,2048]{1,0:T(8,128)(2,1)}), bf16[1024,2048]{1,0:T(8,128)(2,1)}) %all-gather.39.cloned.1.call-update) | async-done | bytes 4194320 | tf_op jit(solution)/shard_map/all_gather | solution.py:178
  1202.1 10.0 bitcast_reduce_fusion
  1213.0 8.9 multiply_reduce_fusion
  1221.9 8.1 multiply_convert_fusion
  1235.0 6.3 convolution_convert_fusion.2
  1241.8 5.8 fusion.18
  1247.7 6.0 fusion.16
  1253.8 6.4 multiply_convert_fusion.2
  1264.2 7.4 fusion.41
  1271.7 7.2 fusion.40
  1278.9 6.1 all-gather.47.cloned.1.call-done
  1285.0 10.8 add_convert_fusion
  1295.9 25.9 %reduce-scatter.44.cloned.1.call-done = bf16[256,1]{1,0:T(8,128)(2,1)} async-done(((bf16[2048,1]{1,0:T(8,128)(2,1)}), bf16[256,1]{1,0:T(8,128)(2,1)}) %reduce-scatter.44.cloned.1.call-update) | async-done | bytes 528
  1323.2 74.2 %reduce-scatter.38.cloned.1.call-done = bf16[2048,256]{1,0:T(8,128)(2,1)} async-done(((bf16[2048,2048]{1,0:T(8,128)(2,1)}), bf16[2048,256]{1,0:T(8,128)(2,1)}) %reduce-scatter.38.cloned.1.call-update) | async-done | bytes 1048592 | tf_op jit(solution)/shard_map/reduce_scatter | solution.py:215
  1400.1 72.1 %reduce-scatter.36.cloned.1.call-done = bf16[256,2048]{1,0:T(8,128)(2,1)} async-done(((bf16[2048,2048]{1,0:T(8,128)(2,1)}), bf16[256,2048]{1,0:T(8,128)(2,1)}) %reduce-scatter.36.cloned.1.call-update) | async-done | bytes 1048592 | tf_op jit(solution)/shard_map/reduce_scatter | solution.py:207
  1475.0 39.3 %all-reduce.6 = (f32[2048]{0:T(1024)S(1)}, f32[2048]{0:T(1024)S(1)}, f32[2048]{0:T(1024)S(1)}, f32[2048]{0:T(1024)S(1)}, f32[2048]{0:T(1024)S(1)}, /*index=5*/f32[2048]{0:T(1024)S(1)}) all-reduce(f32[2048]{0:T(1024)S(1)} %copy-done.27, f32[2048]{0:T(1024)S(1)} %get-tuple-element.114, ...), channel_id=12, replica_groups=mesh['fsdp'=8,'tp'=4] {'fsdp','tp'}, use_global_device_ids=true, to_apply=%region_24.25.clone | all-reduce | flops 12288 | bytes 98304
  1519.2 26.6 %reduce-scatter.40.cloned.1.call-done = bf16[64,1]{1,0:T(8,128)(2,1)} async-done(((bf16[512,1]{1,0:T(8,128)(2,1)}), bf16[64,1]{1,0:T(8,128)(2,1)}) %reduce-scatter.40.cloned.1.call-update) | async-done | bytes 144
  1547.1 44.0 %reduce-scatter.34.cloned.1.call-done = bf16[512,256]{1,0:T(8,128)(2,1)} async-done(((bf16[512,2048]{1,0:T(8,128)(2,1)}), bf16[512,256]{1,0:T(8,128)(2,1)}) %reduce-scatter.34.cloned.1.call-update) | async-done | bytes 262160 | tf_op jit(solution)/shard_map/reduce_scatter | solution.py:212
  1592.9 42.6 %reduce-scatter.32.cloned.1.call-done = bf16[256,512]{0,1:T(8,128)(2,1)} async-done(((bf16[2048,512]{0,1:T(8,128)(2,1)}), bf16[256,512]{0,1:T(8,128)(2,1)}) %reduce-scatter.32.cloned.1.call-update) | async-done | bytes 262160 | tf_op jit(solution)/shard_map/reduce_scatter | solution.py:204
  1637.4 42.9 %reduce-scatter.28.cloned.1.call-done = bf16[256,512]{0,1:T(8,128)(2,1)} async-done(((bf16[2048,512]{0,1:T(8,128)(2,1)}), bf16[256,512]{0,1:T(8,128)(2,1)}) %reduce-scatter.28.cloned.1.call-update) | async-done | bytes 262160 | tf_op jit(solution)/shard_map/reduce_scatter | solution.py:198
  1682.2 42.6 %reduce-scatter.30.cloned.1.call-done = bf16[256,512]{0,1:T(8,128)(2,1)} async-done(((bf16[2048,512]{0,1:T(8,128)(2,1)}), bf16[256,512]{0,1:T(8,128)(2,1)}) %reduce-scatter.30.cloned.1.call-update) | async-done | bytes 262160 | tf_op jit(solution)/shard_map/reduce_scatter | solution.py:201
  1726.7 77.4 %reduce-scatter.26.cloned.1.call-done = bf16[256,2048]{1,0:T(8,128)(2,1)} async-done(((bf16[1024,2048]{1,0:T(8,128)(2,1)}), bf16[256,2048]{1,0:T(8,128)(2,1)}) %reduce-scatter.26.cloned.1.call-update) | async-done | bytes 1048592 | tf_op jit(solution)/shard_map/reduce_scatter | solution.py:193
  (184 shorter events, 78.4 us)
Async XLA Ops:
  7.2 33.2 %all-gather.23.cloned.1.call-start = ((), (), s32[]{:S(2)}) async-start(), calls=%async_computation.16 | async-start | bytes 2359296 | tf_op jit(solution)/shard_map/all_gather | solution.py:97
  7.9 114.4 %all-gather.17.cloned.1.call-start = ((), (), s32[]{:S(2)}) async-start(), calls=%async_computation.13 | async-start | bytes 5242880 | tf_op jit(solution)/shard_map/all_gather | solution.py:136
  8.7 142.4 %all-gather.21.cloned.1.call-start = ((), (), s32[]{:S(2)}) async-start(), calls=%async_computation.15 | async-start | bytes 2359296 | tf_op jit(solution)/shard_map/all_gather | solution.py:96
  9.4 171.3 %all-gather.19.cloned.1.call-start = ((), (), s32[]{:S(2)}) async-start(), calls=%async_computation.14 | async-start | bytes 2359296 | tf_op jit(solution)/shard_map/all_gather | solution.py:98
  10.0 200.7 %all-gather.25.cloned.1.call-start = ((), (), s32[]{:S(2)}) async-start(), calls=%async_computation.17 | async-start | bytes 2359296 | tf_op jit(solution)/shard_map/all_gather | solution.py:105
  10.6 351.4 %reduce-scatter.20.cloned.1.call-start = ((), (), s32[]{:S(2)}) async-start(), calls=%async_computation.18 | async-start | bytes 10485760 | tf_op jit(solution)/shard_map/reduce_scatter | solution.py:144
  12.0 139.0 %copy-start.33 = (f32[512]{0:T(512)S(1)}, f32[512]{0:T(512)}, u32[]{:S(2)}) copy-start(f32[512]{0:T(512)} %param.20) | copy-start | bytes 6148
  127.5 28.8 %copy-start.6 = (bf16[1024,512]{0,1:T(8,128)(2,1)}, bf16[1024,512]{0,1:T(8,128)(2,1)S(1)}, u32[]{:S(2)}) copy-start(bf16[1024,512]{0,1:T(8,128)(2,1)S(1)} %convolution_convert_fusion.7) | copy-start | bytes 3145732
  157.3 23.5 %copy-start.34 = (f32[512]{0:T(512)S(1)}, f32[512]{0:T(512)}, u32[]{:S(2)}) copy-start(f32[512]{0:T(512)} %param.23) | copy-start | bytes 6148
  165.0 29.7 %copy-start.16 = (f32[4,1024]{1,0:T(4,128)}, f32[4,1024]{1,0:T(4,128)S(1)}, u32[]{:S(2)}) copy-start(f32[4,1024]{1,0:T(4,128)S(1)} %get-tuple-element.140) | copy-start | bytes 49156
  217.9 144.1 %copy-start.9 = (bf16[256,2048]{1,0:T(8,128)(2,1)S(1)}, bf16[256,2048]{1,0:T(8,128)(2,1)}, u32[]{:S(2)}) copy-start(bf16[256,2048]{1,0:T(8,128)(2,1)} %param.18) | copy-start | bytes 3145732
  217.9 144.1 %copy-start.28 = (f32[2048]{0:T(1024)S(1)}, f32[2048]{0:T(1024)}, u32[]{:S(2)}) copy-start(f32[2048]{0:T(1024)} %param.25) | copy-start | bytes 24580
  217.9 146.4 %copy-start.18 = (f32[2048]{0:T(1024)S(1)}, f32[2048]{0:T(1024)}, u32[]{:S(2)}) copy-start(f32[2048]{0:T(1024)} %param.26) | copy-start | bytes 24580
  217.9 146.4 %copy-start.21 = (f32[2048]{0:T(1024)S(1)}, f32[2048]{0:T(1024)}, u32[]{:S(2)}) copy-start(f32[2048]{0:T(1024)} %param.27) | copy-start | bytes 24580
  217.9 201.6 %all-gather.29.cloned.1.call-start = ((), (), s32[]{:S(2)}) async-start(), calls=%async_computation.20 | async-start | bytes 9437184 | tf_op jit(solution)/shard_map/all_gather | solution.py:99
  218.7 283.4 %all-gather.27.cloned.1.call-start = ((), (), s32[]{:S(2)}) async-start(), calls=%async_computation.19 | async-start | bytes 5242880 | tf_op jit(solution)/shard_map/all_gather | solution.py:147
  365.8 193.2 %all-gather.31.cloned.1.call-start = ((), (), s32[]{:S(2)}) async-start(), calls=%async_computation.21 | async-start | bytes 9437184 | tf_op jit(solution)/shard_map/all_gather | solution.py:106
  366.5 192.4 %copy-start.32 = (f32[2048]{0:T(1024)S(1)}, f32[2048]{0:T(1024)}, u32[]{:S(2)}) copy-start(f32[2048]{0:T(1024)} %param.29) | copy-start | bytes 24580
  366.5 354.0 %reduce-scatter.22.cloned.1.call-start = ((), (), s32[]{:S(2)}) async-start(), calls=%async_computation.22 | async-start | bytes 10485760 | tf_op jit(solution)/shard_map/reduce_scatter | solution.py:151
  576.5 144.1 %copy-start.29 = (f32[2048]{0:T(1024)S(1)}, f32[2048]{0:T(1024)}, u32[]{:S(2)}) copy-start(f32[2048]{0:T(1024)} %param.31) | copy-start | bytes 24580
  576.5 146.7 %copy-start.10 = (bf16[256,2048]{1,0:T(8,128)(2,1)S(1)}, bf16[256,2048]{1,0:T(8,128)(2,1)}, u32[]{:S(2)}) copy-start(bf16[256,2048]{1,0:T(8,128)(2,1)} %param.35) | copy-start | bytes 3145732
  576.5 146.7 %copy-start.22 = (f32[2048]{0:T(1024)S(1)}, f32[2048]{0:T(1024)}, u32[]{:S(2)}) copy-start(f32[2048]{0:T(1024)} %param.32) | copy-start | bytes 24580
  576.5 235.0 %all-gather.33.cloned.1.call-start = ((), (), s32[]{:S(2)}) async-start(), calls=%async_computation.23 | async-start | bytes 5242880 | tf_op jit(solution)/shard_map/all_gather | solution.py:166
  729.7 138.5 %all-gather.35.cloned.1.call-start = ((), (), s32[]{:S(2)}) async-start(), calls=%async_computation.24 | async-start | bytes 9437184 | tf_op jit(solution)/shard_map/all_gather | solution.py:106
  730.3 194.2 %all-gather.37.cloned.1.call-start = ((), (), s32[]{:S(2)}) async-start(), calls=%async_computation.25 | async-start | bytes 9437184 | tf_op jit(solution)/shard_map/all_gather | solution.py:99
  731.1 352.2 %reduce-scatter.24.cloned.1.call-start = ((), (), s32[]{:S(2)}) async-start(), calls=%async_computation.26 | async-start | bytes 10485760 | tf_op jit(solution)/shard_map/reduce_scatter | solution.py:172
  939.2 185.8 %all-gather.41.cloned.1.call-start = ((), (), s32[]{:S(2)}) async-start(), calls=%async_computation.28 | async-start | bytes 2359296 | tf_op jit(solution)/shard_map/all_gather | solution.py:105
  939.8 257.1 %all-gather.39.cloned.1.call-start = ((), (), s32[]{:S(2)}) async-start(), calls=%async_computation.27 | async-start | bytes 5242880 | tf_op jit(solution)/shard_map/all_gather | solution.py:178
  1090.8 173.4 %all-gather.45.cloned.1.call-start = ((), (), s32[]{:S(2)}) async-start(), calls=%async_computation.30 | async-start | bytes 2359296 | tf_op jit(solution)/shard_map/all_gather | solution.py:97
  1091.4 180.3 %all-gather.43.cloned.1.call-start = ((), (), s32[]{:S(2)}) async-start(), calls=%async_computation.29 | async-start | bytes 2359296 | tf_op jit(solution)/shard_map/all_gather | solution.py:96
  1091.9 193.0 %all-gather.47.cloned.1.call-start = ((), (), s32[]{:S(2)}) async-start(), calls=%async_computation.31 | async-start | bytes 2359296 | tf_op jit(solution)/shard_map/all_gather | solution.py:98
  1092.7 229.0 %reduce-scatter.44.cloned.1.call-start = ((), (), s32[]{:S(2)}) async-start(), calls=%async_computation.41 | async-start | bytes 589824
  1094.1 303.3 %reduce-scatter.38.cloned.1.call-start = ((), (), s32[]{:S(2)}) async-start(), calls=%async_computation.38 | async-start | bytes 9437184 | tf_op jit(solution)/shard_map/reduce_scatter | solution.py:215
  1110.1 362.1 %reduce-scatter.36.cloned.1.call-start = ((), (), s32[]{:S(2)}) async-start(), calls=%async_computation.37 | async-start | bytes 9437184 | tf_op jit(solution)/shard_map/reduce_scatter | solution.py:207
  1124.2 393.6 %reduce-scatter.42.cloned.1.call-start = ((), (), s32[]{:S(2)}) async-start(), calls=%async_computation.40 | async-start | bytes 147456
  1125.0 77.2 %copy-start.14 = (f32[4,1024]{1,0:T(4,128)}, f32[4,1024]{1,0:T(4,128)S(1)}, u32[]{:S(2)}) copy-start(f32[4,1024]{1,0:T(4,128)S(1)} %log_add_fusion) | copy-start | bytes 49156
  1234.2 311.5 %reduce-scatter.40.cloned.1.call-start = ((), (), s32[]{:S(2)}) async-start(), calls=%async_computation.39 | async-start | bytes 147456
  1235.0 356.2 %reduce-scatter.34.cloned.1.call-start = ((), (), s32[]{:S(2)}) async-start(), calls=%async_computation.36 | async-start | bytes 2359296 | tf_op jit(solution)/shard_map/reduce_scatter | solution.py:212
  1241.3 394.2 %reduce-scatter.32.cloned.1.call-start = ((), (), s32[]{:S(2)}) async-start(), calls=%async_computation.35 | async-start | bytes 2359296 | tf_op jit(solution)/shard_map/reduce_scatter | solution.py:204
  1247.7 432.6 %reduce-scatter.28.cloned.1.call-start = ((), (), s32[]{:S(2)}) async-start(), calls=%async_computation.33 | async-start | bytes 2359296 | tf_op jit(solution)/shard_map/reduce_scatter | solution.py:198
  1253.7 471.1 %reduce-scatter.30.cloned.1.call-start = ((), (), s32[]{:S(2)}) async-start(), calls=%async_computation.34 | async-start | bytes 2359296 | tf_op jit(solution)/shard_map/reduce_scatter | solution.py:201
  1264.0 540.1 %reduce-scatter.26.cloned.1.call-start = ((), (), s32[]{:S(2)}) async-start(), calls=%async_computation.32 | async-start | bytes 5242880 | tf_op jit(solution)/shard_map/reduce_scatter | solution.py:193
  1295.8 179.2 %copy-start.23 = (f32[2048]{0:T(1024)S(1)}, f32[2048]{0:T(1024)}, u32[]{:S(2)}) copy-start(f32[2048]{0:T(1024)} %get-tuple-element.116) | copy-start | bytes 24580
  1295.8 179.2 %copy-start.24 = (f32[2048]{0:T(1024)S(1)}, f32[2048]{0:T(1024)}, u32[]{:S(2)}) copy-start(f32[2048]{0:T(1024)} %get-tuple-element.121) | copy-start | bytes 24580
  1295.8 179.1 %copy-start.25 = (f32[2048]{0:T(1024)S(1)}, f32[2048]{0:T(1024)}, u32[]{:S(2)}) copy-start(f32[2048]{0:T(1024)} %get-tuple-element.130) | copy-start | bytes 24580
  1295.9 179.1 %copy-start.26 = (f32[2048]{0:T(1024)S(1)}, f32[2048]{0:T(1024)}, u32[]{:S(2)}) copy-start(f32[2048]{0:T(1024)} %get-tuple-element.119) | copy-start | bytes 24580
  1295.9 179.1 %copy-start.27 = (f32[2048]{0:T(1024)S(1)}, f32[2048]{0:T(1024)}, u32[]{:S(2)}) copy-start(f32[2048]{0:T(1024)} %get-tuple-element.132) | copy-start | bytes 24580
  1323.2 480.8 %copy-start.3 = (f32[256,2048]{1,0:T(8,128)S(1)}, f32[256,2048]{1,0:T(8,128)}, u32[]{:S(2)}) copy-start(f32[256,2048]{1,0:T(8,128)} %copy-done.2) | copy-start | bytes 6291460
  (17 other events, 87.7 us)
Sparse Core Ops, SparseCore 0:
  9.9 30.3 all-gather.22
  41.9 80.3 all-gather.16
  124.2 26.8 all-gather.20
  152.8 27.8 all-gather.18
  182.5 28.1 all-gather.24
  218.0 143.8 reduce-scatter.19
  363.8 55.6 all-gather.28
  421.7 80.3 all-gather.26
  504.0 54.8 all-gather.30
  576.6 143.8 reduce-scatter.21
  729.9 81.6 all-gather.32
  813.3 54.8 all-gather.34
  870.1 54.3 all-gather.36
  939.3 143.8 reduce-scatter.23
  1085.0 29.4 all-gather.40
  1116.5 80.3 all-gather.38
  1198.6 26.8 all-gather.44
  1227.2 27.8 all-gather.42
  1257.1 27.8 all-gather.46
  1288.5 33.2 reduce-scatter.43
  1325.6 71.7 reduce-scatter.37
  1400.9 71.2 reduce-scatter.35
  1476.1 32.8 reduce-scatter.41
  1512.4 33.3 reduce-scatter.39
  1549.4 41.6 reduce-scatter.33
  1594.3 41.2 reduce-scatter.31
  1639.0 41.2 reduce-scatter.27
  1683.6 41.1 reduce-scatter.29
  1727.2 76.8 reduce-scatter.25
where the time goes:
time: 1820 us; the launch traced here: 1810 us
  waiting for transfers between devices  1470 us (81%)
  matrix products  215 us (12%)
  other arithmetic  47.2 us (3%)
  blocking collectives  39.3 us (2%)
  local copies, waits for them, and re-layouts  21.9 us (1%)
    reduce_scatter x1, waiting for transfers between devices, shards(): lax.psum_scatter(project(hidden, outer[1]), 'tp', scatter_dimension=0, ti...  144 us
    reduce_scatter x1, waiting for transfers between devices, shards(): lax.psum_scatter(against(d_pre, up_full), 'tp', scatter_dimension=0, tile...  143 us
    reduce_scatter x1, waiting for transfers between devices, shards(): lax.psum_scatter(project(context, outer[0]), 'tp', scatter_dimension=0, t...  143 us
    all_gather x2, waiting for transfers between devices, collect_outer(): lax.all_gather(down_weight, 'fsdp', axis=1, tiled=True)  98.7 us
    all_gather x2, waiting for transfers between devices, collect_inner(): lax.all_gather(up_weight, 'fsdp', axis=0, tiled=True)  89 us
    all_gather x1, waiting for transfers between devices, shards(): lax.all_gather(first_out.astype(jnp.bfloat16), 'tp', axis=0, tiled=True)  82.5 us
    all_gather x1, waiting for transfers between devices, shards(): rows_all = lax.all_gather(inputs, 'tp', axis=0, tiled=True)  81.9 us
    all_gather x1, waiting for transfers between devices, shards(): lax.all_gather(d_second.astype(jnp.bfloat16), 'tp', axis=0, tiled=True)  80.4 us
  transfers between devices with their start and end apart: 29, of which 25 were waited for; matrix products, arithmetic and copies ran while one was open for 13% of the time, Pallas kernels for 0%

commit v1 on v0

v1 whole, which is shorter than its diff:
```python
import jax
import jax.numpy as jnp
from jax import lax
from jax.sharding import PartitionSpec as P

HD = 128
EPS = 1e-06
NEG = -1000000000.0
AXES = ("fsdp", "tp")
F32 = jnp.float32
BF16 = jnp.bfloat16


def project(left, right):
    return jnp.dot(left, right, preferred_element_type=F32)


def against(left, right):
    return lax.dot_general(left, right, (((1,), (1,)), ((), ())), preferred_element_type=F32)


def across(left, right):
    return lax.dot_general(left, right, (((0,), (0,)), ((), ())), preferred_element_type=F32)


def normalize(total):
    center = total - jnp.mean(total, axis=-1, keepdims=True)
    spread = jnp.mean(center * center, axis=-1, keepdims=True)
    scale_inv = lax.rsqrt(spread + EPS)
    return center * scale_inv, scale_inv


def norm_back(grad, normed, scale_inv, gain):
    scaled = grad * gain
    inner = (
        scaled
        - jnp.mean(scaled, axis=-1, keepdims=True)
        - normed * jnp.mean(scaled * normed, axis=-1, keepdims=True)
    )
    return (scale_inv * inner, jnp.sum(grad * normed, axis=0), jnp.sum(grad, axis=0))


def gelu_tanh(values):
    return jax.nn.gelu(values, approximate=True)


def scores_of(queries, keys, labels):
    scores = jnp.einsum("qhd,khd->hqk", queries, keys, preferred_element_type=F32) * HD ** (-0.5)
    same = labels[:, None] == labels[None, :]
    return jnp.where(same[None], scores, NEG)


def attend(queries, keys, values, labels):
    scores = scores_of(queries, keys, labels)
    top = jnp.max(scores, axis=-1, keepdims=True)
    weights = jnp.exp(scores - top)
    total = jnp.sum(weights, axis=-1, keepdims=True)
    probs = (weights / total).astype(BF16)
    context = jnp.einsum("hqk,khd->qhd", probs, values, preferred_element_type=F32).astype(BF16)
    return context, top[..., 0] + jnp.log(total[..., 0])


def attend_back(queries, keys, values, d_context, log_total, labels):
    probs = jnp.exp(scores_of(queries, keys, labels) - log_total[..., None])
    probs_low = probs.astype(BF16)
    d_value = jnp.einsum("hqk,qhd->khd", probs_low, d_context, preferred_element_type=F32).astype(
        BF16
    )
    d_probs = jnp.einsum("qhd,khd->hqk", d_context, values, preferred_element_type=F32)
    d_scores = (probs * (d_probs - jnp.sum(probs * d_probs, axis=-1, keepdims=True))).astype(BF16)
    d_query = (
        jnp.einsum("hqk,khd->qhd", d_scores, keys, preferred_element_type=F32) * HD ** (-0.5)
    ).astype(BF16)
    d_key = (
        jnp.einsum("hqk,qhd->khd", d_scores, queries, preferred_element_type=F32) * HD ** (-0.5)
    ).astype(BF16)
    return (d_query, d_key, d_value)


class Layout:
    def __init__(self, fsdp, tp):
        self.fsdp, self.tp = fsdp, tp
        self.planes, self.n = fsdp // 2, tp // 2
        f, t = lax.axis_index("fsdp"), lax.axis_index("tp")
        self.g, self.c = f // 2, f % 2
        self.h, self.l = t // self.n, t % self.n

    def move(self, value, rule):
        pairs = []
        for g in range(self.planes):
            for c in range(2):
                for h in range(2):
                    for l in range(self.n):
                        a, b, d, e = rule(g, c, h, l)
                        here = (g * 2 + c) * self.tp + h * self.n + l
                        there = (a * 2 + b) * self.tp + d * self.n + e
                        pairs.append((here, there))
        return lax.ppermute(value, AXES, pairs)

    def core(self, value):
        return self.move(value, lambda g, c, h, l: (g, 1 - c, h, l))

    def half(self, value):
        return self.move(value, lambda g, c, h, l: (g, c, 1 - h, l))

    def trade(self, value):
        return self.move(value, lambda g, c, h, l: (g, h, c, l))

    def plane(self, value, mask):
        return self.move(value, lambda g, c, h, l: (g ^ mask, c, h, l))

    def along(self, value, step):
        return self.move(value, lambda g, c, h, l: (g, c, h, (l + step) % self.n))

    def relative(self, value):
        size = value.shape[-1] // self.planes
        parts = [
            lax.dynamic_slice_in_dim(value, (self.g ^ m) * size, size, axis=value.ndim - 1)
            for m in range(self.planes)
        ]
        return jnp.concatenate(parts, axis=-1)

    def gather(self, own):
        pieces = []
        for step in range(self.n):
            piece = own if step == 0 else self.along(own, step)
            pieces += [piece, self.core(piece)]
        return jnp.concatenate(pieces, axis=0)

    def reduce(self, block):
        total, arrived = None, []
        for step in list(range(1, self.n)) + [0]:
            both = block((self.n - step) % self.n)
            size = both.shape[0] // 2
            mate = self.core(both[size:].astype(BF16))
            summed = both[:size] + mate.astype(F32)
            if step == 0:
                total = summed
            else:
                arrived.append(self.along(summed.astype(BF16), step))
        for piece in arrived:
            total = total + piece.astype(F32)
        return total

    def spread(self, shard, axis):
        other = 1 - axis
        width = shard.shape[other] // 2
        mine = lax.dynamic_slice_in_dim(shard, self.c * width, width, axis=other)
        give = lax.dynamic_slice_in_dim(shard, (1 - self.c) * width, width, axis=other)
        got = self.core(give)
        first = self.c == 0
        near = jnp.concatenate(
            [jnp.where(first, mine, got), jnp.where(first, got, mine)], axis=axis
        )
        near = jnp.concatenate([near, self.half(near)], axis=other)
        size = near.shape[axis] // 2

        def part(value, index):
            return lax.slice_in_dim(value, index * size, (index + 1) * size, axis=axis)

        pieces = {0: (part(near, 0), part(near, 1))}
        for m in sorted(range(1, self.planes), key=lambda v: bin(v).count("1")):
            if bin(m).count("1") == 1:
                whole = self.plane(near, m)
                pieces[m] = (part(whole, 0), part(whole, 1))
            else:
                top, low = 1 << (m.bit_length() - 1), m & -m
                pieces[m] = (
                    self.plane(pieces[m ^ top][0], top),
                    self.plane(pieces[m ^ low][1], low),
                )
        return jnp.concatenate([p for m in range(self.planes) for p in pieces[m]], axis=axis)

    def collect(self, grad, axis):
        other = 1 - axis
        size = grad.shape[axis] // (2 * self.planes)
        width = grad.shape[other] // 2
        total = {
            m: [
                lax.slice_in_dim(grad, (2 * m + k) * size, (2 * m + k + 1) * size, axis=axis)
                for k in range(2)
            ]
            for m in range(self.planes)
        }
        for m in sorted(range(1, self.planes), key=lambda v: -bin(v).count("1")):
            if bin(m).count("1") == 1:
                both = jnp.concatenate([v.astype(BF16) for v in total[m]], axis=axis)
                both = self.plane(both, m).astype(F32)
                for k in range(2):
                    piece = lax.slice_in_dim(both, k * size, (k + 1) * size, axis=axis)
                    total[0][k] = total[0][k] + piece
            else:
                top, low = 1 << (m.bit_length() - 1), m & -m
                first = self.plane(total[m][0].astype(BF16), top).astype(F32)
                total[m ^ top][0] = total[m ^ top][0] + first
                second = self.plane(total[m][1].astype(BF16), low).astype(F32)
                total[m ^ low][1] = total[m ^ low][1] + second
        near = jnp.concatenate(total[0], axis=axis)
        mine = lax.slice_in_dim(near, 0, width, axis=other)
        give = lax.slice_in_dim(near, width, 2 * width, axis=other)
        mine = mine + self.half(give.astype(BF16)).astype(F32)
        keep = lax.dynamic_slice_in_dim(mine, self.c * size, size, axis=axis)
        give = lax.dynamic_slice_in_dim(mine, (1 - self.c) * size, size, axis=axis)
        got = self.core(give.astype(BF16)).astype(F32)
        first = self.c == 0
        return jnp.concatenate(
            [jnp.where(first, keep, got), jnp.where(first, got, keep)], axis=other
        )

    def role(self, vector):
        width = vector.shape[0] // 2
        mine = lax.dynamic_slice_in_dim(vector, self.c * width, width)
        return jnp.concatenate([mine, self.half(mine)])

    def unrole(self, vector):
        width = vector.shape[0] // 2
        table = jnp.zeros((self.tp, 2, width), vector.dtype)
        for k, h in enumerate((self.h, 1 - self.h)):
            piece = vector[k * width : (k + 1) * width].reshape(1, 1, width)
            table = lax.dynamic_update_slice(table, piece, (h * self.n + self.l, self.c, 0))
        return table.reshape(self.tp * 2 * width)


def shards(
    fsdp,
    tp,
    inputs,
    query_weight,
    query_bias,
    key_weight,
    value_weight,
    value_bias,
    output_weight,
    output_bias,
    first_gain,
    first_shift,
    up_weight,
    up_bias,
    down_weight,
    down_bias,
    second_gain,
    second_shift,
    segments,
    cotangent,
):
    lay = Layout(fsdp, tp)
    length = segments.shape[1]
    local = query_weight.shape[1] // HD
    rows_own = inputs.shape[0]

    def heads(table):
        return table.reshape(length, local, HD)

    query_full = lay.spread(query_weight, 0)
    key_full = lay.spread(key_weight, 0)
    value_full = lay.spread(value_weight, 0)
    output_full = lay.spread(output_weight, 1)
    up_full = lay.spread(up_weight, 0)
    down_full = lay.spread(down_weight, 1)

    own = lay.trade(lay.relative(inputs))
    own_cot = lay.trade(lay.relative(cotangent)).astype(F32)
    labels = jnp.where(lay.c == lay.h, segments[0], lay.core(segments[0]))
    label_parts = []
    for step in range(lay.n):
        for core in (lay.c, 1 - lay.c):
            at = (core * lay.n + (lay.l + lay.n - step) % lay.n) * rows_own
            label_parts.append(lax.dynamic_slice_in_dim(labels, at, rows_own))
    labels = jnp.concatenate(label_parts)
    output_bias, first_gain, first_shift, down_bias, second_gain, second_shift = (
        lay.relative(v)
        for v in (output_bias, first_gain, first_shift, down_bias, second_gain, second_shift)
    )
    query_bias, value_bias, up_bias = (lay.role(v) for v in (query_bias, value_bias, up_bias))

    rows_all = lay.gather(own)
    query = (project(rows_all, query_full) + query_bias).astype(BF16)
    keys = project(rows_all, key_full).astype(BF16)
    value = (project(rows_all, value_full) + value_bias).astype(BF16)
    context, log_total = attend(heads(query), heads(keys), heads(value), labels)
    context = context.reshape(length, local * HD)

    def rows_at(table, step):
        return table[2 * rows_own * step : 2 * rows_own * (step + 1)]

    attn = lay.reduce(lambda step: project(rows_at(context, step), output_full))
    first_sum = own.astype(F32) + attn + output_bias
    first_normed, first_inv = normalize(first_sum)
    first_out = first_normed * first_gain + first_shift
    mid_all = lay.gather(first_out.astype(BF16))
    pre = project(mid_all, up_full) + up_bias
    active, gelu_back = jax.vjp(gelu_tanh, pre)
    hidden = active.astype(BF16)
    ffn = lay.reduce(lambda step: project(rows_at(hidden, step), down_full))
    second_sum = first_out + ffn + down_bias
    second_normed, second_inv = normalize(second_sum)
    final = second_normed * second_gain + second_shift
    layer_out = lay.relative(lay.trade(final.astype(BF16)))

    d_second, second_gain_term, second_shift_term = norm_back(
        own_cot, second_normed, second_inv, second_gain
    )
    down_bias_term = jnp.sum(d_second, axis=0)
    d_branch_all = lay.gather(d_second.astype(BF16))
    d_hidden = against(d_branch_all, down_full)
    d_pre = gelu_back(d_hidden)[0].astype(BF16)
    up_bias_term = jnp.sum(d_pre.astype(F32), axis=0)
    d_mid = lay.reduce(lambda step: against(rows_at(d_pre, step), up_full))
    down_term = across(hidden, d_branch_all)
    up_term = across(mid_all, d_pre)
    down_grad = lay.collect(down_term, 1)
    up_grad = lay.collect(up_term, 0)
    d_first = d_mid + d_second
    d_first_sum, first_gain_term, first_shift_term = norm_back(
        d_first, first_normed, first_inv, first_gain
    )
    output_bias_term = jnp.sum(d_first_sum, axis=0)
    d_attn_all = lay.gather(d_first_sum.astype(BF16))
    d_context = against(d_attn_all, output_full).astype(BF16)
    output_term = across(context, d_attn_all)
    output_grad = lay.collect(output_term, 1)
    d_query, d_key, d_value = (
        v.reshape(length, local * HD)
        for v in attend_back(
            heads(query), heads(keys), heads(value), heads(d_context), log_total, labels
        )
    )
    query_bias_term = jnp.sum(d_query.astype(F32), axis=0)
    value_bias_term = jnp.sum(d_value.astype(F32), axis=0)
    d_rows = lay.reduce(
        lambda step: against(rows_at(d_query, step), query_full)
        + against(rows_at(d_key, step), key_full)
        + against(rows_at(d_value, step), value_full)
    )
    input_grad = lay.relative(lay.trade((d_rows + d_first_sum).astype(BF16)))
    query_grad = lay.collect(across(rows_all, d_query), 0)
    key_grad = lay.collect(across(rows_all, d_key), 0)
    value_grad = lay.collect(across(rows_all, d_value), 0)

    def small(terms):
        total = lax.psum(jnp.concatenate(terms), AXES)
        result, at = [], 0
        for term in terms:
            result.append(total[at : at + term.shape[0]])
            at += term.shape[0]
        return result

    f, t = lax.axis_index("fsdp"), lax.axis_index("tp")

    def residual(vector):
        size = vector.shape[0] // (fsdp * tp)
        return lax.dynamic_slice_in_dim(vector, (f * tp + t) * size, size)

    def split(vector):
        size = vector.shape[0] // (fsdp * tp)
        return lax.dynamic_slice_in_dim(vector, (t * fsdp + f) * size, size)[None]

    early = small(
        [
            lay.relative(v)
            for v in (
                down_bias_term,
                second_gain_term,
                second_shift_term,
                output_bias_term,
                first_gain_term,
                first_shift_term,
            )
        ]
        + [lay.unrole(up_bias_term)]
    )
    late = small([lay.unrole(query_bias_term), lay.unrole(value_bias_term)])
    return (
        layer_out,
        input_grad,
        query_grad,
        split(late[0]),
        key_grad,
        value_grad,
        split(late[1]),
        output_grad,
        residual(early[3]),
        residual(early[4]),
        residual(early[5]),
        up_grad,
        split(early[6]),
        down_grad,
        residual(early[0]),
        residual(early[1]),
        residual(early[2]),
    )


def solution(mesh):
    fsdp, tp = mesh.shape["fsdp"], mesh.shape["tp"]

    def body(*arrays):
        return shards(fsdp, tp, *arrays)

    tokens, inner, outer = P(AXES, None), P("fsdp", "tp"), P("tp", "fsdp")
    placed = (
        tokens,
        inner,
        P("tp"),
        inner,
        inner,
        P("tp"),
        outer,
        P(),
        P(),
        P(),
        inner,
        P("tp"),
        outer,
        P(),
        P(),
        P(),
        P("fsdp", None),
        tokens,
    )
    return jax.shard_map(
        body,
        mesh=mesh,
        in_specs=placed,
        out_specs=(
            tokens,
            tokens,
            inner,
            outer,
            inner,
            inner,
            outer,
            outer,
            P(AXES),
            P(AXES),
            P(AXES),
            inner,
            outer,
            outer,
            P(AXES),
            P(AXES),
            P(AXES),
        ),
        check_vma=False,
    )
```

time: 1820 us -> 1060 us (0.58)
  waiting for transfers between devices: 1470 us -> 479 us
  starting transfers between devices: 2.12 us -> 140 us
  other arithmetic: 47.2 us -> 102 us
  local copies, waits for them, and re-layouts: 21.9 us -> 75.4 us
  matrix products: 215 us -> 195 us
    reduce_scatter x10 -> x0, waiting for transfers between devices: 826 us -> none  [the longest x1 144 us: shards(): lax.psum_scatter(project(hidden, outer[1]), 'tp', scatter_dimension=0, ti...]
    all_gather x16 -> x0, waiting for transfers between devices: 586 us -> none  [the longest x2 98.7 us: collect_outer(): lax.all_gather(down_weight, 'fsdp', axis=1, tiled=True)]
    ppermute x0 -> x104, waiting for transfers between devices: none -> 357 us  [move(): return lax.ppermute(value, AXES, pairs)]
    ppermute x0 -> x104, starting transfers between devices: none -> 140 us  [move(): return lax.ppermute(value, AXES, pairs)]
    psum x0 -> x1, waiting for transfers between devices: none -> 122 us  [small(): total = lax.psum(jnp.concatenate(terms), AXES)]
    unnamed x32 -> x1, waiting for transfers between devices: 60.7 us -> 0.02 us
    psum x0 -> x1, blocking collectives: none -> 41.3 us  [small(): total = lax.psum(jnp.concatenate(terms), AXES)]
    unnamed x1 -> x0, blocking collectives: 39.3 us -> none
  transfers between devices with their start and end apart: 29 -> 105, of which waited for: 25 -> 41; matrix products, arithmetic and copies ran while one was open for 13% -> 26% of each run, Pallas kernels for 0% -> 0%
where the time goes in v1:
time: 1060 us; the launch traced here: 1050 us
  waiting for transfers between devices  479 us (45%)
  matrix products  195 us (18%)
  starting transfers between devices  140 us (13%)
  other arithmetic  102 us (10%)
  local copies, waits for them, and re-layouts  75.4 us (7%)
  blocking collectives  41.3 us (4%)
  between operations  17 us (2%)
    ppermute x104, waiting for transfers between devices, move(): return lax.ppermute(value, AXES, pairs)  357 us
    ppermute x104, starting transfers between devices, move(): return lax.ppermute(value, AXES, pairs)  140 us
    psum x1, waiting for transfers between devices, small(): total = lax.psum(jnp.concatenate(terms), AXES)  122 us
    dot_general x8, matrix products, project(): return jnp.dot(left, right, preferred_element_type=F32)  54.7 us
    dot_general x10, matrix products, against(): lax.dot_general(left, right, (((1,), (1,)), ((), ())), preferred_element_...  52.8 us
    dot_general x6, matrix products, across(): lax.dot_general(left, right, (((0,), (0,)), ((), ())), preferred_element_...  48.9 us
    unnamed x241, local copies, waits for them, and re-layouts  43.1 us
    psum x1, blocking collectives, small(): total = lax.psum(jnp.concatenate(terms), AXES)  41.3 us
  transfers between devices with their start and end apart: 105, of which 41 were waited for; matrix products, arithmetic and copies ran while one was open for 26% of the time, Pallas kernels for 0%

profile of v1, /device:TPU:1, one launch (start us, length us, event | category | flops | bytes accessed | tf_op | source)
XLA Modules:
  0.0 1051.0 jit_solution(14376118747391334150)
XLA Ops:
  9.8 5.6 collective-permute-start
  24.2 5.1 collective-permute-done.10
  29.3 10.8 %collective-permute-start.19 = (bf16[256,256]{1,0:T(8,128)(2,1)}, bf16[256,256]{1,0:T(8,128)(2,1)S(1)}, u32[]{:S(2)}, u32[]{:S(2)}) collective-permute-start(bf16[256,256]{1,0:T(8,128)(2,1)} %constant_dynamic-slice_fusion.16), channel_id=1, source_target_pairs={{0,4},{1,5},{2,6},{3,7},{4,0},{5,1},{6,2},{7,3},{8,12},{9,13},{10,... | collective-permute-start | bytes 393224 | tf_op jit(solution)/shard_map/ppermute | solution.py:98
  47.5 21.9 %collective-permute-done.5 = bf16[512,256]{1,0:T(8,128)(2,1)S(1)} collective-permute-done((bf16[512,256]{1,0:T(8,128)(2,1)S(1)}, bf16[512,256]{1,0:T(8,128)(2,1)S(1)}, u32[]{:S(2)}, u32[]{:S(2)}) %collective-permute-start.5) | collective-permute-done | bytes 262176 | tf_op jit(solution)/shard_map/ppermute | solution.py:98
  69.5 11.2 %collective-permute-done.13 = bf16[512,256]{1,0:T(8,128)(2,1)S(1)} collective-permute-done((bf16[512,256]{1,0:T(8,128)(2,1)S(1)}, bf16[512,256]{1,0:T(8,128)(2,1)S(1)}, u32[]{:S(2)}, u32[]{:S(2)}) %collective-permute-start.13) | collective-permute-done | bytes 262176 | tf_op jit(solution)/shard_map/ppermute | solution.py:98
  81.9 4.3 collective-permute-done.20
  99.7 4.8 collective-permute-done.14
  111.1 4.7 collective-permute-done.21
  122.2 4.8 collective-permute-done.27
  146.0 5.1 collective-permute-start.3
  165.2 7.6 fusion.125
  172.8 8.0 fusion
  180.8 7.6 fusion.56
  192.7 10.1 collective-permute-done.45
  213.0 41.4 %collective-permute-done.38 = bf16[512,1024]{1,0:T(8,128)(2,1)S(1)} collective-permute-done((bf16[512,1024]{1,0:T(8,128)(2,1)S(1)}, bf16[512,1024]{1,0:T(8,128)(2,1)S(1)}, u32[]{:S(2)}, u32[]{:S(2)}) %collective-permute-start.38) | collective-permute-done | bytes 1048608 | tf_op jit(solution)/shard_map/ppermute | solution.py:98
  263.6 39.1 %collective-permute-done.39 = bf16[512,2048]{1,0:T(8,128)(2,1)S(1)} collective-permute-done((bf16[512,2048]{1,0:T(8,128)(2,1)S(1)}, bf16[512,2048]{1,0:T(8,128)(2,1)S(1)}, u32[]{:S(2)}, u32[]{:S(2)}) %collective-permute-start.39) | collective-permute-done | bytes 2097184 | tf_op jit(solution)/shard_map/ppermute | solution.py:98
  306.8 18.9 %collective-permute-done.48 = bf16[2048,256]{0,1:T(8,128)(2,1)S(1)} collective-permute-done((bf16[2048,256]{0,1:T(8,128)(2,1)S(1)}, bf16[2048,256]{0,1:T(8,128)(2,1)S(1)}, u32[]{:S(2)}, u32[]{:S(2)}) %collective-permute-start.48) | collective-permute-done | bytes 1048608 | tf_op jit(solution)/shard_map/ppermute | solution.py:98
  330.3 17.8 %collective-permute-done.41 = bf16[256,2048]{1,0:T(8,128)(2,1)S(1)} collective-permute-done((bf16[256,2048]{1,0:T(8,128)(2,1)S(1)}, bf16[256,2048]{1,0:T(8,128)(2,1)S(1)}, u32[]{:S(2)}, u32[]{:S(2)}) %collective-permute-start.41) | collective-permute-done | bytes 1048608 | tf_op jit(solution)/shard_map/ppermute | solution.py:98
  350.3 31.0 %multiply_convert_fusion.1 = (bf16[1024,2048]{1,0:T(8,128)(2,1)}, f32[1024,2048]{1,0:T(8,128)}) fusion(f32[2048]{0:T(1024)S(1)} %pad_maximum_fusion.61, bf16[2048,2048]{1,0:T(8,128)(2,1)} %constant_dynamic-update-slice_fusion.20, bf16[256,2048]{1,0:T(8,128)(2,1)S(1)} %collective-permute-done.36, bf16[256,2048]{1,0:T(8,128)(2,1)S(1)} %collective-permute-done.35, ...), kind=kOutput, calls=%fused_computation.20 | convolution fusion | flops 8627683328 | bytes 25174016 | tf_op jit(solution)/shard_map/dot_general | solution.py:15
  381.3 6.4 fusion.44
  389.5 7.2 fusion.49
  398.3 4.4 collective-permute-start.54
  403.0 29.8 %collective-permute-done.52 = bf16[256,2048]{1,0:T(8,128)(2,1)S(1)} collective-permute-done((bf16[256,2048]{1,0:T(8,128)(2,1)S(1)}, bf16[256,2048]{1,0:T(8,128)(2,1)S(1)}, u32[]{:S(2)}, u32[]{:S(2)}) %collective-permute-start.52) | collective-permute-done | bytes 1048608 | tf_op jit(solution)/shard_map/ppermute | solution.py:98
  442.8 19.2 %collective-permute-done.56 = bf16[256,2048]{1,0:T(8,128)(2,1)} collective-permute-done((bf16[256,2048]{1,0:T(8,128)(2,1)S(1)}, bf16[256,2048]{1,0:T(8,128)(2,1)}, u32[]{:S(2)}, u32[]{:S(2)}) %collective-permute-start.56) | collective-permute-done | bytes 1048608 | tf_op jit(solution)/shard_map/ppermute | solution.py:98
  478.0 21.7 %convert_reduce_fusion = (f32[2048]{0:T(1024)S(1)}, bf16[1024,2048]{1,0:T(8,128)(2,1)S(1)}) fusion(f32[1024,2048]{1,0:T(8,128)} %get-tuple-element.207, f32[2048]{0:T(1024)S(1)} %pad_maximum_fusion.61, bf16[2048,2048]{0,1:T(8,128)(2,1)} %copy-done.53, bf16[256,2048]{1,0:T(8,128)(2,1)S(1)} %collective-permute-done.57, ...), kind=kOutput, calls=%fused_computation.18 | convolution fusion | flops 8654944256 | bytes 25182208 | tf_op jit(solution)/shard_map/dot_general | solution.py:19
  499.7 8.5 fusion.37
  508.2 8.5 fusion.41
  520.4 16.8 %fusion.130 = (bf16[2048,2048]{1,0:T(8,128)(2,1)}, f32[2048,2048]{1,0:T(8,128)}) fusion(bf16[1024,2048]{1,0:T(8,128)(2,1)} %copy-done.90, bf16[256,2048]{1,0:T(8,128)(2,1)} %copy-done.84, bf16[256,2048]{1,0:T(8,128)(2,1)} %copy-done.82, bf16[256,2048]{1,0:T(8,128)(2,1)} %copy-done.83, bf16[256,2048]{1,0:T(8,128)(2,1)} %copy-done.49), kind=kOutput, calls=%fused_computation.399 | convolution fusion | flops 8610906112 | bytes 33554432 | tf_op jit(solution)/shard_map/dot_general | solution.py:23
  543.4 16.3 %fusion.131 = (bf16[2048,2048]{0,1:T(8,128)(2,1)}, f32[2048,2048]{0,1:T(8,128)}) fusion(bf16[1024,2048]{1,0:T(8,128)(2,1)} %get-tuple-element.206, bf16[256,2048]{1,0:T(8,128)(2,1)S(1)} %copy-done.88, bf16[256,2048]{1,0:T(8,128)(2,1)} %collective-permute-done.56, bf16[256,2048]{1,0:T(8,128)(2,1)S(1)} %copy-done.86, ...), kind=kOutput, calls=%fused_computation.400 | convolution fusion | flops 8610906112 | bytes 33554432 | tf_op jit(solution)/shard_map/dot_general | solution.py:23
  574.0 14.1 %collective-permute-done.98 = bf16[2048,256]{0,1:T(8,128)(2,1)S(1)} collective-permute-done((bf16[2048,256]{0,1:T(8,128)(2,1)S(1)}, bf16[2048,256]{0,1:T(8,128)(2,1)S(1)}, u32[]{:S(2)}, u32[]{:S(2)}) %collective-permute-start.98) | collective-permute-done | bytes 1048608 | tf_op jit(solution)/shard_map/ppermute | solution.py:98
  604.6 122.1 %all-reduce.2.cloned.1.call-done = f32[20480]{0:T(1024)} async-done(((f32[20480]{0:T(1024)}), f32[20480]{0:T(1024)}) %all-reduce.2.cloned.1.call-update) | async-done | bytes 81936 | tf_op jit(solution)/shard_map/psum | solution.py:341
  756.0 6.3 convolution_convert_fusion
  763.0 9.5 multiply_reduce_fusion
  772.6 8.0 multiply_convert_fusion
  786.2 7.3 multiply_convert_fusion.2
  793.5 4.9 convert_reduce_fusion.2
  813.7 4.5 fusion.127
  820.6 4.8 fusion.126
  827.7 41.3 %psum.14 = f32[4096]{0:T(1024)S(1)} all-reduce(f32[4096]{0:T(1024)S(1)} %pad_maximum_fusion.57), channel_id=1, replica_groups=mesh['fsdp'=8,'tp'=4] {'fsdp','tp'}, use_global_device_ids=true, to_apply=%region_13.14 | all-reduce | flops 4096 | bytes 32768 | tf_op jit(solution)/shard_map/psum | solution.py:341
  916.7 4.5 collective-permute-done.71
  921.2 5.9 collective-permute-start.53
  938.0 5.6 collective-permute-done.83
  954.1 15.3 %collective-permute-done.78 = bf16[512,256]{1,0:T(8,128)(2,1)S(1)} collective-permute-done((bf16[512,256]{1,0:T(8,128)(2,1)S(1)}, bf16[512,256]{1,0:T(8,128)(2,1)S(1)}, u32[]{:S(2)}, u32[]{:S(2)}) %collective-permute-start.78) | collective-permute-done | bytes 262176 | tf_op jit(solution)/shard_map/ppermute | solution.py:98
  969.4 7.0 collective-permute-start.66
  981.0 6.9 collective-permute-start.79
  988.0 15.7 %collective-permute-done.84 = bf16[512,256]{1,0:T(8,128)(2,1)S(1)} collective-permute-done((bf16[512,256]{1,0:T(8,128)(2,1)S(1)}, bf16[512,256]{1,0:T(8,128)(2,1)S(1)}, u32[]{:S(2)}, u32[]{:S(2)}) %collective-permute-start.84) | collective-permute-done | bytes 262176 | tf_op jit(solution)/shard_map/ppermute | solution.py:98
  1005.6 7.0 collective-permute-done.66
  1019.4 21.8 %collective-permute-done.67 = bf16[256,2048]{1,0:T(8,128)(2,1)S(1)} collective-permute-done((bf16[256,2048]{1,0:T(8,128)(2,1)S(1)}, bf16[256,2048]{1,0:T(8,128)(2,1)S(1)}, u32[]{:S(2)}, u32[]{:S(2)}) %collective-permute-start.67) | collective-permute-done | bytes 1048608 | tf_op jit(solution)/shard_map/ppermute | solution.py:98
  (643 shorter events, 323.1 us)
Async XLA Ops:
  7.2 719.5 %all-reduce.2.cloned.1.call-start = ((), (), s32[]{:S(2)}) async-start(), calls=%async_computation | async-start | bytes 163840 | tf_op jit(solution)/shard_map/psum | solution.py:341
  9.8 107.2 %collective-permute-start = (bf16[256,2048]{1,0:T(8,128)(2,1)}, bf16[256,2048]{1,0:T(8,128)(2,1)S(1)}, u32[]{:S(2)}, u32[]{:S(2)}) collective-permute-start(bf16[256,2048]{1,0:T(8,128)(2,1)} %pad_maximum_fusion.15), channel_id=1, source_target_pairs={{0,0},{1,1},{2,4},{3,5},{4,2},{5,3},{6,6},{7,7},{8,8},{9,9},{10,12... | collective-permute-start | bytes 3145736 | tf_op jit(solution)/shard_map/ppermute | solution.py:98
  15.5 26.8 %collective-permute-start.4 = (bf16[256,256]{1,0:T(8,128)(2,1)S(1)}, bf16[256,256]{1,0:T(8,128)(2,1)}, u32[]{:S(2)}, u32[]{:S(2)}) collective-permute-start(bf16[256,256]{1,0:T(8,128)(2,1)S(1)} %constant_dynamic-slice_fusion.18), channel_id=1, source_target_pairs={{0,4},{1,5},{2,6},{3,7},{4,0},{5,1},{6,2},{7,3},{8,12},{9,13},{10,... | collective-permute-start | bytes 393224 | tf_op jit(solution)/shard_map/ppermute | solution.py:98
  16.4 27.3 %collective-permute-start.12 = (bf16[256,256]{1,0:T(8,128)(2,1)}, bf16[256,256]{1,0:T(8,128)(2,1)}, u32[]{:S(2)}, u32[]{:S(2)}) collective-permute-start(bf16[256,256]{1,0:T(8,128)(2,1)} %constant_dynamic-slice_fusion.17), channel_id=1, source_target_pairs={{0,4},{1,5},{2,6},{3,7},{4,0},{5,1},{6,2},{7,3},{8,12},{9,13},{10,... | collective-permute-start | bytes 393224 | tf_op jit(solution)/shard_map/ppermute | solution.py:98
  42.3 50.9 %collective-permute-start.44 = (bf16[1024,256]{0,1:T(8,128)(2,1)}, bf16[1024,256]{0,1:T(8,128)(2,1)S(1)}, u32[]{:S(2)}, u32[]{:S(2)}) collective-permute-start(bf16[1024,256]{0,1:T(8,128)(2,1)} %copy.55), channel_id=1, source_target_pairs={{0,4},{1,5},{2,6},{3,7},{4,0},{5,1},{6,2},{7,3},{8,12},{9,13},{10,... | collective-permute-start | bytes 1572872 | tf_op jit(solution)/shard_map/ppermute | solution.py:98
  44.8 35.9 %collective-permute-start.13 = (bf16[512,256]{1,0:T(8,128)(2,1)S(1)}, bf16[512,256]{1,0:T(8,128)(2,1)S(1)}, u32[]{:S(2)}, u32[]{:S(2)}) collective-permute-start(bf16[512,256]{1,0:T(8,128)(2,1)S(1)} %pad_maximum_fusion.54), channel_id=1, source_target_pairs={{0,2},{1,3},{2,0},{3,1},{4,6},{5,7},{6,4},{7,5},{8,10},{9,11},{10,... | collective-permute-start | bytes 786440 | tf_op jit(solution)/shard_map/ppermute | solution.py:98
  47.3 39.0 %collective-permute-start.20 = (bf16[512,256]{1,0:T(8,128)(2,1)S(1)}, bf16[512,256]{1,0:T(8,128)(2,1)S(1)}, u32[]{:S(2)}, u32[]{:S(2)}) collective-permute-start(bf16[512,256]{1,0:T(8,128)(2,1)S(1)} %pad_maximum_fusion.55), channel_id=1, source_target_pairs={{0,2},{1,3},{2,0},{3,1},{4,6},{5,7},{6,4},{7,5},{8,10},{9,11},{10,... | collective-permute-start | bytes 786440 | tf_op jit(solution)/shard_map/ppermute | solution.py:98
  117.0 29.0 %collective-permute-start.2 = (bf16[256,2048]{1,0:T(8,128)(2,1)S(1)}, bf16[256,2048]{1,0:T(8,128)(2,1)S(1)}, u32[]{:S(2)}, u32[]{:S(2)}) collective-permute-start(bf16[256,2048]{1,0:T(8,128)(2,1)S(1)} %collective-permute-done), channel_id=1, source_target_pairs={{0,1},{1,0},{2,3},{3,2},{4,5},{5,4},{6,7},{7,6},{8,9},{9,8},{10,11... | collective-permute-start | bytes 3145736 | tf_op jit(solution)/shard_map/ppermute | solution.py:98
  152.4 53.4 %collective-permute-start.37 = (bf16[256,1024]{1,0:T(8,128)(2,1)}, bf16[256,1024]{1,0:T(8,128)(2,1)}, u32[]{:S(2)}, u32[]{:S(2)}) collective-permute-start(bf16[256,1024]{1,0:T(8,128)(2,1)} %constant_dynamic-slice_fusion.14), channel_id=1, source_target_pairs={{0,4},{1,5},{2,6},{3,7},{4,0},{5,1},{6,2},{7,3},{8,12},{9,13},{10,... | collective-permute-start | bytes 1572872 | tf_op jit(solution)/shard_map/ppermute | solution.py:98
  154.5 48.3 %collective-permute-start.45 = (bf16[1024,512]{0,1:T(8,128)(2,1)S(1)}, bf16[1024,512]{0,1:T(8,128)(2,1)}, u32[]{:S(2)}, u32[]{:S(2)}) collective-permute-start(bf16[1024,512]{0,1:T(8,128)(2,1)S(1)} %pad_maximum_fusion.17), channel_id=1, source_target_pairs={{0,2},{1,3},{2,0},{3,1},{4,6},{5,7},{6,4},{7,5},{8,10},{9,11},{10,... | collective-permute-start | bytes 3145736 | tf_op jit(solution)/shard_map/ppermute | solution.py:98
  204.5 52.1 %collective-permute-start.46 = (bf16[2048,512]{0,1:T(8,128)(2,1)S(1)}, bf16[2048,512]{0,1:T(8,128)(2,1)S(1)}, u32[]{:S(2)}, u32[]{:S(2)}) collective-permute-start(bf16[2048,512]{0,1:T(8,128)(2,1)S(1)} %get-tuple-element.132), channel_id=1, source_target_pairs={{0,8},{1,9},{2,10},{3,11},{4,12},{5,13},{6,14},{7,15},{8,0},{9,1},... | collective-permute-start | bytes 6291464 | tf_op jit(solution)/shard_map/ppermute | solution.py:98
  207.1 47.2 %collective-permute-start.38 = (bf16[512,1024]{1,0:T(8,128)(2,1)S(1)}, bf16[512,1024]{1,0:T(8,128)(2,1)S(1)}, u32[]{:S(2)}, u32[]{:S(2)}) collective-permute-start(bf16[512,1024]{1,0:T(8,128)(2,1)S(1)} %pad_maximum_fusion.16), channel_id=1, source_target_pairs={{0,2},{1,3},{2,0},{3,1},{4,6},{5,7},{6,4},{7,5},{8,10},{9,11},{10,... | collective-permute-start | bytes 3145736 | tf_op jit(solution)/shard_map/ppermute | solution.py:98
  208.7 49.2 %collective-permute-start.31 = (bf16[256,2048]{1,0:T(8,128)(2,1)S(1)}, bf16[256,2048]{1,0:T(8,128)(2,1)S(1)}, u32[]{:S(2)}, u32[]{:S(2)}) collective-permute-start(bf16[256,2048]{1,0:T(8,128)(2,1)S(1)} %slice.1012), channel_id=1, source_target_pairs={{0,4},{1,5},{2,6},{3,7},{4,0},{5,1},{6,2},{7,3},{8,12},{9,13},{10,... | collective-permute-start | bytes 3145736 | tf_op jit(solution)/shard_map/ppermute | solution.py:98
  209.9 48.1 %collective-permute-start.33 = (bf16[256,2048]{1,0:T(8,128)(2,1)S(1)}, bf16[256,2048]{1,0:T(8,128)(2,1)S(1)}, u32[]{:S(2)}, u32[]{:S(2)}) collective-permute-start(bf16[256,2048]{1,0:T(8,128)(2,1)S(1)} %fusion.51), channel_id=1, source_target_pairs={{0,1},{1,0},{2,3},{3,2},{4,5},{5,4},{6,7},{7,6},{8,9},{9,8},{10,11... | collective-permute-start | bytes 3145736 | tf_op jit(solution)/shard_map/ppermute | solution.py:98
  211.8 50.5 %collective-permute-start.47 = (bf16[2048,512]{0,1:T(8,128)(2,1)S(1)}, bf16[2048,512]{0,1:T(8,128)(2,1)S(1)}, u32[]{:S(2)}, u32[]{:S(2)}) collective-permute-start(bf16[2048,512]{0,1:T(8,128)(2,1)S(1)} %get-tuple-element.132), channel_id=1, source_target_pairs={{0,16},{1,17},{2,18},{3,19},{4,20},{5,21},{6,22},{7,23},{8,24},{9,... | collective-permute-start | bytes 6291464 | tf_op jit(solution)/shard_map/ppermute | solution.py:98
  256.1 46.6 %collective-permute-start.39 = (bf16[512,2048]{1,0:T(8,128)(2,1)S(1)}, bf16[512,2048]{1,0:T(8,128)(2,1)S(1)}, u32[]{:S(2)}, u32[]{:S(2)}) collective-permute-start(bf16[512,2048]{1,0:T(8,128)(2,1)S(1)} %get-tuple-element.130), channel_id=1, source_target_pairs={{0,8},{1,9},{2,10},{3,11},{4,12},{5,13},{6,14},{7,15},{8,0},{9,1},... | collective-permute-start | bytes 6291464 | tf_op jit(solution)/shard_map/ppermute | solution.py:98
  256.6 47.6 %collective-permute-start.40 = (bf16[512,2048]{1,0:T(8,128)(2,1)S(1)}, bf16[512,2048]{1,0:T(8,128)(2,1)S(1)}, u32[]{:S(2)}, u32[]{:S(2)}) collective-permute-start(bf16[512,2048]{1,0:T(8,128)(2,1)S(1)} %get-tuple-element.130), channel_id=1, source_target_pairs={{0,16},{1,17},{2,18},{3,19},{4,20},{5,21},{6,22},{7,23},{8,24},{9,... | collective-permute-start | bytes 6291464 | tf_op jit(solution)/shard_map/ppermute | solution.py:98
  258.0 67.7 %collective-permute-start.48 = (bf16[2048,256]{0,1:T(8,128)(2,1)S(1)}, bf16[2048,256]{0,1:T(8,128)(2,1)S(1)}, u32[]{:S(2)}, u32[]{:S(2)}) collective-permute-start(bf16[2048,256]{0,1:T(8,128)(2,1)S(1)} %slice.689), channel_id=1, source_target_pairs={{0,16},{1,17},{2,18},{3,19},{4,20},{5,21},{6,22},{7,23},{8,24},{9,... | collective-permute-start | bytes 3145736 | tf_op jit(solution)/shard_map/ppermute | solution.py:98
  261.3 67.1 %collective-permute-start.35 = (bf16[256,2048]{1,0:T(8,128)(2,1)S(1)}, bf16[256,2048]{1,0:T(8,128)(2,1)S(1)}, u32[]{:S(2)}, u32[]{:S(2)}) collective-permute-start(bf16[256,2048]{1,0:T(8,128)(2,1)S(1)} %fusion.55), channel_id=1, source_target_pairs={{0,1},{1,0},{2,3},{3,2},{4,5},{5,4},{6,7},{7,6},{8,9},{9,8},{10,11... | collective-permute-start | bytes 3145736 | tf_op jit(solution)/shard_map/ppermute | solution.py:98
  262.3 67.8 %collective-permute-start.49 = (bf16[2048,256]{0,1:T(8,128)(2,1)S(1)}, bf16[2048,256]{0,1:T(8,128)(2,1)S(1)}, u32[]{:S(2)}, u32[]{:S(2)}) collective-permute-start(bf16[2048,256]{0,1:T(8,128)(2,1)S(1)} %slice.690), channel_id=1, source_target_pairs={{0,8},{1,9},{2,10},{3,11},{4,12},{5,13},{6,14},{7,15},{8,0},{9,1},... | collective-permute-start | bytes 3145736 | tf_op jit(solution)/shard_map/ppermute | solution.py:98
  302.9 45.3 %collective-permute-start.41 = (bf16[256,2048]{1,0:T(8,128)(2,1)S(1)}, bf16[256,2048]{1,0:T(8,128)(2,1)S(1)}, u32[]{:S(2)}, u32[]{:S(2)}) collective-permute-start(bf16[256,2048]{1,0:T(8,128)(2,1)S(1)} %slice.686), channel_id=1, source_target_pairs={{0,16},{1,17},{2,18},{3,19},{4,20},{5,21},{6,22},{7,23},{8,24},{9,... | collective-permute-start | bytes 3145736 | tf_op jit(solution)/shard_map/ppermute | solution.py:98
  304.2 45.0 %collective-permute-start.42 = (bf16[256,2048]{1,0:T(8,128)(2,1)S(1)}, bf16[256,2048]{1,0:T(8,128)(2,1)S(1)}, u32[]{:S(2)}, u32[]{:S(2)}) collective-permute-start(bf16[256,2048]{1,0:T(8,128)(2,1)S(1)} %slice.687), channel_id=1, source_target_pairs={{0,8},{1,9},{2,10},{3,11},{4,12},{5,13},{6,14},{7,15},{8,0},{9,1},... | collective-permute-start | bytes 3145736 | tf_op jit(solution)/shard_map/ppermute | solution.py:98
  397.3 35.5 %collective-permute-start.52 = (bf16[256,2048]{1,0:T(8,128)(2,1)S(1)}, bf16[256,2048]{1,0:T(8,128)(2,1)S(1)}, u32[]{:S(2)}, u32[]{:S(2)}) collective-permute-start(bf16[256,2048]{1,0:T(8,128)(2,1)S(1)} %fusion.43), channel_id=1, source_target_pairs={{0,1},{1,0},{2,3},{3,2},{4,5},{5,4},{6,7},{7,6},{8,9},{9,8},{10,11... | collective-permute-start | bytes 3145736 | tf_op jit(solution)/shard_map/ppermute | solution.py:98
  398.3 35.9 %collective-permute-start.54 = (bf16[256,2048]{1,0:T(8,128)(2,1)S(1)}, bf16[256,2048]{1,0:T(8,128)(2,1)S(1)}, u32[]{:S(2)}, u32[]{:S(2)}) collective-permute-start(bf16[256,2048]{1,0:T(8,128)(2,1)S(1)} %pad_maximum_fusion.19), channel_id=1, source_target_pairs={{0,0},{1,1},{2,4},{3,5},{4,2},{5,3},{6,6},{7,7},{8,8},{9,9},{10,12... | collective-permute-start | bytes 3145736 | tf_op jit(solution)/shard_map/ppermute | solution.py:98
  439.0 39.0 %collective-permute-start.55 = (bf16[256,2048]{1,0:T(8,128)(2,1)S(1)}, bf16[256,2048]{1,0:T(8,128)(2,1)S(1)}, u32[]{:S(2)}, u32[]{:S(2)}) collective-permute-start(bf16[256,2048]{1,0:T(8,128)(2,1)S(1)} %convert_element_type.350), channel_id=1, source_target_pairs={{0,4},{1,5},{2,6},{3,7},{4,0},{5,1},{6,2},{7,3},{8,12},{9,13},{10,... | collective-permute-start | bytes 3145736 | tf_op jit(solution)/shard_map/ppermute | solution.py:98
  518.0 44.9 %collective-permute-start.59 = (bf16[256,2048]{1,0:T(8,128)(2,1)}, bf16[256,2048]{1,0:T(8,128)(2,1)}, u32[]{:S(2)}, u32[]{:S(2)}) collective-permute-start(bf16[256,2048]{1,0:T(8,128)(2,1)} %slice.1007), channel_id=1, source_target_pairs={{0,4},{1,5},{2,6},{3,7},{4,0},{5,1},{6,2},{7,3},{8,12},{9,13},{10,... | collective-permute-start | bytes 3145736 | tf_op jit(solution)/shard_map/ppermute | solution.py:98
  520.2 76.2 %collective-permute-start.58 = (bf16[256,2048]{1,0:T(8,128)(2,1)}, bf16[256,2048]{1,0:T(8,128)(2,1)}, u32[]{:S(2)}, u32[]{:S(2)}) collective-permute-start(bf16[256,2048]{1,0:T(8,128)(2,1)} %slice.1008), channel_id=1, source_target_pairs={{0,4},{1,5},{2,6},{3,7},{4,0},{5,1},{6,2},{7,3},{8,12},{9,13},{10,... | collective-permute-start | bytes 3145736 | tf_op jit(solution)/shard_map/ppermute | solution.py:98
  562.9 26.2 %collective-permute-start.100 = (bf16[2048,256]{0,1:T(8,128)(2,1)S(1)}, bf16[2048,256]{0,1:T(8,128)(2,1)S(1)}, u32[]{:S(2)}, u32[]{:S(2)}) collective-permute-start(bf16[2048,256]{0,1:T(8,128)(2,1)S(1)} %get-tuple-element.60), channel_id=1, source_target_pairs={{0,8},{1,9},{2,10},{3,11},{4,12},{5,13},{6,14},{7,15},{8,0},{9,1},... | collective-permute-start | bytes 3145736 | tf_op jit(solution)/shard_map/ppermute | solution.py:98
  565.8 31.2 %collective-permute-start.60 = (bf16[256,2048]{1,0:T(8,128)(2,1)S(1)}, bf16[256,2048]{1,0:T(8,128)(2,1)S(1)}, u32[]{:S(2)}, u32[]{:S(2)}) collective-permute-start(bf16[256,2048]{1,0:T(8,128)(2,1)S(1)} %fusion.36), channel_id=1, source_target_pairs={{0,1},{1,0},{2,3},{3,2},{4,5},{5,4},{6,7},{7,6},{8,9},{9,8},{10,11... | collective-permute-start | bytes 3145736 | tf_op jit(solution)/shard_map/ppermute | solution.py:98
  571.8 160.6 %collective-permute-start.95 = (bf16[512,2048]{1,0:T(8,128)(2,1)}, bf16[512,2048]{1,0:T(8,128)(2,1)}, u32[]{:S(2)}, u32[]{:S(2)}) collective-permute-start(bf16[512,2048]{1,0:T(8,128)(2,1)} %pad_maximum_fusion.10), channel_id=1, source_target_pairs={{0,16},{1,17},{2,18},{3,19},{4,20},{5,21},{6,22},{7,23},{8,24},{9,... | collective-permute-start | bytes 6291464 | tf_op jit(solution)/shard_map/ppermute | solution.py:98
  588.1 146.9 %collective-permute-start.93 = (bf16[512,2048]{1,0:T(8,128)(2,1)}, bf16[512,2048]{1,0:T(8,128)(2,1)}, u32[]{:S(2)}, u32[]{:S(2)}) collective-permute-start(bf16[512,2048]{1,0:T(8,128)(2,1)} %pad_maximum_fusion.9), channel_id=1, source_target_pairs={{0,8},{1,9},{2,10},{3,11},{4,12},{5,13},{6,14},{7,15},{8,0},{9,1},... | collective-permute-start | bytes 6291464 | tf_op jit(solution)/shard_map/ppermute | solution.py:98
  593.6 151.9 %collective-permute-start.101 = (bf16[2048,512]{0,1:T(8,128)(2,1)}, bf16[2048,512]{0,1:T(8,128)(2,1)}, u32[]{:S(2)}, u32[]{:S(2)}) collective-permute-start(bf16[2048,512]{0,1:T(8,128)(2,1)} %pad_maximum_fusion.13), channel_id=1, source_target_pairs={{0,16},{1,17},{2,18},{3,19},{4,20},{5,21},{6,22},{7,23},{8,24},{9,... | collective-permute-start | bytes 6291464 | tf_op jit(solution)/shard_map/ppermute | solution.py:98
  596.4 151.2 %collective-permute-start.99 = (bf16[2048,512]{0,1:T(8,128)(2,1)}, bf16[2048,512]{0,1:T(8,128)(2,1)}, u32[]{:S(2)}, u32[]{:S(2)}) collective-permute-start(bf16[2048,512]{0,1:T(8,128)(2,1)} %pad_maximum_fusion.12), channel_id=1, source_target_pairs={{0,8},{1,9},{2,10},{3,11},{4,12},{5,13},{6,14},{7,15},{8,0},{9,1},... | collective-permute-start | bytes 6291464 | tf_op jit(solution)/shard_map/ppermute | solution.py:98
  601.9 130.4 %collective-permute-start.62 = (bf16[256,2048]{1,0:T(8,128)(2,1)S(1)}, bf16[256,2048]{1,0:T(8,128)(2,1)}, u32[]{:S(2)}, u32[]{:S(2)}) collective-permute-start(bf16[256,2048]{1,0:T(8,128)(2,1)S(1)} %convert_element_type.356), channel_id=1, source_target_pairs={{0,1},{1,0},{2,3},{3,2},{4,5},{5,4},{6,7},{7,6},{8,9},{9,8},{10,11... | collective-permute-start | bytes 3145736 | tf_op jit(solution)/shard_map/ppermute | solution.py:98
  743.1 126.0 %collective-permute-start.96 = (bf16[512,1024]{1,0:T(8,128)(2,1)}, bf16[512,1024]{1,0:T(8,128)(2,1)}, u32[]{:S(2)}, u32[]{:S(2)}) collective-permute-start(bf16[512,1024]{1,0:T(8,128)(2,1)} %fusion.29), channel_id=1, source_target_pairs={{0,2},{1,3},{2,0},{3,1},{4,6},{5,7},{6,4},{7,5},{8,10},{9,11},{10,... | collective-permute-start | bytes 3145736 | tf_op jit(solution)/shard_map/ppermute | solution.py:98
  756.0 121.7 %collective-permute-start.102 = (bf16[1024,512]{0,1:T(8,128)(2,1)}, bf16[1024,512]{0,1:T(8,128)(2,1)}, u32[]{:S(2)}, u32[]{:S(2)}) collective-permute-start(bf16[1024,512]{0,1:T(8,128)(2,1)} %fusion.26), channel_id=1, source_target_pairs={{0,2},{1,3},{2,0},{3,1},{4,6},{5,7},{6,4},{7,5},{8,10},{9,11},{10,... | collective-permute-start | bytes 3145736 | tf_op jit(solution)/shard_map/ppermute | solution.py:98
  819.1 66.7 %collective-permute-start.74 = (bf16[256,512]{1,0:T(8,128)(2,1)}, bf16[256,512]{1,0:T(8,128)(2,1)}, u32[]{:S(2)}, u32[]{:S(2)}) collective-permute-start(bf16[256,512]{1,0:T(8,128)(2,1)} %get-tuple-element.96), channel_id=1, source_target_pairs={{0,16},{1,17},{2,18},{3,19},{4,20},{5,21},{6,22},{7,23},{8,24},{9,... | collective-permute-start | bytes 786440 | tf_op jit(solution)/shard_map/ppermute | solution.py:98
  820.4 66.1 %collective-permute-start.76 = (bf16[256,512]{1,0:T(8,128)(2,1)}, bf16[256,512]{1,0:T(8,128)(2,1)}, u32[]{:S(2)}, u32[]{:S(2)}) collective-permute-start(bf16[256,512]{1,0:T(8,128)(2,1)} %get-tuple-element.97), channel_id=1, source_target_pairs={{0,8},{1,9},{2,10},{3,11},{4,12},{5,13},{6,14},{7,15},{8,0},{9,1},... | collective-permute-start | bytes 786440 | tf_op jit(solution)/shard_map/ppermute | solution.py:98
  826.3 62.8 %collective-permute-start.68 = (bf16[256,512]{1,0:T(8,128)(2,1)}, bf16[256,512]{1,0:T(8,128)(2,1)}, u32[]{:S(2)}, u32[]{:S(2)}) collective-permute-start(bf16[256,512]{1,0:T(8,128)(2,1)} %get-tuple-element.100), channel_id=1, source_target_pairs={{0,16},{1,17},{2,18},{3,19},{4,20},{5,21},{6,22},{7,23},{8,24},{9,... | collective-permute-start | bytes 786440 | tf_op jit(solution)/shard_map/ppermute | solution.py:98
  913.8 29.8 %collective-permute-start.83 = (bf16[512,512]{1,0:T(8,128)(2,1)S(1)}, bf16[512,512]{1,0:T(8,128)(2,1)S(1)}, u32[]{:S(2)}, u32[]{:S(2)}) collective-permute-start(bf16[512,512]{1,0:T(8,128)(2,1)S(1)} %copy-done.56), channel_id=1, source_target_pairs={{0,16},{1,17},{2,18},{3,19},{4,20},{5,21},{6,22},{7,23},{8,24},{9,... | collective-permute-start | bytes 1572872 | tf_op jit(solution)/shard_map/ppermute | solution.py:98
  921.2 98.2 %collective-permute-start.53 = (bf16[256,2048]{1,0:T(8,128)(2,1)S(1)}, bf16[256,2048]{1,0:T(8,128)(2,1)S(1)}, u32[]{:S(2)}, u32[]{:S(2)}) collective-permute-start(bf16[256,2048]{1,0:T(8,128)(2,1)S(1)} %copy-done.48), channel_id=1, source_target_pairs={{0,0},{1,1},{2,4},{3,5},{4,2},{5,3},{6,6},{7,7},{8,8},{9,9},{10,12... | collective-permute-start | bytes 3145736 | tf_op jit(solution)/shard_map/ppermute | solution.py:98
  932.3 73.2 %collective-permute-start.64 = (bf16[256,2048]{1,0:T(8,128)(2,1)S(1)}, bf16[256,2048]{1,0:T(8,128)(2,1)S(1)}, u32[]{:S(2)}, u32[]{:S(2)}) collective-permute-start(bf16[256,2048]{1,0:T(8,128)(2,1)S(1)} %copy-done.42), channel_id=1, source_target_pairs={{0,4},{1,5},{2,6},{3,7},{4,0},{5,1},{6,2},{7,3},{8,12},{9,13},{10,... | collective-permute-start | bytes 3145736 | tf_op jit(solution)/shard_map/ppermute | solution.py:98
  948.0 28.6 %collective-permute-start.72 = (bf16[512,256]{1,0:T(8,128)(2,1)S(1)}, bf16[512,256]{1,0:T(8,128)(2,1)S(1)}, u32[]{:S(2)}, u32[]{:S(2)}) collective-permute-start(bf16[512,256]{1,0:T(8,128)(2,1)S(1)} %fusion.86), channel_id=1, source_target_pairs={{0,2},{1,3},{2,0},{3,1},{4,6},{5,7},{6,4},{7,5},{8,10},{9,11},{10,... | collective-permute-start | bytes 786440 | tf_op jit(solution)/shard_map/ppermute | solution.py:98
  952.4 28.6 %collective-permute-start.90 = (bf16[256,512]{1,0:T(8,128)(2,1)S(1)}, bf16[256,512]{1,0:T(8,128)(2,1)S(1)}, u32[]{:S(2)}, u32[]{:S(2)}) collective-permute-start(bf16[256,512]{1,0:T(8,128)(2,1)S(1)} %fusion.77), channel_id=1, source_target_pairs={{0,2},{1,3},{2,0},{3,1},{4,6},{5,7},{6,4},{7,5},{8,10},{9,11},{10,... | collective-permute-start | bytes 786440 | tf_op jit(solution)/shard_map/ppermute | solution.py:98
  969.4 43.2 %collective-permute-start.66 = (bf16[256,2048]{1,0:T(8,128)(2,1)S(1)}, bf16[256,2048]{1,0:T(8,128)(2,1)S(1)}, u32[]{:S(2)}, u32[]{:S(2)}) collective-permute-start(bf16[256,2048]{1,0:T(8,128)(2,1)S(1)} %fusion.32), channel_id=1, source_target_pairs={{0,1},{1,0},{2,3},{3,2},{4,5},{5,4},{6,7},{7,6},{8,9},{9,8},{10,11... | collective-permute-start | bytes 3145736 | tf_op jit(solution)/shard_map/ppermute | solution.py:98
  976.5 27.2 %collective-permute-start.84 = (bf16[512,256]{1,0:T(8,128)(2,1)S(1)}, bf16[512,256]{1,0:T(8,128)(2,1)S(1)}, u32[]{:S(2)}, u32[]{:S(2)}) collective-permute-start(bf16[512,256]{1,0:T(8,128)(2,1)S(1)} %fusion.80), channel_id=1, source_target_pairs={{0,2},{1,3},{2,0},{3,1},{4,6},{5,7},{6,4},{7,5},{8,10},{9,11},{10,... | collective-permute-start | bytes 786440 | tf_op jit(solution)/shard_map/ppermute | solution.py:98
  981.0 34.7 %collective-permute-start.79 = (bf16[256,256]{1,0:T(8,128)(2,1)S(1)}, bf16[256,256]{1,0:T(8,128)(2,1)S(1)}, u32[]{:S(2)}, u32[]{:S(2)}) collective-permute-start(bf16[256,256]{1,0:T(8,128)(2,1)S(1)} %dynamic-slice_convert_fusion.4), channel_id=1, source_target_pairs={{0,4},{1,5},{2,6},{3,7},{4,0},{5,1},{6,2},{7,3},{8,12},{9,13},{10,... | collective-permute-start | bytes 393224 | tf_op jit(solution)/shard_map/ppermute | solution.py:98
  1013.2 28.1 %collective-permute-start.67 = (bf16[256,2048]{1,0:T(8,128)(2,1)S(1)}, bf16[256,2048]{1,0:T(8,128)(2,1)S(1)}, u32[]{:S(2)}, u32[]{:S(2)}) collective-permute-start(bf16[256,2048]{1,0:T(8,128)(2,1)S(1)} %fusion.35), channel_id=1, source_target_pairs={{0,0},{1,1},{2,4},{3,5},{4,2},{5,3},{6,6},{7,7},{8,8},{9,9},{10,12... | collective-permute-start | bytes 3145736 | tf_op jit(solution)/shard_map/ppermute | solution.py:98
  (152 other events, 2040.8 us)
Sparse Core Ops, SparseCore 0:
  604.1 122.5 all-reduce.1

commit v2 on v1

--- a/solution.py
+++ b/solution.py
@@ -1,6 +1,10 @@
+import functools
+
 import jax
 import jax.numpy as jnp
 from jax import lax
+from jax.experimental import pallas as pl
+from jax.experimental.pallas import tpu as pltpu
 from jax.sharding import PartitionSpec as P
 
 HD = 128
@@ -9,6 +13,8 @@
 AXES = ("fsdp", "tp")
 F32 = jnp.float32
 BF16 = jnp.bfloat16
+MESH = pl.DeviceIdType.MESH
+VMEM = 60 * 2**20
 
 
 def project(left, right):
@@ -221,6 +227,631 @@
         return table.reshape(self.tp * 2 * width)
 
 
+def dot(left, right, dims=((1,), (0,))):
+    return lax.dot_general(left, right, (dims, ((), ())), preferred_element_type=F32)
+
+
+NN, NT, TN = ((1,), (0,)), ((1,), (1,)), ((0,), (0,))
+
+
+class Sizes:
+    def __init__(self, fsdp, tp, inputs, query_weight, up_weight, segments):
+        self.fsdp, self.tp = fsdp, tp
+        self.planes, self.n = fsdp // 2, tp // 2
+        self.rows, self.dim = inputs.shape
+        self.length = segments.shape[1]
+        self.fine = query_weight.shape[0]
+        self.wide = 2 * self.fine
+        self.heads = query_weight.shape[1]
+        self.half = self.heads // 2
+        self.units = up_weight.shape[1]
+        self.uhalf = self.units // 2
+
+
+INNER = (True, True, True, False, True, False)
+
+
+class Links:
+    def __init__(self, size, send, recv):
+        self.size, self.send, self.recv = size, send, recv
+        f, t = lax.axis_index("fsdp"), lax.axis_index("tp")
+        self.g, self.c = f // 2, f % 2
+        self.h, self.l = t // size.n, t % size.n
+        self.done = set()
+        self.sent = []
+        self.next = 0
+
+    def device(self, g, c, h, l):
+        return (g * 2 + c, h * self.size.n + l)
+
+    def mate(self):
+        return self.device(self.g, 1 - self.c, self.h, self.l)
+
+    def across(self):
+        return self.device(self.g, self.c, 1 - self.h, self.l)
+
+    def corner(self):
+        return self.device(self.g, 1 - self.c, 1 - self.h, self.l)
+
+    def plane(self, mask):
+        return self.device(self.g ^ mask, self.c, self.h, self.l)
+
+    def along(self, step):
+        return self.device(self.g, self.c, self.h, (self.l + step) % self.size.n)
+
+    def barrier(self):
+        size = self.size
+        peers = [self.mate(), self.across(), self.corner()]
+        mask = 1
+        while mask < size.planes:
+            peers.append(self.plane(mask))
+            mask *= 2
+        peers += [self.along(step) for step in range(1, size.n)]
+        semaphore = pltpu.get_barrier_semaphore()
+        for peer in peers:
+            pl.semaphore_signal(semaphore, inc=1, device_id=peer, device_id_type=MESH)
+        pl.semaphore_wait(semaphore, len(peers))
+
+    def slots(self, count=1):
+        first = self.next
+        self.next += count
+        return first
+
+    def copy(self, slot, source, target, device):
+        return pltpu.make_async_remote_copy(
+            src_ref=source,
+            dst_ref=target,
+            send_sem=self.send.at[slot],
+            recv_sem=self.recv.at[slot],
+            device_id=device,
+            device_id_type=MESH,
+        )
+
+    def go(self, slot, source, target, device):
+        copy = self.copy(slot, source, target, device)
+        copy.start()
+        self.sent.append(copy)
+        return copy
+
+
+class Local:
+    def __init__(self, semaphores):
+        self.semaphores, self.next = semaphores, 0
+
+    def start(self, source, target):
+        copy = pltpu.make_async_copy(source, target, self.semaphores.at[self.next])
+        self.next += 1
+        copy.start()
+        return copy
+
+
+class Spread:
+    def __init__(self, links, local, shard, full, inner):
+        self.links, self.local = links, local
+        self.shard, self.full, self.inner = shard, full, inner
+        self.base = links.slots(3 + 2 * (links.size.planes - 1))
+        self.waited = set()
+
+    def part(self, index):
+        axis = 1 if self.inner else 0
+        width = self.shard.shape[axis] // 2
+        at = pl.multiple_of(index * width, width)
+        return self.shard.at[:, pl.ds(at, width)] if self.inner else self.shard.at[pl.ds(at, width)]
+
+    def home(self, e, c):
+        fine = self.links.size.fine
+        at = pl.ds(pl.multiple_of(c * fine, fine), fine)
+        if self.inner:
+            return self.full.at[e, at, :]
+        width = self.full.shape[1] // 2
+        return self.full.at[0, pl.ds(e * width, width), at]
+
+    def block(self, m, e=None):
+        wide = self.links.size.wide
+        if self.inner:
+            at = pl.ds(m * wide, wide)
+            return self.full.at[:, at, :] if e is None else self.full.at[e, at, :]
+        width = self.full.shape[1] // 2
+        return self.full.at[m] if e is None else self.full.at[m, pl.ds(e * width, width)]
+
+    def first(self):
+        k = self.links
+        mine, other = self.part(k.c), self.part(1 - k.c)
+        self.own = self.local.start(mine, self.home(0, k.c))
+        self.steps = [
+            k.go(self.base, other, self.home(0, k.c), k.mate()),
+            k.go(self.base + 1, mine, self.home(1, k.c), k.across()),
+            k.go(self.base + 2, other, self.home(1, k.c), k.corner()),
+        ]
+
+    def second(self):
+        k = self.links
+        for step in self.steps:
+            step.wait_recv()
+        self.own.wait()
+        self.pieces = {}
+        mask = 1
+        while mask < k.size.planes:
+            copy = k.go(self.base + 1 + 2 * mask, self.block(0), self.block(mask), k.plane(mask))
+            self.pieces[mask, 0] = self.pieces[mask, 1] = copy
+            mask *= 2
+
+    def arrive(self, m, e):
+        copy = self.pieces[m, e]
+        if id(copy) not in self.waited:
+            self.waited.add(id(copy))
+            copy.wait_recv()
+
+    def third(self):
+        k = self.links
+        for m in sorted(range(1, k.size.planes), key=lambda v: bin(v).count("1")):
+            if bin(m).count("1") > 1:
+                top, low = 1 << (m.bit_length() - 1), m & -m
+                for e, bit in ((0, top), (1, low)):
+                    self.arrive(m ^ bit, e)
+                    self.pieces[m, e] = k.go(
+                        self.base + 1 + 2 * m + e,
+                        self.block(m ^ bit, e),
+                        self.block(m, e),
+                        k.plane(bit),
+                    )
+
+    def finish(self):
+        for m in range(1, self.links.size.planes):
+            for e in range(2):
+                self.arrive(m, e)
+
+
+class Activations:
+    def __init__(self, links, rows, give, take, out, came):
+        self.links, self.rows = links, rows
+        self.give, self.take, self.out, self.came = give, take, out, came
+        size = links.size
+        self.gather_slots = links.slots(2 * size.n)
+        self.mate_slots = links.slots(size.n * size.planes)
+        self.along_slots = links.slots(size.n * size.planes)
+
+    def piece(self, index):
+        size = self.links.size
+        return self.rows.at[pl.ds(index * size.rows, size.rows)]
+
+    def gather_start(self):
+        k, base = self.links, self.gather_slots
+        self.far = [
+            k.go(base + step, self.piece(0), self.piece(2 * step), k.along(step))
+            for step in range(1, k.size.n)
+        ]
+        self.near = [k.go(base + k.size.n, self.piece(0), self.piece(1), k.mate())]
+
+    def gather_relay(self):
+        k, base = self.links, self.gather_slots
+        for step in range(1, k.size.n):
+            self.far[step - 1].wait_recv()
+            self.near.append(
+                k.go(
+                    base + k.size.n + step,
+                    self.piece(2 * step),
+                    self.piece(2 * step + 1),
+                    k.mate(),
+                )
+            )
+
+    def gather_wait(self, step):
+        self.near[step].wait_recv()
+
+    def gather_end(self):
+        over = self.far + self.near
+        for copy in over:
+            copy.wait_send()
+        self.links.sent = [c for c in self.links.sent if all(c is not o for o in over)]
+
+    def reduce(self, tile, put):
+        k = self.links
+        size = k.size
+        planes, n = size.planes, size.n
+
+        def near(step, m):
+            at = step * planes + m
+            return k.copy(self.mate_slots + at, self.give.at[at], self.take.at[at], k.mate())
+
+        def far(step, m):
+            at = (step - 1) * planes + m
+            return k.copy(self.along_slots + at, self.out.at[at], self.came.at[at], k.along(step))
+
+        for step in list(range(1, n)) + [0]:
+            index = 2 * ((n - step) % n)
+
+            @pl.loop(0, planes)
+            def _(m, step=step, index=index):
+                self.give[step * planes + m] = tile(m, index + 1).astype(BF16)
+                near(step, m).start()
+
+            @pl.loop(0, planes)
+            def _(m, step=step, index=index):
+                total = tile(m, index)
+                near(step, m).wait_recv()
+                total = total + self.take[step * planes + m].astype(F32)
+                if step:
+                    self.out[(step - 1) * planes + m] = total.astype(BF16)
+                    far(step, m).start()
+                else:
+                    for other in range(1, n):
+                        far(other, m).wait_recv()
+                        total = total + self.came[(other - 1) * planes + m].astype(F32)
+                    put(m, total)
+
+        @pl.loop(0, planes)
+        def _(m):
+            for step in range(n):
+                near(step, m).wait_send()
+            for step in range(1, n):
+                far(step, m).wait_send()
+
+
+def mean_of(value):
+    return jnp.mean(value, axis=-1, keepdims=True)
+
+
+def forward_kernel(size, *refs):
+    (
+        inputs,
+        cotangent,
+        label_row,
+        label_column,
+        role_bias,
+        residual,
+        *shards_,
+    ) = refs[:12]
+    (
+        fulls_q,
+        fulls_k,
+        fulls_v,
+        fulls_o,
+        fulls_u,
+        fulls_d,
+        rows_out,
+        qkv_out,
+        context_out,
+        lse_out,
+        mid_out,
+        pre_out,
+        hidden_out,
+        normed_out,
+        inverse_out,
+        final_out,
+        d_second_out,
+        sums_out,
+    ) = refs[12:30]
+    (
+        rows,
+        wq,
+        qkv,
+        context,
+        lse,
+        wo,
+        wu,
+        wd,
+        hidden,
+        pre,
+        give,
+        take,
+        out,
+        came,
+        cot,
+        labels_r,
+        labels_c,
+        bias,
+        vectors,
+        send,
+        recv,
+        near_sem,
+    ) = refs[30:]
+    k = Links(size, send, recv)
+    local = Local(near_sem)
+    R, D, L, wide, half, uhalf = (
+        size.rows,
+        size.dim,
+        size.length,
+        size.wide,
+        size.half,
+        size.uhalf,
+    )
+    planes, n = size.planes, size.n
+    k.barrier()
+    stay = k.c == k.h
+
+    fulls = (fulls_q, fulls_k, fulls_v, fulls_o, fulls_u, fulls_d)
+    spread = [Spread(k, local, s, w, i) for s, w, i in zip(shards_, fulls, INNER)]
+    act = Activations(k, rows, give, take, out, came)
+
+    def trade(source, target):
+        base = k.slots(planes)
+        first_local = local.next
+        local.next += planes
+
+        def pieces(m):
+            at = pl.multiple_of((k.g ^ m) * wide, wide)
+            return source.at[:, pl.ds(at, wide)], target(m)
+
+        @pl.when(stay)
+        def _():
+            for m in range(planes):
+                a, b = pieces(m)
+                pltpu.make_async_copy(a, b, near_sem.at[first_local + m]).start()
+
+        @pl.when(jnp.logical_not(stay))
+        def _():
+            for m in range(planes):
+                a, b = pieces(m)
+                k.copy(base + m, a, b, k.corner()).start()
+
+        def wait():
+            @pl.when(stay)
+            def _():
+                for m in range(planes):
+                    a, b = pieces(m)
+                    pltpu.make_async_copy(a, b, near_sem.at[first_local + m]).wait()
+
+            @pl.when(jnp.logical_not(stay))
+            def _():
+                for m in range(planes):
+                    a, b = pieces(m)
+                    k.copy(base + m, a, b, k.corner()).wait()
+
+        return wait
+
+    rows_ready = trade(inputs, lambda m: rows.at[pl.ds(0, R), pl.ds(m * wide, wide)])
+    for index in range(3):
+        spread[index].first()
+
+    label_slots = k.slots(2)
+    label_pairs = ((label_row, labels_r), (label_column, labels_c))
+
+    @pl.when(stay)
+    def _():
+        for index, (a, b) in enumerate(label_pairs):
+            k.copy(label_slots + index, a, b, k.mate()).start()
+
+    label_local = local.next
+    local.next += 2
+
+    @pl.when(stay)
+    def _():
+        for index, (a, b) in enumerate(label_pairs):
+            pltpu.make_async_copy(a, b, near_sem.at[label_local + index]).start()
+
+    bias_slot = k.slots()
+    bias_copy = k.go(bias_slot, role_bias.at[k.c], bias.at[1], k.across())
+    bias_local = local.start(role_bias.at[k.c], bias.at[0])
+
+    for m in range(planes):
+        vectors[:, pl.ds(m * wide, wide)] = residual[k.g ^ m]
+
+    rows_ready()
+    act.gather_start()
+    spread[0].second()
+    spread[3].first()
+    spread[1].second()
+    spread[2].second()
+    spread[4].first()
+    act.gather_relay()
+
+    saved = []
+    loads = {}
+
+    def load(index, buffer):
+        spread[index].finish()
+        loads[index] = local.start(fulls[index], buffer)
+
+    for index in range(3):
+        spread[index].third()
+    spread[3].second()
+    for step in range(n):
+        act.gather_wait(step)
+    saved.append(local.start(rows, rows_out))
+    bias_copy.wait_recv()
+    bias_local.wait()
+
+    @pl.when(stay)
+    def _():
+        for index, (a, b) in enumerate(label_pairs):
+            pltpu.make_async_copy(a, b, near_sem.at[label_local + index]).wait()
+            k.copy(label_slots + index, a, b, k.mate()).wait_send()
+
+    @pl.when(jnp.logical_not(stay))
+    def _():
+        for index, (a, b) in enumerate(label_pairs):
+            k.copy(label_slots + index, a, b, k.mate()).wait_recv()
+
+    load(0, wq.at[0])
+    load(1, wq.at[1])
+    for index in range(3):
+        loads[index].wait()
+        for e in range(2):
+            result = dot(rows[...], wq[index % 2, e])
+            if index != 1:
+                at = 0 if index == 0 else half
+                result = result + bias[e, :, pl.ds(at, half)]
+            qkv[index, :, pl.ds(e * half, half)] = result.astype(BF16)
+        if index == 0:
+            load(2, wq.at[0])
+    saved.append(local.start(qkv, qkv_out))
+    act.gather_end()
+
+    spread[4].second()
+    spread[5].first()
+    cot_ready = trade(cotangent, lambda m: cot.at[:, pl.ds(m * wide, wide)])
+    spread[3].third()
+
+    order = []
+    for step in range(n):
+        for core in (k.c, 1 - k.c):
+            order.append(core * n + (k.l + n - step) % n)
+    row = jnp.concatenate([labels_r[q] for q in order], axis=-1)
+    for piece, q in enumerate(order):
+        column = labels_c[pl.ds(pl.multiple_of(q * R, R), R), :]
+        same = column == row
+
+        lane = lax.broadcasted_iota(jnp.int32, (R, HD), 1)
+        where = pl.ds(piece * R, R)
+
+        def one(head, kept, where=where, same=same):
+            at = pl.ds(pl.multiple_of(head * HD, HD), HD)
+            scores = dot(qkv[0, where, at], qkv[1, :, at], NT) * HD ** (-0.5)
+            scores = jnp.where(same, scores, NEG)
+            top = jnp.max(scores, axis=-1, keepdims=True)
+            weights = jnp.exp(scores - top)
+            summed = jnp.sum(weights, axis=-1, keepdims=True)
+            probs = (weights * (1.0 / summed)).astype(BF16)
+            context[where, at] = dot(probs, qkv[2, :, at]).astype(BF16)
+            return jnp.where(lane == head, top + jnp.log(summed), kept)
+
+        lse[where, :] = lax.fori_loop(0, size.heads // HD, one, jnp.zeros((R, HD), F32))
+
+    saved.append(local.start(context, context_out))
+    saved.append(local.start(lse, lse_out))
+
+    load(3, wo)
+    loads[3].wait()
+
+    def attn_tile(m, index):
+        return dot(context[pl.ds(index * R, R), :], wo[m])
+
+    def attn_put(m, value):
+        at = pl.ds(pl.multiple_of(m * wide, wide), wide)
+        normed_out[:, at] = value + rows[pl.ds(0, R), at].astype(F32) + vectors[0:1, at]
+
+    saved[0].wait()
+    act.reduce(attn_tile, attn_put)
+    center = normed_out[...] - mean_of(normed_out[...])
+    inverse = lax.rsqrt(mean_of(center * center) + EPS)
+    normed = center * inverse
+    normed_out[...] = normed
+    inverse_out[...] = inverse
+    rows[pl.ds(0, R), :] = (normed * vectors[1:2, :] + vectors[2:3, :]).astype(BF16)
+    act.gather_start()
+    spread[4].third()
+    spread[5].second()
+    act.gather_relay()
+    load(4, wu)
+    loads[4].wait()
+    tile = min(512, uhalf)
+    for step in range(n):
+        act.gather_wait(step)
+        where = pl.ds(step * 2 * R, 2 * R)
+        for e in range(2):
+
+            @pl.loop(0, uhalf // tile)
+            def _(j, e=e, where=where):
+                at = pl.ds(pl.multiple_of(j * tile, tile), tile)
+                to = pl.ds(pl.multiple_of(e * uhalf + j * tile, tile), tile)
+                skip = pl.ds(pl.multiple_of(2 * half + j * tile, 128), tile)
+                value = dot(rows[where, :], wu[e, :, at]) + bias[e, :, skip]
+                pre[where, to] = value.astype(BF16)
+                hidden[where, to] = gelu_tanh(value).astype(BF16)
+
+    saved.append(local.start(rows, mid_out))
+    saved.append(local.start(pre, pre_out))
+    saved.append(local.start(hidden, hidden_out))
+    act.gather_end()
+    spread[5].third()
+    load(5, wd)
+    loads[5].wait()
+
+    def ffn_tile(m, index):
+        return dot(hidden[pl.ds(index * R, R), :], wd[m])
+
+    def ffn_put(m, value):
+        at = pl.ds(pl.multiple_of(m * wide, wide), wide)
+        first = normed_out[:, at] * vectors[1:2, at] + vectors[2:3, at]
+        d_second_out[:, at] = value + first + vectors[3:4, at]
+
+    act.reduce(ffn_tile, ffn_put)
+    cot_ready()
+    center = d_second_out[...] - mean_of(d_second_out[...])
+    inverse = lax.rsqrt(mean_of(center * center) + EPS)
+    normed = center * inverse
+    final_out[...] = (normed * vectors[4:5, :] + vectors[5:6, :]).astype(BF16)
+    grad = cot[...].astype(F32)
+    scaled = grad * vectors[4:5, :]
+    inner = scaled - mean_of(scaled) - normed * mean_of(scaled * normed)
+    d_second = inverse * inner
+    d_second_out[...] = d_second
+    sums_out[0:1, :] = jnp.sum(d_second, axis=0, keepdims=True)
+    sums_out[1:2, :] = jnp.sum(grad * normed, axis=0, keepdims=True)
+    sums_out[2:3, :] = jnp.sum(grad, axis=0, keepdims=True)
+    for copy in saved[1:]:
+        copy.wait()
+    for copy in k.sent:
+        copy.wait_send()
+
+
+def forward(size, arrays):
+    R, D, L, T = size.rows, size.dim, size.length, size.tp
+    P_, n, wide, half, uhalf = size.planes, size.n, size.wide, size.half, size.uhalf
+    C, U = size.heads, size.units
+    whole = [jax.ShapeDtypeStruct((2, D, half), BF16)] * 3 + [
+        jax.ShapeDtypeStruct((P_, C, wide), BF16),
+        jax.ShapeDtypeStruct((2, D, uhalf), BF16),
+        jax.ShapeDtypeStruct((P_, U, wide), BF16),
+    ]
+    kept = [
+        jax.ShapeDtypeStruct((L, D), BF16),
+        jax.ShapeDtypeStruct((3, L, C), BF16),
+        jax.ShapeDtypeStruct((L, C), BF16),
+        jax.ShapeDtypeStruct((L, HD), F32),
+        jax.ShapeDtypeStruct((L, D), BF16),
+        jax.ShapeDtypeStruct((L, U), BF16),
+        jax.ShapeDtypeStruct((L, U), BF16),
+    ]
+    ends = [
+        jax.ShapeDtypeStruct((R, D), F32),
+        jax.ShapeDtypeStruct((R, 1), F32),
+        jax.ShapeDtypeStruct((R, D), BF16),
+        jax.ShapeDtypeStruct((R, D), F32),
+        jax.ShapeDtypeStruct((3, D), F32),
+    ]
+    anywhere = pl.BlockSpec(memory_space=pl.ANY)
+    vmem = pl.BlockSpec(memory_space=pltpu.VMEM)
+    width = 2 * half + uhalf
+    slots = 6 * (3 + 2 * (P_ - 1)) + 2 * P_ + 3 + 2 * n + 2 * n * P_
+    scratch = [
+        pltpu.VMEM((L, D), BF16),
+        pltpu.VMEM((2, 2, D, half), BF16),
+        pltpu.VMEM((3, L, C), BF16),
+        pltpu.VMEM((L, C), BF16),
+        pltpu.VMEM((L, HD), F32),
+        pltpu.VMEM((P_, C, wide), BF16),
+        pltpu.VMEM((2, D, uhalf), BF16),
+        pltpu.VMEM((P_, U, wide), BF16),
+        pltpu.VMEM((L, U), BF16),
+        pltpu.VMEM((L, U), BF16),
+        pltpu.VMEM((n * P_, R, wide), BF16),
+        pltpu.VMEM((n * P_, R, wide), BF16),
+        pltpu.VMEM((max(n - 1, 1) * P_, R, wide), BF16),
+        pltpu.VMEM((max(n - 1, 1) * P_, R, wide), BF16),
+        pltpu.VMEM((R, D), BF16),
+        pltpu.VMEM((T, 1, R), jnp.int32),
+        pltpu.VMEM((L, 1), jnp.int32),
+        pltpu.VMEM((2, 1, width), F32),
+        pltpu.VMEM((8, D), F32),
+        pltpu.SemaphoreType.DMA((slots,)),
+        pltpu.SemaphoreType.DMA((slots,)),
+        pltpu.SemaphoreType.DMA((32 + 2 * P_,)),
+    ]
+    return pl.pallas_call(
+        functools.partial(forward_kernel, size),
+        out_shape=whole + kept + ends,
+        in_specs=[anywhere, anywhere, vmem, vmem, vmem, vmem] + [anywhere] * 6,
+        out_specs=[anywhere] * 13 + [vmem] * 5,
+        scratch_shapes=scratch,
+        compiler_params=pltpu.CompilerParams(
+            collective_id=0, has_side_effects=True, vmem_limit_bytes=VMEM
+        ),
+        name="forward",
+    )(*arrays)
+
+
 def shards(
     fsdp,
     tp,
@@ -251,15 +882,44 @@
     def heads(table):
         return table.reshape(length, local, HD)
 
-    query_full = lay.spread(query_weight, 0)
-    key_full = lay.spread(key_weight, 0)
-    value_full = lay.spread(value_weight, 0)
-    output_full = lay.spread(output_weight, 1)
-    up_full = lay.spread(up_weight, 0)
-    down_full = lay.spread(down_weight, 1)
-
-    own = lay.trade(lay.relative(inputs))
-    own_cot = lay.trade(lay.relative(cotangent)).astype(F32)
+    size = Sizes(fsdp, tp, inputs, query_weight, up_weight, segments)
+    residual_vectors = jnp.stack(
+        [output_bias, first_gain, first_shift, down_bias, second_gain, second_shift] + [output_bias] * 2
+    )
+    residual_vectors = residual_vectors.reshape(8, size.planes, size.wide).transpose(1, 0, 2)
+    role_bias = jnp.concatenate(
+        [v.reshape(2, -1) for v in (query_bias, value_bias, up_bias)], axis=1
+    )[:, None]
+    results = forward(
+        size,
+        (
+            inputs,
+            cotangent,
+            segments.reshape(tp, 1, rows_own),
+            segments.reshape(length, 1),
+            role_bias,
+            residual_vectors,
+            query_weight,
+            key_weight,
+            value_weight,
+            output_weight,
+            up_weight,
+            down_weight,
+        ),
+    )
+    query_full, key_full, value_full, up_full = (
+        jnp.concatenate([results[i][0], results[i][1]], axis=1) for i in (0, 1, 2, 4)
+    )
+    output_full, down_full = (
+        results[i].transpose(1, 0, 2).reshape(results[i].shape[1], -1) for i in (3, 5)
+    )
+    rows_all, (query, keys, value), context, log_total, mid_all, pre, hidden = results[6:13]
+    first_normed, first_inv, final, d_second, sums = results[13:]
+    log_total = log_total[:, :local].T
+    layer_out = lay.relative(lay.trade(final))
+    down_bias_term, second_gain_term, second_shift_term = sums[0], sums[1], sums[2]
+    first_gain = lay.relative(first_gain)
+    gelu_back = jax.vjp(gelu_tanh, pre.astype(F32))[1]
     labels = jnp.where(lay.c == lay.h, segments[0], lay.core(segments[0]))
     label_parts = []
     for step in range(lay.n):
@@ -267,40 +927,10 @@
             at = (core * lay.n + (lay.l + lay.n - step) % lay.n) * rows_own
             label_parts.append(lax.dynamic_slice_in_dim(labels, at, rows_own))
     labels = jnp.concatenate(label_parts)
-    output_bias, first_gain, first_shift, down_bias, second_gain, second_shift = (
-        lay.relative(v)
-        for v in (output_bias, first_gain, first_shift, down_bias, second_gain, second_shift)
-    )
-    query_bias, value_bias, up_bias = (lay.role(v) for v in (query_bias, value_bias, up_bias))
-
-    rows_all = lay.gather(own)
-    query = (project(rows_all, query_full) + query_bias).astype(BF16)
-    keys = project(rows_all, key_full).astype(BF16)
-    value = (project(rows_all, value_full) + value_bias).astype(BF16)
-    context, log_total = attend(heads(query), heads(keys), heads(value), labels)
-    context = context.reshape(length, local * HD)
 
     def rows_at(table, step):
         return table[2 * rows_own * step : 2 * rows_own * (step + 1)]
 
-    attn = lay.reduce(lambda step: project(rows_at(context, step), output_full))
-    first_sum = own.astype(F32) + attn + output_bias
-    first_normed, first_inv = normalize(first_sum)
-    first_out = first_normed * first_gain + first_shift
-    mid_all = lay.gather(first_out.astype(BF16))
-    pre = project(mid_all, up_full) + up_bias
-    active, gelu_back = jax.vjp(gelu_tanh, pre)
-    hidden = active.astype(BF16)
-    ffn = lay.reduce(lambda step: project(rows_at(hidden, step), down_full))
-    second_sum = first_out + ffn + down_bias
-    second_normed, second_inv = normalize(second_sum)
-    final = second_normed * second_gain + second_shift
-    layer_out = lay.relative(lay.trade(final.astype(BF16)))
-
-    d_second, second_gain_term, second_shift_term = norm_back(
-        own_cot, second_normed, second_inv, second_gain
-    )
-    down_bias_term = jnp.sum(d_second, axis=0)
     d_branch_all = lay.gather(d_second.astype(BF16))
     d_hidden = against(d_branch_all, down_full)
     d_pre = gelu_back(d_hidden)[0].astype(BF16)

time: 1060 us -> 1010 us (0.953)
  Pallas kernels: 0 us -> 338 us
  waiting for transfers between devices: 479 us -> 218 us
  starting transfers between devices: 140 us -> 65.5 us
  matrix products: 195 us -> 136 us
  local copies, waits for them, and re-layouts: 75.4 us -> 92.7 us
  other arithmetic: 102 us -> 88.2 us
    pallas_call x0 -> x1, Pallas kernels: none -> 338 us  [forward(): pl.pallas_call(functools.partial(forward_kernel, size), out_shape=whole +...]
    ppermute x104 -> x51, waiting for transfers between devices: 357 us -> 96.6 us  [move(): return lax.ppermute(value, AXES, pairs)]
    ppermute x104 -> x51, starting transfers between devices: 140 us -> 65.4 us  [move(): return lax.ppermute(value, AXES, pairs)]
    dot_general x9 -> x0, matrix products: 62.3 us -> none  [the longest x8 54.7 us: project(): return jnp.dot(left, right, preferred_element_type=F32)]
    unnamed x241 -> x158, local copies, waits for them, and re-layouts: 43.1 us -> 23.5 us
    transpose x0 -> x4, local copies, waits for them, and re-layouts: none -> 18.3 us  [the longest x2 15.6 us: shards(): results[i].transpose(1, 0, 2).reshape(results[i].shape[1], -1)]
    reduce_sum x6 -> x0, other arithmetic: 12.4 us -> none  [the longest x1 8.01 us: attend(): total = jnp.sum(weights, axis=-1, keepdims=True)]
    squeeze x0 -> x3, local copies, waits for them, and re-layouts: none -> 11.8 us  [shards(): results[i][0]]
  transfers between devices with their start and end apart: 105 -> 52, of which waited for: 41 -> 15; matrix products, arithmetic and copies ran while one was open for 26% -> 26% of each run, Pallas kernels for 0% -> 0%
where the time goes in v2:
time: 1010 us; the launch traced here: 994 us
  Pallas kernels  338 us (33%)
  waiting for transfers between devices  218 us (22%)
  matrix products  136 us (13%)
  local copies, waits for them, and re-layouts  92.7 us (9%)
  other arithmetic  88.2 us (9%)
  starting transfers between devices  65.5 us (6%)
  blocking collectives  41.1 us (4%)
  between operations  15.7 us (2%)
    pallas_call x1, Pallas kernels, forward(): pl.pallas_call(functools.partial(forward_kernel, size), out_shape=whole +...  338 us
    psum x1, waiting for transfers between devices, small(): total = lax.psum(jnp.concatenate(terms), AXES)  121 us
    ppermute x51, waiting for transfers between devices, move(): return lax.ppermute(value, AXES, pairs)  96.6 us
    ppermute x51, starting transfers between devices, move(): return lax.ppermute(value, AXES, pairs)  65.4 us
    dot_general x6, matrix products, across(): lax.dot_general(left, right, (((0,), (0,)), ((), ())), preferred_element_...  48.3 us
    dot_general x10, matrix products, against(): lax.dot_general(left, right, (((1,), (1,)), ((), ())), preferred_element_...  44.1 us
    psum x1, blocking collectives, small(): total = lax.psum(jnp.concatenate(terms), AXES)  41.1 us
    unnamed x158, local copies, waits for them, and re-layouts  23.5 us
  transfers between devices with their start and end apart: 52, of which 15 were waited for; matrix products, arithmetic and copies ran while one was open for 26% of the time, Pallas kernels for 0%

profile of v2, /device:TPU:1, one launch (start us, length us, event | category | flops | bytes accessed | tf_op | source)
XLA Modules:
  0.0 994.4 jit_solution(4508594775365827390)
XLA Ops:
  13.2 337.9 %forward.1 = (bf16[2,2048,256]{2,1,0:T(8,128)(2,1)}, bf16[2,2048,256]{2,1,0:T(8,128)(2,1)}, bf16[2,2048,256]{2,1,0:T(8,128)(2,1)}, bf16[4,512,512]{2,1,0:T(8,128...) custom-call(bf16[256,2048]{1,0:T(8,128)(2,1)} %refs_0_.1, ...), custom_call_target="tpu_custom_call" | custom-call | tf_op jit(solution)/shard_map/forward/pallas_call | solution.py:842
  351.1 2.9 convert_element_type.273
  358.0 4.8 collective-permute-start
  367.1 3.1 fusion.80
  381.9 4.3 slice_bitcast_fusion.3
  387.6 6.1 slice_bitcast_fusion.1
  395.0 5.2 collective-permute-start.4
  402.2 4.1 copy.51
  409.5 11.5 %copy.50 = bf16[2048,4,512]{0,2,1:T(8,128)(2,1)} copy(bf16[2048,4,512]{2,0,1:T(8,128)(2,1)} %bitcast.113) | data formatting | bytes 16777216 | tf_op jit(solution)/shard_map/transpose | solution.py:914
  425.6 19.9 %convert_reduce_fusion = (f32[2048]{0:T(1024)S(1)}, bf16[1024,2048]{1,0:T(8,128)(2,1)S(1)}) fusion(bf16[1024,2048]{1,0:T(8,128)(2,1)} %get-tuple-element.41, bf16[2048,2048]{0,1:T(8,128)(2,1)} %bitcast.114, bf16[256,2048]{1,0:T(8,128)(2,1)} %collective-permute-done.4, bf16[256,2048]{1,0:T(8,128)(2,1)} %collective-permute-done.3, ...), kind=kOutput, calls=%fused_computation.17 | convolution fusion | flops 8654944256 | bytes 20979712 | tf_op jit(solution)/shard_map/dot_general | solution.py:25
  445.5 6.2 fusion.11
  451.7 6.4 fusion.12
  458.2 2.9 slice.863
  461.1 2.7 slice.862
  464.4 14.4 %fusion.100 = (bf16[2048,2048]{1,0:T(8,128)(2,1)S(1)}, f32[2048,2048]{1,0:T(8,128)}) fusion(bf16[1024,2048]{1,0:T(8,128)(2,1)S(1)} %copy-done.54, bf16[1024,2048]{1,0:T(8,128)(2,1)} %copy-done.60), kind=kOutput, calls=%fused_computation.286 | convolution fusion | flops 8594128896 | bytes 33554432 | tf_op jit(solution)/shard_map/dot_general | solution.py:29
  482.6 16.6 %fusion.101 = (bf16[2048,2048]{0,1:T(8,128)(2,1)}, f32[2048,2048]{0,1:T(8,128)}) fusion(bf16[1024,2048]{1,0:T(8,128)(2,1)S(1)} %copy-done.53, bf16[256,2048]{1,0:T(8,128)(2,1)} %collective-permute-done.4, bf16[256,2048]{1,0:T(8,128)(2,1)} %collective-permute-done.3, bf16[256,2048]{1,0:T(8,128)(2,1)} %collective-permute-done.2, ...), kind=kOutput, calls=%fused_computation.287 | convolution fusion | flops 8610906112 | bytes 33554432 | tf_op jit(solution)/shard_map/dot_general | solution.py:29
  499.2 2.8 fusion.78
  507.4 3.5 fusion.22
  514.1 14.7 %collective-permute-done.45 = bf16[2048,256]{0,1:T(8,128)(2,1)S(1)} collective-permute-done((bf16[2048,256]{0,1:T(8,128)(2,1)S(1)}, bf16[2048,256]{0,1:T(8,128)(2,1)S(1)}, u32[]{:S(2)}, u32[]{:S(2)}) %collective-permute-start.45) | collective-permute-done | bytes 1048608 | tf_op jit(solution)/shard_map/ppermute | solution.py:104
  530.1 2.9 fusion.19
  545.3 121.1 %all-reduce.2.cloned.1.call-done = f32[20480]{0:T(1024)} async-done(((f32[20480]{0:T(1024)}), f32[20480]{0:T(1024)}) %all-reduce.2.cloned.1.call-update) | async-done | bytes 81936 | tf_op jit(solution)/shard_map/psum | solution.py:971
  676.8 3.6 slice_add_fusion.6
  688.4 3.6 slice_add_fusion
  695.3 3.8 convolution_convert_fusion
  699.2 8.2 fusion.39
  707.4 15.3 %multiply_reduce_fusion = (f32[4,1024]{1,0:T(4,128)}, f32[4,1024,1024]{1,2,0:T(8,128)}) fusion(f32[4,1024,1024]{1,2,0:T(8,128)} %fusion.39, f32[4,1024]{1,0:T(4,128)S(1)} %copy-done.48, bf16[1024,4,128]{0,2,1:T(8,128)(2,1)S(1)} %bitcast.109, bf16[1024,4,128]{0,2,1:T(8,128)(2,1)} %bitcast.111, pred[1024,1024]{0,1:T(8,128)(4,1)} %broadcast_compare_fusion), kind=kOutput, calls=%fused_computation.1 | convolution fusion | flops 1094709248 | bytes 36732928 | tf_op jit(solution)/shard_map/qhd,khd->hqk/dot_general | solution.py:54
  722.7 10.1 %convert_reduce_fusion.1 = (f32[4,128]{1,0:T(4,128)S(1)}, bf16[4,128,1024]{2,1,0:T(8,128)(2,1)}) fusion(bf16[1024,4,128]{0,2,1:T(8,128)(2,1)} %bitcast.116, f32[4,1024,1024]{1,2,0:T(8,128)} %get-tuple-element.217), kind=kOutput, calls=%fused_computation.83 | convolution fusion | flops 1079508480 | bytes 18876416 | tf_op jit(solution)/shard_map/hqk,qhd->khd/dot_general | solution.py:72
  732.8 10.5 %multiply_convert_fusion = bf16[4,1024,1024]{1,2,0:T(8,128)(2,1)} fusion(f32[4,1024,1024]{1,2,0:T(8,128)} %get-tuple-element.217, f32[4,1024,1024]{1,2,0:T(8,128)S(1)} %bitcast.108, f32[4,1024]{1,0:T(4,128)} %get-tuple-element.216), kind=kLoop, calls=%fused_computation | loop fusion | flops 12582912 | bytes 41959424 | tf_op jit(solution)/shard_map/convert_element_type | solution.py:76
  743.3 7.5 multiply_convert_fusion.1
  753.1 5.7 fusion.99
  774.5 4.5 fusion.98
  781.0 41.1 %psum.14 = f32[4096]{0:T(1024)S(1)} all-reduce(f32[4096]{0:T(1024)S(1)} %pad_maximum_fusion.46), channel_id=1, replica_groups=mesh['fsdp'=8,'tp'=4] {'fsdp','tp'}, use_global_device_ids=true, to_apply=%region_5.6 | all-reduce | flops 4096 | bytes 32768 | tf_op jit(solution)/shard_map/psum | solution.py:971
  822.7 4.8 fusion.97
  828.7 3.2 fusion.16
  832.6 2.4 fusion.96
  842.3 3.0 collective-permute-start.44
  865.7 3.2 collective-permute-start.11
  870.0 2.4 collective-permute-done.30
  872.4 3.3 collective-permute-start.12
  879.3 4.4 collective-permute-done.24
  891.3 3.5 collective-permute-done.18
  900.9 11.2 %collective-permute-done.37 = bf16[256,512]{1,0:T(8,128)(2,1)S(1)} collective-permute-done((bf16[256,512]{1,0:T(8,128)(2,1)S(1)}, bf16[256,512]{1,0:T(8,128)(2,1)S(1)}, u32[]{:S(2)}, u32[]{:S(2)}) %collective-permute-start.37) | collective-permute-done | bytes 262176 | tf_op jit(solution)/shard_map/ppermute | solution.py:104
  912.2 6.1 collective-permute-start.38
  918.6 4.6 collective-permute-done.31
  923.4 5.5 collective-permute-done.25
  928.9 3.3 collective-permute-start.32
  936.7 21.6 %collective-permute-done.13 = bf16[256,2048]{1,0:T(8,128)(2,1)S(1)} collective-permute-done((bf16[256,2048]{1,0:T(8,128)(2,1)S(1)}, bf16[256,2048]{1,0:T(8,128)(2,1)S(1)}, u32[]{:S(2)}, u32[]{:S(2)}) %collective-permute-start.13) | collective-permute-done | bytes 1048608 | tf_op jit(solution)/shard_map/ppermute | solution.py:104
  964.4 21.7 %collective-permute-done.14 = bf16[256,2048]{1,0:T(8,128)(2,1)S(1)} collective-permute-done((bf16[256,2048]{1,0:T(8,128)(2,1)S(1)}, bf16[256,2048]{1,0:T(8,128)(2,1)S(1)}, u32[]{:S(2)}, u32[]{:S(2)}) %collective-permute-start.14) | collective-permute-done | bytes 1048608 | tf_op jit(solution)/shard_map/ppermute | solution.py:104
  (386 shorter events, 166.6 us)
Async XLA Ops:
  7.2 659.2 %all-reduce.2.cloned.1.call-start = ((), (), s32[]{:S(2)}) async-start(), calls=%async_computation | async-start | bytes 163840 | tf_op jit(solution)/shard_map/psum | solution.py:971
  354.0 41.0 %collective-permute-start.3 = (bf16[256,2048]{1,0:T(8,128)(2,1)}, bf16[256,2048]{1,0:T(8,128)(2,1)}, u32[]{:S(2)}, u32[]{:S(2)}) collective-permute-start(bf16[256,2048]{1,0:T(8,128)(2,1)} %convert_element_type.273), channel_id=1, source_target_pairs={{0,1},{1,0},{2,3},{3,2},{4,5},{5,4},{6,7},{7,6},{8,9},{9,8},{10,11... | collective-permute-start | bytes 3145736 | tf_op jit(solution)/shard_map/ppermute | solution.py:104
  356.3 69.3 %collective-permute-start.2 = (bf16[256,2048]{1,0:T(8,128)(2,1)}, bf16[256,2048]{1,0:T(8,128)(2,1)}, u32[]{:S(2)}, u32[]{:S(2)}) collective-permute-start(bf16[256,2048]{1,0:T(8,128)(2,1)} %convert_element_type.273), channel_id=1, source_target_pairs={{0,4},{1,5},{2,6},{3,7},{4,0},{5,1},{6,2},{7,3},{8,12},{9,13},{10,... | collective-permute-start | bytes 3145736 | tf_op jit(solution)/shard_map/ppermute | solution.py:104
  358.0 63.1 %collective-permute-start.1 = (s32[1024]{0:T(1024)S(1)}, s32[1024]{0:T(1024)}, u32[]{:S(2)}, u32[]{:S(2)}) collective-permute-start(s32[1024]{0:T(1024)S(1)} %bitcast.139), channel_id=1, source_target_pairs={{0,4},{1,5},{2,6},{3,7},{4,0},{5,1},{6,2},{7,3},{8,12},{9,13},{10,... | collective-permute-start | bytes 12296 | tf_op jit(solution)/shard_map/ppermute | solution.py:104
  358.0 65.5 %collective-permute-start = (bf16[256,2048]{1,0:T(8,128)(2,1)}, bf16[256,2048]{1,0:T(8,128)(2,1)}, u32[]{:S(2)}, u32[]{:S(2)}) collective-permute-start(bf16[256,2048]{1,0:T(8,128)(2,1)} %get-tuple-element.35), channel_id=1, source_target_pairs={{0,0},{1,1},{2,4},{3,5},{4,2},{5,3},{6,6},{7,7},{8,8},{9,9},{10,12... | collective-permute-start | bytes 3145736 | tf_op jit(solution)/shard_map/ppermute | solution.py:104
  395.0 30.6 %collective-permute-start.4 = (bf16[256,2048]{1,0:T(8,128)(2,1)}, bf16[256,2048]{1,0:T(8,128)(2,1)}, u32[]{:S(2)}, u32[]{:S(2)}) collective-permute-start(bf16[256,2048]{1,0:T(8,128)(2,1)} %collective-permute-done.3), channel_id=1, source_target_pairs={{0,4},{1,5},{2,6},{3,7},{4,0},{5,1},{6,2},{7,3},{8,12},{9,13},{10,... | collective-permute-start | bytes 3145736 | tf_op jit(solution)/shard_map/ppermute | solution.py:104
  463.9 39.7 %collective-permute-start.6 = (bf16[256,2048]{1,0:T(8,128)(2,1)}, bf16[256,2048]{1,0:T(8,128)(2,1)}, u32[]{:S(2)}, u32[]{:S(2)}) collective-permute-start(bf16[256,2048]{1,0:T(8,128)(2,1)} %slice.862), channel_id=1, source_target_pairs={{0,4},{1,5},{2,6},{3,7},{4,0},{5,1},{6,2},{7,3},{8,12},{9,13},{10,... | collective-permute-start | bytes 3145736 | tf_op jit(solution)/shard_map/ppermute | solution.py:104
  463.9 72.6 %collective-permute-start.5 = (bf16[256,2048]{1,0:T(8,128)(2,1)}, bf16[256,2048]{1,0:T(8,128)(2,1)S(1)}, u32[]{:S(2)}, u32[]{:S(2)}) collective-permute-start(bf16[256,2048]{1,0:T(8,128)(2,1)} %slice.863), channel_id=1, source_target_pairs={{0,4},{1,5},{2,6},{3,7},{4,0},{5,1},{6,2},{7,3},{8,12},{9,13},{10,... | collective-permute-start | bytes 3145736 | tf_op jit(solution)/shard_map/ppermute | solution.py:104
  480.5 26.0 %collective-permute-start.39 = (bf16[256,2048]{1,0:T(8,128)(2,1)}, bf16[256,2048]{1,0:T(8,128)(2,1)}, u32[]{:S(2)}, u32[]{:S(2)}) collective-permute-start(bf16[256,2048]{1,0:T(8,128)(2,1)} %get-tuple-element.106), channel_id=1, source_target_pairs={{0,16},{1,17},{2,18},{3,19},{4,20},{5,21},{6,22},{7,23},{8,24},{9,... | collective-permute-start | bytes 3145736 | tf_op jit(solution)/shard_map/ppermute | solution.py:104
  482.6 24.8 %collective-permute-start.41 = (bf16[256,2048]{1,0:T(8,128)(2,1)}, bf16[256,2048]{1,0:T(8,128)(2,1)}, u32[]{:S(2)}, u32[]{:S(2)}) collective-permute-start(bf16[256,2048]{1,0:T(8,128)(2,1)} %get-tuple-element.107), channel_id=1, source_target_pairs={{0,8},{1,9},{2,10},{3,11},{4,12},{5,13},{6,14},{7,15},{8,0},{9,1},... | collective-permute-start | bytes 3145736 | tf_op jit(solution)/shard_map/ppermute | solution.py:104
  502.1 26.8 %collective-permute-start.45 = (bf16[2048,256]{0,1:T(8,128)(2,1)S(1)}, bf16[2048,256]{0,1:T(8,128)(2,1)S(1)}, u32[]{:S(2)}, u32[]{:S(2)}) collective-permute-start(bf16[2048,256]{0,1:T(8,128)(2,1)S(1)} %get-tuple-element.102), channel_id=1, source_target_pairs={{0,16},{1,17},{2,18},{3,19},{4,20},{5,21},{6,22},{7,23},{8,24},{9,... | collective-permute-start | bytes 3145736 | tf_op jit(solution)/shard_map/ppermute | solution.py:104
  503.6 26.5 %collective-permute-start.47 = (bf16[2048,256]{0,1:T(8,128)(2,1)S(1)}, bf16[2048,256]{0,1:T(8,128)(2,1)S(1)}, u32[]{:S(2)}, u32[]{:S(2)}) collective-permute-start(bf16[2048,256]{0,1:T(8,128)(2,1)S(1)} %get-tuple-element.103), channel_id=1, source_target_pairs={{0,8},{1,9},{2,10},{3,11},{4,12},{5,13},{6,14},{7,15},{8,0},{9,1},... | collective-permute-start | bytes 3145736 | tf_op jit(solution)/shard_map/ppermute | solution.py:104
  506.5 31.2 %collective-permute-start.7 = (bf16[256,2048]{1,0:T(8,128)(2,1)S(1)}, bf16[256,2048]{1,0:T(8,128)(2,1)S(1)}, u32[]{:S(2)}, u32[]{:S(2)}) collective-permute-start(bf16[256,2048]{1,0:T(8,128)(2,1)S(1)} %fusion.27), channel_id=1, source_target_pairs={{0,1},{1,0},{2,3},{3,2},{4,5},{5,4},{6,7},{7,6},{8,9},{9,8},{10,11... | collective-permute-start | bytes 3145736 | tf_op jit(solution)/shard_map/ppermute | solution.py:104
  512.4 159.7 %collective-permute-start.42 = (bf16[512,2048]{1,0:T(8,128)(2,1)}, bf16[512,2048]{1,0:T(8,128)(2,1)}, u32[]{:S(2)}, u32[]{:S(2)}) collective-permute-start(bf16[512,2048]{1,0:T(8,128)(2,1)} %pad_maximum_fusion.11), channel_id=1, source_target_pairs={{0,16},{1,17},{2,18},{3,19},{4,20},{5,21},{6,22},{7,23},{8,24},{9,... | collective-permute-start | bytes 6291464 | tf_op jit(solution)/shard_map/ppermute | solution.py:104
  528.8 145.8 %collective-permute-start.40 = (bf16[512,2048]{1,0:T(8,128)(2,1)}, bf16[512,2048]{1,0:T(8,128)(2,1)}, u32[]{:S(2)}, u32[]{:S(2)}) collective-permute-start(bf16[512,2048]{1,0:T(8,128)(2,1)} %pad_maximum_fusion.10), channel_id=1, source_target_pairs={{0,8},{1,9},{2,10},{3,11},{4,12},{5,13},{6,14},{7,15},{8,0},{9,1},... | collective-permute-start | bytes 6291464 | tf_op jit(solution)/shard_map/ppermute | solution.py:104
  534.7 149.5 %collective-permute-start.48 = (bf16[2048,512]{0,1:T(8,128)(2,1)}, bf16[2048,512]{0,1:T(8,128)(2,1)}, u32[]{:S(2)}, u32[]{:S(2)}) collective-permute-start(bf16[2048,512]{0,1:T(8,128)(2,1)} %pad_maximum_fusion.14), channel_id=1, source_target_pairs={{0,16},{1,17},{2,18},{3,19},{4,20},{5,21},{6,22},{7,23},{8,24},{9,... | collective-permute-start | bytes 6291464 | tf_op jit(solution)/shard_map/ppermute | solution.py:104
  536.4 149.9 %collective-permute-start.46 = (bf16[2048,512]{0,1:T(8,128)(2,1)}, bf16[2048,512]{0,1:T(8,128)(2,1)}, u32[]{:S(2)}, u32[]{:S(2)}) collective-permute-start(bf16[2048,512]{0,1:T(8,128)(2,1)} %pad_maximum_fusion.13), channel_id=1, source_target_pairs={{0,8},{1,9},{2,10},{3,11},{4,12},{5,13},{6,14},{7,15},{8,0},{9,1},... | collective-permute-start | bytes 6291464 | tf_op jit(solution)/shard_map/ppermute | solution.py:104
  541.4 130.6 %collective-permute-start.9 = (bf16[256,2048]{1,0:T(8,128)(2,1)S(1)}, bf16[256,2048]{1,0:T(8,128)(2,1)}, u32[]{:S(2)}, u32[]{:S(2)}) collective-permute-start(bf16[256,2048]{1,0:T(8,128)(2,1)S(1)} %convert_element_type.280), channel_id=1, source_target_pairs={{0,1},{1,0},{2,3},{3,2},{4,5},{5,4},{6,7},{7,6},{8,9},{9,8},{10,11... | collective-permute-start | bytes 3145736 | tf_op jit(solution)/shard_map/ppermute | solution.py:104
  672.0 21.6 %collective-permute-start.8 = (bf16[256,2048]{1,0:T(8,128)(2,1)S(1)}, bf16[256,2048]{1,0:T(8,128)(2,1)S(1)}, u32[]{:S(2)}, u32[]{:S(2)}) collective-permute-start(bf16[256,2048]{1,0:T(8,128)(2,1)S(1)} %convert_element_type.280), channel_id=1, source_target_pairs={{0,4},{1,5},{2,6},{3,7},{4,0},{5,1},{6,2},{7,3},{8,12},{9,13},{10,... | collective-permute-start | bytes 3145736 | tf_op jit(solution)/shard_map/ppermute | solution.py:104
  672.1 21.6 %collective-permute-start.10 = (bf16[256,2048]{1,0:T(8,128)(2,1)}, bf16[256,2048]{1,0:T(8,128)(2,1)S(1)}, u32[]{:S(2)}, u32[]{:S(2)}) collective-permute-start(bf16[256,2048]{1,0:T(8,128)(2,1)} %collective-permute-done.9), channel_id=1, source_target_pairs={{0,4},{1,5},{2,6},{3,7},{4,0},{5,1},{6,2},{7,3},{8,12},{9,13},{10,... | collective-permute-start | bytes 3145736 | tf_op jit(solution)/shard_map/ppermute | solution.py:104
  681.8 145.7 %collective-permute-start.43 = (bf16[512,1024]{1,0:T(8,128)(2,1)}, bf16[512,1024]{1,0:T(8,128)(2,1)}, u32[]{:S(2)}, u32[]{:S(2)}) collective-permute-start(bf16[512,1024]{1,0:T(8,128)(2,1)} %fusion.20), channel_id=1, source_target_pairs={{0,2},{1,3},{2,0},{3,1},{4,6},{5,7},{6,4},{7,5},{8,10},{9,11},{10,... | collective-permute-start | bytes 3145736 | tf_op jit(solution)/shard_map/ppermute | solution.py:104
  693.3 141.8 %collective-permute-start.49 = (bf16[1024,512]{0,1:T(8,128)(2,1)}, bf16[1024,512]{0,1:T(8,128)(2,1)}, u32[]{:S(2)}, u32[]{:S(2)}) collective-permute-start(bf16[1024,512]{0,1:T(8,128)(2,1)} %fusion.17), channel_id=1, source_target_pairs={{0,2},{1,3},{2,0},{3,1},{4,6},{5,7},{6,4},{7,5},{8,10},{9,11},{10,... | collective-permute-start | bytes 3145736 | tf_op jit(solution)/shard_map/ppermute | solution.py:104
  759.8 78.5 %collective-permute-start.33 = (bf16[512,256]{1,0:T(8,128)(2,1)}, bf16[512,256]{1,0:T(8,128)(2,1)}, u32[]{:S(2)}, u32[]{:S(2)}) collective-permute-start(bf16[512,256]{1,0:T(8,128)(2,1)} %get-tuple-element.135), channel_id=1, source_target_pairs={{0,16},{1,17},{2,18},{3,19},{4,20},{5,21},{6,22},{7,23},{8,24},{9,... | collective-permute-start | bytes 786440 | tf_op jit(solution)/shard_map/ppermute | solution.py:104
  761.0 78.0 %collective-permute-start.35 = (bf16[512,256]{1,0:T(8,128)(2,1)}, bf16[512,256]{1,0:T(8,128)(2,1)}, u32[]{:S(2)}, u32[]{:S(2)}) collective-permute-start(bf16[512,256]{1,0:T(8,128)(2,1)} %get-tuple-element.136), channel_id=1, source_target_pairs={{0,8},{1,9},{2,10},{3,11},{4,12},{5,13},{6,14},{7,15},{8,0},{9,1},... | collective-permute-start | bytes 786440 | tf_op jit(solution)/shard_map/ppermute | solution.py:104
  779.8 61.6 %collective-permute-start.27 = (bf16[256,512]{1,0:T(8,128)(2,1)}, bf16[256,512]{1,0:T(8,128)(2,1)}, u32[]{:S(2)}, u32[]{:S(2)}) collective-permute-start(bf16[256,512]{1,0:T(8,128)(2,1)} %get-tuple-element.139), channel_id=1, source_target_pairs={{0,16},{1,17},{2,18},{3,19},{4,20},{5,21},{6,22},{7,23},{8,24},{9,... | collective-permute-start | bytes 786440 | tf_op jit(solution)/shard_map/ppermute | solution.py:104
  827.6 14.7 %collective-permute-start.29 = (bf16[256,512]{1,0:T(8,128)(2,1)}, bf16[256,512]{1,0:T(8,128)(2,1)S(1)}, u32[]{:S(2)}, u32[]{:S(2)}) collective-permute-start(bf16[256,512]{1,0:T(8,128)(2,1)} %get-tuple-element.140), channel_id=1, source_target_pairs={{0,8},{1,9},{2,10},{3,11},{4,12},{5,13},{6,14},{7,15},{8,0},{9,1},... | collective-permute-start | bytes 786440 | tf_op jit(solution)/shard_map/ppermute | solution.py:104
  835.1 13.5 %collective-permute-start.21 = (bf16[256,512]{1,0:T(8,128)(2,1)S(1)}, bf16[256,512]{1,0:T(8,128)(2,1)S(1)}, u32[]{:S(2)}, u32[]{:S(2)}) collective-permute-start(bf16[256,512]{1,0:T(8,128)(2,1)S(1)} %get-tuple-element.143), channel_id=1, source_target_pairs={{0,16},{1,17},{2,18},{3,19},{4,20},{5,21},{6,22},{7,23},{8,24},{9,... | collective-permute-start | bytes 786440 | tf_op jit(solution)/shard_map/ppermute | solution.py:104
  839.0 12.9 %collective-permute-start.15 = (bf16[256,512]{1,0:T(8,128)(2,1)S(1)}, bf16[256,512]{1,0:T(8,128)(2,1)S(1)}, u32[]{:S(2)}, u32[]{:S(2)}) collective-permute-start(bf16[256,512]{1,0:T(8,128)(2,1)S(1)} %get-tuple-element.147), channel_id=1, source_target_pairs={{0,16},{1,17},{2,18},{3,19},{4,20},{5,21},{6,22},{7,23},{8,24},{9,... | collective-permute-start | bytes 786440 | tf_op jit(solution)/shard_map/ppermute | solution.py:104
  842.3 13.2 %collective-permute-start.44 = (bf16[256,1024]{1,0:T(8,128)(2,1)S(1)}, bf16[256,1024]{1,0:T(8,128)(2,1)S(1)}, u32[]{:S(2)}, u32[]{:S(2)}) collective-permute-start(bf16[256,1024]{1,0:T(8,128)(2,1)S(1)} %dynamic-slice_convert_fusion.1), channel_id=1, source_target_pairs={{0,4},{1,5},{2,6},{3,7},{4,0},{5,1},{6,2},{7,3},{8,12},{9,13},{10,... | collective-permute-start | bytes 1572872 | tf_op jit(solution)/shard_map/ppermute | solution.py:104
  851.9 13.7 %collective-permute-start.34 = (bf16[512,512]{1,0:T(8,128)(2,1)}, bf16[512,512]{1,0:T(8,128)(2,1)}, u32[]{:S(2)}, u32[]{:S(2)}) collective-permute-start(bf16[512,512]{1,0:T(8,128)(2,1)} %pad_maximum_fusion.43), channel_id=1, source_target_pairs={{0,8},{1,9},{2,10},{3,11},{4,12},{5,13},{6,14},{7,15},{8,0},{9,1},... | collective-permute-start | bytes 1572872 | tf_op jit(solution)/shard_map/ppermute | solution.py:104
  852.5 20.0 %collective-permute-start.30 = (bf16[512,512]{1,0:T(8,128)(2,1)}, bf16[512,512]{1,0:T(8,128)(2,1)}, u32[]{:S(2)}, u32[]{:S(2)}) collective-permute-start(bf16[512,512]{1,0:T(8,128)(2,1)} %pad_maximum_fusion.41), channel_id=1, source_target_pairs={{0,16},{1,17},{2,18},{3,19},{4,20},{5,21},{6,22},{7,23},{8,24},{9,... | collective-permute-start | bytes 1572872 | tf_op jit(solution)/shard_map/ppermute | solution.py:104
  855.4 21.5 %collective-permute-start.28 = (bf16[512,512]{1,0:T(8,128)(2,1)}, bf16[512,512]{1,0:T(8,128)(2,1)}, u32[]{:S(2)}, u32[]{:S(2)}) collective-permute-start(bf16[512,512]{1,0:T(8,128)(2,1)} %pad_maximum_fusion.40), channel_id=1, source_target_pairs={{0,8},{1,9},{2,10},{3,11},{4,12},{5,13},{6,14},{7,15},{8,0},{9,1},... | collective-permute-start | bytes 1572872 | tf_op jit(solution)/shard_map/ppermute | solution.py:104
  856.4 27.3 %collective-permute-start.24 = (bf16[512,512]{1,0:T(8,128)(2,1)}, bf16[512,512]{1,0:T(8,128)(2,1)}, u32[]{:S(2)}, u32[]{:S(2)}) collective-permute-start(bf16[512,512]{1,0:T(8,128)(2,1)} %pad_maximum_fusion.38), channel_id=1, source_target_pairs={{0,16},{1,17},{2,18},{3,19},{4,20},{5,21},{6,22},{7,23},{8,24},{9,... | collective-permute-start | bytes 1572872 | tf_op jit(solution)/shard_map/ppermute | solution.py:104
  861.2 26.1 %collective-permute-start.22 = (bf16[512,512]{1,0:T(8,128)(2,1)}, bf16[512,512]{1,0:T(8,128)(2,1)}, u32[]{:S(2)}, u32[]{:S(2)}) collective-permute-start(bf16[512,512]{1,0:T(8,128)(2,1)} %pad_maximum_fusion.37), channel_id=1, source_target_pairs={{0,8},{1,9},{2,10},{3,11},{4,12},{5,13},{6,14},{7,15},{8,0},{9,1},... | collective-permute-start | bytes 1572872 | tf_op jit(solution)/shard_map/ppermute | solution.py:104
  865.7 71.0 %collective-permute-start.11 = (bf16[256,2048]{1,0:T(8,128)(2,1)S(1)}, bf16[256,2048]{1,0:T(8,128)(2,1)S(1)}, u32[]{:S(2)}, u32[]{:S(2)}) collective-permute-start(bf16[256,2048]{1,0:T(8,128)(2,1)S(1)} %copy-done.38), channel_id=1, source_target_pairs={{0,4},{1,5},{2,6},{3,7},{4,0},{5,1},{6,2},{7,3},{8,12},{9,13},{10,... | collective-permute-start | bytes 3145736 | tf_op jit(solution)/shard_map/ppermute | solution.py:104
  872.4 39.7 %collective-permute-start.12 = (bf16[256,2048]{1,0:T(8,128)(2,1)}, bf16[256,2048]{1,0:T(8,128)(2,1)S(1)}, u32[]{:S(2)}, u32[]{:S(2)}) collective-permute-start(bf16[256,2048]{1,0:T(8,128)(2,1)} %slice.860), channel_id=1, source_target_pairs={{0,4},{1,5},{2,6},{3,7},{4,0},{5,1},{6,2},{7,3},{8,12},{9,13},{10,... | collective-permute-start | bytes 3145736 | tf_op jit(solution)/shard_map/ppermute | solution.py:104
  876.9 17.9 %collective-permute-start.18 = (bf16[512,512]{1,0:T(8,128)(2,1)S(1)}, bf16[512,512]{1,0:T(8,128)(2,1)S(1)}, u32[]{:S(2)}, u32[]{:S(2)}) collective-permute-start(bf16[512,512]{1,0:T(8,128)(2,1)S(1)} %copy-done.44), channel_id=1, source_target_pairs={{0,16},{1,17},{2,18},{3,19},{4,20},{5,21},{6,22},{7,23},{8,24},{9,... | collective-permute-start | bytes 1572872 | tf_op jit(solution)/shard_map/ppermute | solution.py:104
  883.7 14.0 %collective-permute-start.16 = (bf16[512,512]{1,0:T(8,128)(2,1)S(1)}, bf16[512,512]{1,0:T(8,128)(2,1)S(1)}, u32[]{:S(2)}, u32[]{:S(2)}) collective-permute-start(bf16[512,512]{1,0:T(8,128)(2,1)S(1)} %copy-done.43), channel_id=1, source_target_pairs={{0,8},{1,9},{2,10},{3,11},{4,12},{5,13},{6,14},{7,15},{8,0},{9,1},... | collective-permute-start | bytes 1572872 | tf_op jit(solution)/shard_map/ppermute | solution.py:104
  887.3 24.7 %collective-permute-start.37 = (bf16[256,512]{1,0:T(8,128)(2,1)S(1)}, bf16[256,512]{1,0:T(8,128)(2,1)S(1)}, u32[]{:S(2)}, u32[]{:S(2)}) collective-permute-start(bf16[256,512]{1,0:T(8,128)(2,1)S(1)} %fusion.52), channel_id=1, source_target_pairs={{0,2},{1,3},{2,0},{3,1},{4,6},{5,7},{6,4},{7,5},{8,10},{9,11},{10,... | collective-permute-start | bytes 786440 | tf_op jit(solution)/shard_map/ppermute | solution.py:104
  894.8 28.5 %collective-permute-start.31 = (bf16[512,256]{1,0:T(8,128)(2,1)S(1)}, bf16[512,256]{1,0:T(8,128)(2,1)S(1)}, u32[]{:S(2)}, u32[]{:S(2)}) collective-permute-start(bf16[512,256]{1,0:T(8,128)(2,1)S(1)} %fusion.55), channel_id=1, source_target_pairs={{0,2},{1,3},{2,0},{3,1},{4,6},{5,7},{6,4},{7,5},{8,10},{9,11},{10,... | collective-permute-start | bytes 786440 | tf_op jit(solution)/shard_map/ppermute | solution.py:104
  897.7 31.2 %collective-permute-start.25 = (bf16[512,256]{1,0:T(8,128)(2,1)S(1)}, bf16[512,256]{1,0:T(8,128)(2,1)S(1)}, u32[]{:S(2)}, u32[]{:S(2)}) collective-permute-start(bf16[512,256]{1,0:T(8,128)(2,1)S(1)} %fusion.58), channel_id=1, source_target_pairs={{0,2},{1,3},{2,0},{3,1},{4,6},{5,7},{6,4},{7,5},{8,10},{9,11},{10,... | collective-permute-start | bytes 786440 | tf_op jit(solution)/shard_map/ppermute | solution.py:104
  912.0 22.5 %collective-permute-start.19 = (bf16[512,256]{1,0:T(8,128)(2,1)S(1)}, bf16[512,256]{1,0:T(8,128)(2,1)S(1)}, u32[]{:S(2)}, u32[]{:S(2)}) collective-permute-start(bf16[512,256]{1,0:T(8,128)(2,1)S(1)} %fusion.61), channel_id=1, source_target_pairs={{0,2},{1,3},{2,0},{3,1},{4,6},{5,7},{6,4},{7,5},{8,10},{9,11},{10,... | collective-permute-start | bytes 786440 | tf_op jit(solution)/shard_map/ppermute | solution.py:104
  912.2 24.4 %collective-permute-start.38 = (bf16[256,256]{1,0:T(8,128)(2,1)S(1)}, bf16[256,256]{1,0:T(8,128)(2,1)S(1)}, u32[]{:S(2)}, u32[]{:S(2)}) collective-permute-start(bf16[256,256]{1,0:T(8,128)(2,1)S(1)} %dynamic-slice_convert_fusion.2), channel_id=1, source_target_pairs={{0,4},{1,5},{2,6},{3,7},{4,0},{5,1},{6,2},{7,3},{8,12},{9,13},{10,... | collective-permute-start | bytes 393224 | tf_op jit(solution)/shard_map/ppermute | solution.py:104
  923.3 35.0 %collective-permute-start.13 = (bf16[256,2048]{1,0:T(8,128)(2,1)S(1)}, bf16[256,2048]{1,0:T(8,128)(2,1)S(1)}, u32[]{:S(2)}, u32[]{:S(2)}) collective-permute-start(bf16[256,2048]{1,0:T(8,128)(2,1)S(1)} %fusion.23), channel_id=1, source_target_pairs={{0,1},{1,0},{2,3},{3,2},{4,5},{5,4},{6,7},{7,6},{8,9},{9,8},{10,11... | collective-permute-start | bytes 3145736 | tf_op jit(solution)/shard_map/ppermute | solution.py:104
  928.9 31.9 %collective-permute-start.32 = (bf16[256,256]{1,0:T(8,128)(2,1)S(1)}, bf16[256,256]{1,0:T(8,128)(2,1)S(1)}, u32[]{:S(2)}, u32[]{:S(2)}) collective-permute-start(bf16[256,256]{1,0:T(8,128)(2,1)S(1)} %dynamic-slice_convert_fusion.3), channel_id=1, source_target_pairs={{0,4},{1,5},{2,6},{3,7},{4,0},{5,1},{6,2},{7,3},{8,12},{9,13},{10,... | collective-permute-start | bytes 393224 | tf_op jit(solution)/shard_map/ppermute | solution.py:104
  934.5 27.2 %collective-permute-start.26 = (bf16[256,256]{1,0:T(8,128)(2,1)S(1)}, bf16[256,256]{1,0:T(8,128)(2,1)S(1)}, u32[]{:S(2)}, u32[]{:S(2)}) collective-permute-start(bf16[256,256]{1,0:T(8,128)(2,1)S(1)} %dynamic-slice_convert_fusion.4), channel_id=1, source_target_pairs={{0,4},{1,5},{2,6},{3,7},{4,0},{5,1},{6,2},{7,3},{8,12},{9,13},{10,... | collective-permute-start | bytes 393224 | tf_op jit(solution)/shard_map/ppermute | solution.py:104
  936.6 27.0 %collective-permute-start.20 = (bf16[256,256]{1,0:T(8,128)(2,1)S(1)}, bf16[256,256]{1,0:T(8,128)(2,1)S(1)}, u32[]{:S(2)}, u32[]{:S(2)}) collective-permute-start(bf16[256,256]{1,0:T(8,128)(2,1)S(1)} %dynamic-slice_convert_fusion.5), channel_id=1, source_target_pairs={{0,4},{1,5},{2,6},{3,7},{4,0},{5,1},{6,2},{7,3},{8,12},{9,13},{10,... | collective-permute-start | bytes 393224 | tf_op jit(solution)/shard_map/ppermute | solution.py:104
  958.9 27.2 %collective-permute-start.14 = (bf16[256,2048]{1,0:T(8,128)(2,1)S(1)}, bf16[256,2048]{1,0:T(8,128)(2,1)S(1)}, u32[]{:S(2)}, u32[]{:S(2)}) collective-permute-start(bf16[256,2048]{1,0:T(8,128)(2,1)S(1)} %fusion.26), channel_id=1, source_target_pairs={{0,0},{1,1},{2,4},{3,5},{4,2},{5,3},{6,6},{7,7},{8,8},{9,9},{10,12... | collective-permute-start | bytes 3145736 | tf_op jit(solution)/shard_map/ppermute | solution.py:104
  (69 other events, 1078.3 us)
Sparse Core Ops, SparseCore 0:
  543.2 123.1 all-reduce.1

commit v3 on v2

--- a/solution.py
+++ b/solution.py
@@ -14,217 +14,11 @@
 F32 = jnp.float32
 BF16 = jnp.bfloat16
 MESH = pl.DeviceIdType.MESH
-VMEM = 60 * 2**20
-
-
-def project(left, right):
-    return jnp.dot(left, right, preferred_element_type=F32)
-
-
-def against(left, right):
-    return lax.dot_general(left, right, (((1,), (1,)), ((), ())), preferred_element_type=F32)
-
-
-def across(left, right):
-    return lax.dot_general(left, right, (((0,), (0,)), ((), ())), preferred_element_type=F32)
-
-
-def normalize(total):
-    center = total - jnp.mean(total, axis=-1, keepdims=True)
-    spread = jnp.mean(center * center, axis=-1, keepdims=True)
-    scale_inv = lax.rsqrt(spread + EPS)
-    return center * scale_inv, scale_inv
-
-
-def norm_back(grad, normed, scale_inv, gain):
-    scaled = grad * gain
-    inner = (
-        scaled
-        - jnp.mean(scaled, axis=-1, keepdims=True)
-        - normed * jnp.mean(scaled * normed, axis=-1, keepdims=True)
-    )
-    return (scale_inv * inner, jnp.sum(grad * normed, axis=0), jnp.sum(grad, axis=0))
+VMEM = 62 * 2**20
 
 
 def gelu_tanh(values):
     return jax.nn.gelu(values, approximate=True)
-
-
-def scores_of(queries, keys, labels):
-    scores = jnp.einsum("qhd,khd->hqk", queries, keys, preferred_element_type=F32) * HD ** (-0.5)
-    same = labels[:, None] == labels[None, :]
-    return jnp.where(same[None], scores, NEG)
-
-
-def attend(queries, keys, values, labels):
-    scores = scores_of(queries, keys, labels)
-    top = jnp.max(scores, axis=-1, keepdims=True)
-    weights = jnp.exp(scores - top)
-    total = jnp.sum(weights, axis=-1, keepdims=True)
-    probs = (weights / total).astype(BF16)
-    context = jnp.einsum("hqk,khd->qhd", probs, values, preferred_element_type=F32).astype(BF16)
-    return context, top[..., 0] + jnp.log(total[..., 0])
-
-
-def attend_back(queries, keys, values, d_context, log_total, labels):
-    probs = jnp.exp(scores_of(queries, keys, labels) - log_total[..., None])
-    probs_low = probs.astype(BF16)
-    d_value = jnp.einsum("hqk,qhd->khd", probs_low, d_context, preferred_element_type=F32).astype(
-        BF16
-    )
-    d_probs = jnp.einsum("qhd,khd->hqk", d_context, values, preferred_element_type=F32)
-    d_scores = (probs * (d_probs - jnp.sum(probs * d_probs, axis=-1, keepdims=True))).astype(BF16)
-    d_query = (
-        jnp.einsum("hqk,khd->qhd", d_scores, keys, preferred_element_type=F32) * HD ** (-0.5)
-    ).astype(BF16)
-    d_key = (
-        jnp.einsum("hqk,qhd->khd", d_scores, queries, preferred_element_type=F32) * HD ** (-0.5)
-    ).astype(BF16)
-    return (d_query, d_key, d_value)
-
-
-class Layout:
-    def __init__(self, fsdp, tp):
-        self.fsdp, self.tp = fsdp, tp
-        self.planes, self.n = fsdp // 2, tp // 2
-        f, t = lax.axis_index("fsdp"), lax.axis_index("tp")
-        self.g, self.c = f // 2, f % 2
-        self.h, self.l = t // self.n, t % self.n
-
-    def move(self, value, rule):
-        pairs = []
-        for g in range(self.planes):
-            for c in range(2):
-                for h in range(2):
-                    for l in range(self.n):
-                        a, b, d, e = rule(g, c, h, l)
-                        here = (g * 2 + c) * self.tp + h * self.n + l
-                        there = (a * 2 + b) * self.tp + d * self.n + e
-                        pairs.append((here, there))
-        return lax.ppermute(value, AXES, pairs)
-
-    def core(self, value):
-        return self.move(value, lambda g, c, h, l: (g, 1 - c, h, l))
-
-    def half(self, value):
-        return self.move(value, lambda g, c, h, l: (g, c, 1 - h, l))
-
-    def trade(self, value):
-        return self.move(value, lambda g, c, h, l: (g, h, c, l))
-
-    def plane(self, value, mask):
-        return self.move(value, lambda g, c, h, l: (g ^ mask, c, h, l))
-
-    def along(self, value, step):
-        return self.move(value, lambda g, c, h, l: (g, c, h, (l + step) % self.n))
-
-    def relative(self, value):
-        size = value.shape[-1] // self.planes
-        parts = [
-            lax.dynamic_slice_in_dim(value, (self.g ^ m) * size, size, axis=value.ndim - 1)
-            for m in range(self.planes)
-        ]
-        return jnp.concatenate(parts, axis=-1)
-
-    def gather(self, own):
-        pieces = []
-        for step in range(self.n):
-            piece = own if step == 0 else self.along(own, step)
-            pieces += [piece, self.core(piece)]
-        return jnp.concatenate(pieces, axis=0)
-
-    def reduce(self, block):
-        total, arrived = None, []
-        for step in list(range(1, self.n)) + [0]:
-            both = block((self.n - step) % self.n)
-            size = both.shape[0] // 2
-            mate = self.core(both[size:].astype(BF16))
-            summed = both[:size] + mate.astype(F32)
-            if step == 0:
-                total = summed
-            else:
-                arrived.append(self.along(summed.astype(BF16), step))
-        for piece in arrived:
-            total = total + piece.astype(F32)
-        return total
-
-    def spread(self, shard, axis):
-        other = 1 - axis
-        width = shard.shape[other] // 2
-        mine = lax.dynamic_slice_in_dim(shard, self.c * width, width, axis=other)
-        give = lax.dynamic_slice_in_dim(shard, (1 - self.c) * width, width, axis=other)
-        got = self.core(give)
-        first = self.c == 0
-        near = jnp.concatenate(
-            [jnp.where(first, mine, got), jnp.where(first, got, mine)], axis=axis
-        )
-        near = jnp.concatenate([near, self.half(near)], axis=other)
-        size = near.shape[axis] // 2
-
-        def part(value, index):
-            return lax.slice_in_dim(value, index * size, (index + 1) * size, axis=axis)
-
-        pieces = {0: (part(near, 0), part(near, 1))}
-        for m in sorted(range(1, self.planes), key=lambda v: bin(v).count("1")):
-            if bin(m).count("1") == 1:
-                whole = self.plane(near, m)
-                pieces[m] = (part(whole, 0), part(whole, 1))
-            else:
-                top, low = 1 << (m.bit_length() - 1), m & -m
-                pieces[m] = (
-                    self.plane(pieces[m ^ top][0], top),
-                    self.plane(pieces[m ^ low][1], low),
-                )
-        return jnp.concatenate([p for m in range(self.planes) for p in pieces[m]], axis=axis)
-
-    def collect(self, grad, axis):
-        other = 1 - axis
-        size = grad.shape[axis] // (2 * self.planes)
-        width = grad.shape[other] // 2
-        total = {
-            m: [
-                lax.slice_in_dim(grad, (2 * m + k) * size, (2 * m + k + 1) * size, axis=axis)
-                for k in range(2)
-            ]
-            for m in range(self.planes)
-        }
-        for m in sorted(range(1, self.planes), key=lambda v: -bin(v).count("1")):
-            if bin(m).count("1") == 1:
-                both = jnp.concatenate([v.astype(BF16) for v in total[m]], axis=axis)
-                both = self.plane(both, m).astype(F32)
-                for k in range(2):
-                    piece = lax.slice_in_dim(both, k * size, (k + 1) * size, axis=axis)
-                    total[0][k] = total[0][k] + piece
-            else:
-                top, low = 1 << (m.bit_length() - 1), m & -m
-                first = self.plane(total[m][0].astype(BF16), top).astype(F32)
-                total[m ^ top][0] = total[m ^ top][0] + first
-                second = self.plane(total[m][1].astype(BF16), low).astype(F32)
-                total[m ^ low][1] = total[m ^ low][1] + second
-        near = jnp.concatenate(total[0], axis=axis)
-        mine = lax.slice_in_dim(near, 0, width, axis=other)
-        give = lax.slice_in_dim(near, width, 2 * width, axis=other)
-        mine = mine + self.half(give.astype(BF16)).astype(F32)
-        keep = lax.dynamic_slice_in_dim(mine, self.c * size, size, axis=axis)
-        give = lax.dynamic_slice_in_dim(mine, (1 - self.c) * size, size, axis=axis)
-        got = self.core(give.astype(BF16)).astype(F32)
-        first = self.c == 0
-        return jnp.concatenate(
-            [jnp.where(first, keep, got), jnp.where(first, got, keep)], axis=other
-        )
-
-    def role(self, vector):
-        width = vector.shape[0] // 2
-        mine = lax.dynamic_slice_in_dim(vector, self.c * width, width)
-        return jnp.concatenate([mine, self.half(mine)])
-
-    def unrole(self, vector):
-        width = vector.shape[0] // 2
-        table = jnp.zeros((self.tp, 2, width), vector.dtype)
-        for k, h in enumerate((self.h, 1 - self.h)):
-            piece = vector[k * width : (k + 1) * width].reshape(1, 1, width)
-            table = lax.dynamic_update_slice(table, piece, (h * self.n + self.l, self.c, 0))
-        return table.reshape(self.tp * 2 * width)
 
 
 def dot(left, right, dims=((1,), (0,))):
@@ -445,47 +239,55 @@
             copy.wait_send()
         self.links.sent = [c for c in self.links.sent if all(c is not o for o in over)]
 
-    def reduce(self, tile, put):
+    def near_copy(self, step, m):
         k = self.links
-        size = k.size
-        planes, n = size.planes, size.n
-
-        def near(step, m):
-            at = step * planes + m
-            return k.copy(self.mate_slots + at, self.give.at[at], self.take.at[at], k.mate())
-
-        def far(step, m):
-            at = (step - 1) * planes + m
-            return k.copy(self.along_slots + at, self.out.at[at], self.came.at[at], k.along(step))
-
-        for step in list(range(1, n)) + [0]:
-            index = 2 * ((n - step) % n)
-
-            @pl.loop(0, planes)
-            def _(m, step=step, index=index):
-                self.give[step * planes + m] = tile(m, index + 1).astype(BF16)
-                near(step, m).start()
-
-            @pl.loop(0, planes)
-            def _(m, step=step, index=index):
-                total = tile(m, index)
-                near(step, m).wait_recv()
-                total = total + self.take[step * planes + m].astype(F32)
-                if step:
-                    self.out[(step - 1) * planes + m] = total.astype(BF16)
-                    far(step, m).start()
-                else:
-                    for other in range(1, n):
-                        far(other, m).wait_recv()
-                        total = total + self.came[(other - 1) * planes + m].astype(F32)
-                    put(m, total)
+        at = step * k.size.planes + m
+        return k.copy(self.mate_slots + at, self.give.at[m], self.take.at[at], k.mate())
+
+    def far_copy(self, step, m):
+        k = self.links
+        at = (step - 1) * k.size.planes + m
+        return k.copy(self.along_slots + at, self.out.at[at], self.came.at[at], k.along(step))
+
+    def reduce_step(self, step, tile, put):
+        planes, n = self.links.size.planes, self.links.size.n
+        index = 2 * ((n - step) % n)
 
         @pl.loop(0, planes)
         def _(m):
-            for step in range(n):
-                near(step, m).wait_send()
+            value = tile(m, index + 1).astype(BF16)
+            if step != 1 and n > 1:
+                self.near_copy(step - 1 if step else n - 1, m).wait_send()
+            self.give[m] = value
+            self.near_copy(step, m).start()
+
+        @pl.loop(0, planes)
+        def _(m):
+            total = tile(m, index)
+            self.near_copy(step, m).wait_recv()
+            total = total + self.take[step * planes + m].astype(F32)
+            if step:
+                self.out[(step - 1) * planes + m] = total.astype(BF16)
+                self.far_copy(step, m).start()
+            else:
+                for other in range(1, n):
+                    self.far_copy(other, m).wait_recv()
+                    total = total + self.came[(other - 1) * planes + m].astype(F32)
+                put(m, total)
+
+    def reduce_end(self):
+        planes, n = self.links.size.planes, self.links.size.n
+
+        @pl.loop(0, planes)
+        def _(m):
+            self.near_copy(0, m).wait_send()
             for step in range(1, n):
-                far(step, m).wait_send()
+                self.far_copy(step, m).wait_send()
+
+    def reduce(self, tile, put):
+        for step in list(range(1, self.links.size.n)) + [0]:
+            self.reduce_step(step, tile, put)
+        self.reduce_end()
 
 
 def mean_of(value):
@@ -521,7 +323,9 @@
         final_out,
         d_second_out,
         sums_out,
-    ) = refs[12:30]
+        label_row_out,
+        label_column_out,
+    ) = refs[12:32]
     (
         rows,
         wq,
@@ -545,7 +349,7 @@
         send,
         recv,
         near_sem,
-    ) = refs[30:]
+    ) = refs[32:]
     k = Links(size, send, recv)
     local = Local(near_sem)
     R, D, L, wide, half, uhalf = (
@@ -688,8 +492,10 @@
         for core in (k.c, 1 - k.c):
             order.append(core * n + (k.l + n - step) % n)
     row = jnp.concatenate([labels_r[q] for q in order], axis=-1)
+    label_row_out[...] = row
     for piece, q in enumerate(order):
         column = labels_c[pl.ds(pl.multiple_of(q * R, R), R), :]
+        label_column_out[pl.ds(piece * R, R), :] = column
         same = column == row
 
         lane = lax.broadcasted_iota(jnp.int32, (R, HD), 1)
@@ -723,12 +529,18 @@
 
     saved[0].wait()
     act.reduce(attn_tile, attn_put)
-    center = normed_out[...] - mean_of(normed_out[...])
-    inverse = lax.rsqrt(mean_of(center * center) + EPS)
-    normed = center * inverse
-    normed_out[...] = normed
-    inverse_out[...] = inverse
-    rows[pl.ds(0, R), :] = (normed * vectors[1:2, :] + vectors[2:3, :]).astype(BF16)
+
+    @pl.loop(0, R // 16)
+    def _(i):
+        at = pl.ds(pl.multiple_of(i * 16, 16), 16)
+        summed = normed_out[at, :]
+        center = summed - mean_of(summed)
+        scale = lax.rsqrt(mean_of(center * center) + EPS)
+        normed = center * scale
+        normed_out[at, :] = normed
+        inverse_out[at, :] = scale
+        rows[at, :] = (normed * vectors[1:2, :] + vectors[2:3, :]).astype(BF16)
+
     act.gather_start()
     spread[4].third()
     spread[5].second()
@@ -768,18 +580,23 @@
 
     act.reduce(ffn_tile, ffn_put)
     cot_ready()
-    center = d_second_out[...] - mean_of(d_second_out[...])
-    inverse = lax.rsqrt(mean_of(center * center) + EPS)
-    normed = center * inverse
-    final_out[...] = (normed * vectors[4:5, :] + vectors[5:6, :]).astype(BF16)
-    grad = cot[...].astype(F32)
-    scaled = grad * vectors[4:5, :]
-    inner = scaled - mean_of(scaled) - normed * mean_of(scaled * normed)
-    d_second = inverse * inner
-    d_second_out[...] = d_second
-    sums_out[0:1, :] = jnp.sum(d_second, axis=0, keepdims=True)
-    sums_out[1:2, :] = jnp.sum(grad * normed, axis=0, keepdims=True)
-    sums_out[2:3, :] = jnp.sum(grad, axis=0, keepdims=True)
+    sums_out[...] = jnp.zeros_like(sums_out)
+
+    @pl.loop(0, R // 16)
+    def _(i):
+        at = pl.ds(pl.multiple_of(i * 16, 16), 16)
+        summed = d_second_out[at, :]
+        center = summed - mean_of(summed)
+        scale = lax.rsqrt(mean_of(center * center) + EPS)
+        normed = center * scale
+        final_out[at, :] = (normed * vectors[4:5, :] + vectors[5:6, :]).astype(BF16)
+        grad = cot[at, :].astype(F32)
+        scaled = grad * vectors[4:5, :]
+        d_second = scale * (scaled - mean_of(scaled) - normed * mean_of(scaled * normed))
+        d_second_out[at, :] = d_second
+        for index, value in enumerate((d_second, grad * normed, grad)):
+            sums_out[index : index + 1, :] += jnp.sum(value, axis=0, keepdims=True)
+
     for copy in saved[1:]:
         copy.wait()
     for copy in k.sent:
@@ -810,6 +627,8 @@
         jax.ShapeDtypeStruct((R, D), BF16),
         jax.ShapeDtypeStruct((R, D), F32),
         jax.ShapeDtypeStruct((3, D), F32),
+        jax.ShapeDtypeStruct((1, L), jnp.int32),
+        jax.ShapeDtypeStruct((L, 1), jnp.int32),
     ]
     anywhere = pl.BlockSpec(memory_space=pl.ANY)
     vmem = pl.BlockSpec(memory_space=pltpu.VMEM)
@@ -826,7 +645,7 @@
         pltpu.VMEM((P_, U, wide), BF16),
         pltpu.VMEM((L, U), BF16),
         pltpu.VMEM((L, U), BF16),
-        pltpu.VMEM((n * P_, R, wide), BF16),
+        pltpu.VMEM((P_, R, wide), BF16),
         pltpu.VMEM((n * P_, R, wide), BF16),
         pltpu.VMEM((max(n - 1, 1) * P_, R, wide), BF16),
         pltpu.VMEM((max(n - 1, 1) * P_, R, wide), BF16),
@@ -843,12 +662,675 @@
         functools.partial(forward_kernel, size),
         out_shape=whole + kept + ends,
         in_specs=[anywhere, anywhere, vmem, vmem, vmem, vmem] + [anywhere] * 6,
-        out_specs=[anywhere] * 13 + [vmem] * 5,
+        out_specs=[anywhere] * 13 + [vmem] * 7,
         scratch_shapes=scratch,
         compiler_params=pltpu.CompilerParams(
             collective_id=0, has_side_effects=True, vmem_limit_bytes=VMEM
         ),
         name="forward",
+    )(*arrays)
+
+
+class Collect:
+    def __init__(self, links, grad, came, last, inner):
+        self.links, self.grad, self.came, self.last, self.inner = links, grad, came, last, inner
+        self.planes = links.size.planes
+        self.base = links.slots(2 * (self.planes - 1) + 3)
+        self.flying = {}
+
+    def block(self, m, e):
+        wide = self.links.size.wide
+        if self.inner:
+            return self.grad.at[e, pl.ds(m * wide, wide), :]
+        width = self.grad.shape[1] // 2
+        return self.grad.at[m, pl.ds(e * width, width), :]
+
+    def home(self, e, c):
+        fine = self.links.size.fine
+        at = pl.ds(pl.multiple_of(c * fine, fine), fine)
+        if self.inner:
+            return self.grad.at[e, at, :]
+        width = self.grad.shape[1] // 2
+        return self.grad.at[0, pl.ds(e * width, width), at]
+
+    @staticmethod
+    def bit(m, e):
+        return m & -m if e else 1 << (m.bit_length() - 1)
+
+    def sources(self, m, e):
+        return [o for o in range(1, self.planes) if o != m and o ^ self.bit(o, e) == m]
+
+    def order(self):
+        count = lambda v: bin(v).count("1")
+        pairs = [(m, e) for m in range(1, self.planes) for e in range(2)]
+        return sorted(pairs, key=lambda p: (-count(p[0]), len(self.sources(*p))))
+
+    def send(self, m, e):
+        self.flying[m, e] = self.links.go(
+            self.base + 2 * (m - 1) + e,
+            self.block(m, e),
+            self.came.at[m - 1, e],
+            self.links.plane(self.bit(m, e)),
+        )
+
+    def ready(self, m):
+        for e in range(2):
+            if m and not self.sources(m, e):
+                self.send(m, e)
+
+    def levels(self):
+        return sorted({bin(m).count("1") for m, e in self.order() if self.sources(m, e)}, reverse=True)
+
+    def advance(self, adder, level):
+        for m, e in self.order():
+            if bin(m).count("1") == level and self.sources(m, e):
+                adder(self, m, e)
+                self.send(m, e)
+
+    def finish(self, adder):
+        k = self.links
+        for e in range(2):
+            adder(self, 0, e)
+        k.go(self.base + 2 * (self.planes - 1), self.home(0, 1 - k.c), self.last.at[1], k.mate())
+        k.go(self.base + 2 * (self.planes - 1) + 1, self.home(1, k.c), self.last.at[2], k.across())
+        k.go(
+            self.base + 2 * (self.planes - 1) + 2,
+            self.home(1, 1 - k.c),
+            self.last.at[3],
+            k.corner(),
+        )
+        self.final = k.sent[-3:]
+
+    def arrive(self):
+        for copy in self.final:
+            copy.wait_recv()
+
+
+def gelu_slope(v):
+    scale = 0.7978845608028654
+    square = v * v
+    t = jnp.tanh(scale * v * (1.0 + 0.044715 * square))
+    return 0.5 * (1.0 + t) + 0.5 * v * (1.0 - t * t) * scale * (1.0 + 3 * 0.044715 * square)
+
+
+def backward_kernel(size, *refs):
+    (
+        full_q,
+        full_k,
+        full_v,
+        full_o,
+        full_u,
+        full_d,
+        rows_in,
+        qkv_in,
+        context_in,
+        lse_in,
+        mid_in,
+        pre_in,
+        hidden_in,
+        normed,
+        inverse,
+        final,
+        d_second,
+        sums,
+        label_row,
+        label_column,
+        residual,
+    ) = refs[:21]
+    (
+        layer_out,
+        input_grad,
+        grad_d,
+        grad_u,
+        grad_o,
+        grad_x,
+        came_d,
+        came_u,
+        came_o,
+        came_x,
+        last_d,
+        last_u,
+        last_o,
+        last_x,
+        small_d,
+        small_q,
+        small_u,
+    ) = refs[21:38]
+    (
+        rows,
+        wbuf,
+        wu,
+        wo,
+        abuf,
+        dp,
+        qkv,
+        dqkv,
+        context,
+        d_context,
+        lse,
+        give,
+        take,
+        out,
+        came,
+        dfs,
+        dk,
+        dv,
+        stage,
+        parts_inner,
+        parts_outer,
+        got_d,
+        got_q,
+        got_u,
+        gain,
+        ends_acc,
+        send,
+        recv,
+        near_sem,
+        stage_sem,
+        part_sem,
+        free_sem,
+    ) = refs[38:]
+    k = Links(size, send, recv)
+    local = Local(near_sem)
+    R, D, L, wide, half, uhalf, T = (
+        size.rows,
+        size.dim,
+        size.length,
+        size.wide,
+        size.half,
+        size.uhalf,
+        size.tp,
+    )
+    planes, n, C, U = size.planes, size.n, size.heads, size.units
+    width = 3 * half
+    act = Activations(k, rows, give, take, out, came)
+    down = Collect(k, grad_d, came_d, last_d, False)
+    up = Collect(k, grad_u, came_u, last_u, True)
+    outer = Collect(k, grad_o, came_o, last_o, False)
+    inner = Collect(k, grad_x, came_x, last_x, True)
+    k.barrier()
+    stay = k.c == k.h
+
+    def trade(source, target):
+        base = k.slots(planes)
+        first_local = local.next
+        local.next += planes
+
+        def pieces(m):
+            at = pl.multiple_of((k.g ^ m) * wide, wide)
+            return source.at[:, pl.ds(m * wide, wide)], target.at[:, pl.ds(at, wide)]
+
+        def both(go):
+            @pl.when(stay)
+            def _():
+                for m in range(planes):
+                    copy = pltpu.make_async_copy(*pieces(m), near_sem.at[first_local + m])
+                    copy.start() if go else copy.wait()
+
+            @pl.when(jnp.logical_not(stay))
+            def _():
+                for m in range(planes):
+                    copy = k.copy(base + m, *pieces(m), k.corner())
+                    copy.start() if go else copy.wait()
+
+        both(True)
+        return lambda: both(False)
+
+    loads = {}
+    start = local.start(d_second, dfs)
+    start.wait()
+    rows[pl.ds(0, R), :] = dfs[...].astype(BF16)
+    act.gather_start()
+    loads["pre"] = [local.start(pre_in, dp)]
+    loads["down"] = [
+        local.start(full_d.at[m], wbuf.at[pl.ds(0, U), pl.ds(m * wide, wide)])
+        for m in range(planes)
+    ]
+    loads["up"] = [local.start(full_u.at[e], wu.at[:, pl.ds(e * uhalf, uhalf)]) for e in range(2)]
+    loads["hidden"] = [local.start(hidden_in, abuf.at[:, pl.ds(0, U)])]
+    layer_done = trade(final, layer_out)
+    loads["attention"] = [
+        local.start(qkv_in, qkv),
+        local.start(context_in, context),
+        local.start(lse_in, lse),
+        local.start(full_o, wo),
+    ]
+    for m in range(planes):
+        gain[:, pl.ds(m * wide, wide)] = residual[k.g ^ m]
+
+    def loaded(name):
+        for copy in loads[name]:
+            copy.wait()
+
+    small_d[...] = jnp.zeros_like(small_d)
+    small_q[...] = jnp.zeros_like(small_q)
+    small_u[...] = jnp.zeros_like(small_u)
+    places = [(k.h * n + k.l) * 2 + k.c, ((1 - k.h) * n + k.l) * 2 + k.c]
+
+    tile = min(512, U)
+    loaded("pre")
+    loaded("down")
+    for step in range(n):
+        if step == 1:
+            act.gather_relay()
+        act.gather_wait(step)
+        where = pl.ds(step * 2 * R, 2 * R)
+
+        @pl.loop(0, U // tile)
+        def _(j, where=where):
+            at = pl.ds(pl.multiple_of(j * tile, tile), tile)
+            d_hidden = dot(rows[where, :], wbuf[at, pl.ds(0, D)], NT)
+            value = (d_hidden * gelu_slope(dp[where, at].astype(F32))).astype(BF16)
+            dp[where, at] = value
+
+    if n == 1:
+        act.gather_relay()
+    act.gather_end()
+    loads["weights"] = [
+        local.start(
+            full.at[e], wbuf.at[pl.ds(0, D), pl.ds(e * width + index * half, half)]
+        )
+        for index, full in enumerate((full_q, full_k, full_v))
+        for e in range(2)
+    ]
+
+    def mid_tile(m, index):
+        at = pl.ds(pl.multiple_of(m * wide, wide), wide)
+        return dot(dp[pl.ds(index * R, R), :], wu[at, :], NT)
+
+    def mid_put(m, value):
+        at = pl.ds(pl.multiple_of(m * wide, wide), wide)
+        dfs[:, at] += value
+
+    def store(count, value, target):
+        def copy(i, slot):
+            piece = target(i)
+            a, b = piece.shape
+            return pltpu.make_async_copy(
+                stage.at[slot, pl.ds(0, a), pl.ds(0, b)], piece, stage_sem.at[slot]
+            )
+
+        @pl.loop(0, count)
+        def _(i):
+            slot = i % 2
+
+            @pl.when(i >= 2)
+            def _():
+                copy(i - 2, slot).wait()
+
+            result = value(i).astype(BF16)
+            stage[slot, pl.ds(0, result.shape[0]), pl.ds(0, result.shape[1])] = result
+            copy(i, slot).start()
+
+        for i in range(max(count - 2, 0), count):
+            copy(i, i % 2).wait()
+
+    def adder(work, m, e):
+        sources = work.sources(m, e)
+        block = work.block(m, e)
+        a, b = block.shape
+        if work.inner:
+            cols = min(256, half, uhalf)
+            count, shape = b // cols, (a, cols)
+        else:
+            lines = min(256, half, uhalf)
+            count, shape = a // lines, (lines, b)
+
+        def piece(ref, i):
+            if work.inner:
+                return ref.at[:, pl.ds(pl.multiple_of(i * shape[1], 128), shape[1])]
+            return ref.at[pl.ds(pl.multiple_of(i * shape[0], 16), shape[0]), :]
+
+        parts = parts_inner if work.inner else parts_outer
+        inputs = [block] + [work.came.at[o - 1, e] for o in sources]
+
+        def fetch(i, slot):
+            return [
+                pltpu.make_async_copy(
+                    piece(ref, i),
+                    parts.at[slot, index, pl.ds(0, shape[0]), pl.ds(0, shape[1])],
+                    part_sem.at[slot, index],
+                )
+                for index, ref in enumerate(inputs)
+            ]
+
+        def put(i, slot):
+            return pltpu.make_async_copy(
+                stage.at[slot, pl.ds(0, shape[0]), pl.ds(0, shape[1])],
+                piece(block, i),
+                stage_sem.at[slot],
+            )
+
+        for o in sources:
+            work.flying[o, e].wait_recv()
+        for copy in fetch(0, 0):
+            copy.start()
+        for i in range(count):
+            slot = i % 2
+            if i + 1 < count:
+                for copy in fetch(i + 1, 1 - slot):
+                    copy.start()
+            for copy in fetch(i, slot):
+                copy.wait()
+            if i >= 2:
+                put(i - 2, slot).wait()
+            total = sum(
+                parts[slot, index, pl.ds(0, shape[0]), pl.ds(0, shape[1])].astype(F32)
+                for index in range(len(inputs))
+            )
+            stage[slot, pl.ds(0, shape[0]), pl.ds(0, shape[1])] = total.astype(BF16)
+            put(i, slot).start()
+        for i in range(max(count - 2, 0), count):
+            put(i, i % 2).wait()
+
+    def piece_order():
+        return sorted(range(planes), key=lambda m: (-bin(m).count("1"), m))
+
+    loaded("up")
+    for step in range(1, n):
+        act.reduce_step(step, mid_tile, mid_put)
+
+    loaded("hidden")
+    lines = min(512, U)
+    for m in piece_order():
+        store(
+            U // lines,
+            lambda i, m=m: dot(
+                abuf[:, pl.ds(pl.multiple_of(i * lines, lines), lines)],
+                rows[:, pl.ds(m * wide, wide)],
+                TN,
+            ),
+            lambda i, m=m: grad_d.at[m, pl.ds(pl.multiple_of(i * lines, lines), lines), :],
+        )
+        down.ready(m)
+    for step in range(1, n):
+        pl.semaphore_signal(free_sem, inc=1, device_id=k.along(step), device_id_type=MESH)
+    loads["mid"] = [local.start(mid_in, abuf.at[:, pl.ds(0, D)])]
+    act.reduce_step(0, mid_tile, mid_put)
+    act.reduce_end()
+
+    ends_acc[...] = jnp.zeros_like(ends_acc)
+    ends_acc[0:3, :] = sums[...]
+
+    @pl.loop(0, R // 16)
+    def _(i):
+        at = pl.ds(pl.multiple_of(i * 16, 16), 16)
+        grad = dfs[at, :]
+        normal = normed[at, :]
+        scaled = grad * gain[1:2, :]
+        d_sum = inverse[at, :] * (
+            scaled - mean_of(scaled) - normal * mean_of(scaled * normal)
+        )
+        rows[at, :] = d_sum.astype(BF16)
+        dfs[at, :] = d_sum
+        for index, value in enumerate((d_sum, grad * normal, grad)):
+            ends_acc[3 + index : 4 + index, :] += jnp.sum(value, axis=0, keepdims=True)
+
+    if n > 1:
+        pl.semaphore_wait(free_sem, n - 1)
+    act.gather_start()
+    for m in range(planes):
+        small_d[k.g ^ m] = ends_acc[:, m * wide : (m + 1) * wide]
+
+    loaded("mid")
+    columns = min(512, uhalf)
+    per = uhalf // columns
+    for m in piece_order():
+        store(
+            2 * per,
+            lambda i, m=m: dot(
+                abuf[:, pl.ds(m * wide, wide)],
+                dp[:, pl.ds(pl.multiple_of(i * columns, columns), columns)],
+                TN,
+            ),
+            lambda i, m=m: grad_u.at[
+                i // per,
+                pl.ds(m * wide, wide),
+                pl.ds(pl.multiple_of((i % per) * columns, columns), columns),
+            ],
+        )
+        up.ready(m)
+        if m == piece_order()[0]:
+            for level in down.levels():
+                down.advance(adder, level)
+    for e in range(2):
+        value = jnp.sum(dp[:, pl.ds(e * uhalf, uhalf)].astype(F32), axis=0, keepdims=True)
+        line = lax.broadcasted_iota(jnp.int32, small_u.shape, 0)
+        small_u[...] = jnp.where(line == places[e], value, small_u[...])
+    loads["rows"] = [local.start(rows_in, abuf.at[:, pl.ds(0, D)])]
+    loaded("attention")
+    for step in range(n):
+        if step == 1:
+            act.gather_relay()
+        act.gather_wait(step)
+        where = pl.ds(step * 2 * R, 2 * R)
+        total = dot(rows[where, pl.ds(0, wide)], wo[0], NT)
+        for m in range(1, planes):
+            total = total + dot(rows[where, pl.ds(m * wide, wide)], wo[m], NT)
+        d_context[where, :] = total.astype(BF16)
+    if n == 1:
+        act.gather_relay()
+    for m in piece_order():
+        store(
+            1,
+            lambda i, m=m: dot(context[...], rows[:, pl.ds(m * wide, wide)], TN),
+            lambda i, m=m: grad_o.at[m],
+        )
+        outer.ready(m)
+    act.gather_end()
+
+    lane = lax.broadcasted_iota(jnp.int32, (R, HD), 1)
+    per_half = half // HD
+
+    def attend_head(head):
+        at = pl.ds(pl.multiple_of(head * HD, HD), HD)
+        base = (head // per_half) * width + (head % per_half) * HD
+        ats = [pl.ds(pl.multiple_of(base + index * half, HD), HD) for index in range(3)]
+        dk[...] = jnp.zeros_like(dk)
+        dv[...] = jnp.zeros_like(dv)
+
+        @pl.loop(0, T)
+        def _(piece):
+            where = pl.ds(pl.multiple_of(piece * R, R), R)
+            queries, keys, values = qkv[0, where, at], qkv[1, :, at], qkv[2, :, at]
+            grads = d_context[where, at]
+            scores = dot(queries, keys, NT) * HD ** (-0.5)
+            same = label_column[where, :] == label_row[...]
+            log_total = jnp.sum(jnp.where(lane == head, lse[where, :], 0.0), axis=-1, keepdims=True)
+            probs = jnp.exp(jnp.where(same, scores, NEG) - log_total)
+            d_probs = dot(grads, values, NT)
+            inner_sum = jnp.sum(probs * d_probs, axis=-1, keepdims=True)
+            d_scores = (probs * (d_probs - inner_sum)).astype(BF16)
+            dqkv[where, ats[0]] = (dot(d_scores, keys) * HD ** (-0.5)).astype(BF16)
+            dk[...] += dot(d_scores, queries, TN)
+            dv[...] += dot(probs.astype(BF16), grads, TN)
+
+        dqkv[:, ats[1]] = (dk[...] * HD ** (-0.5)).astype(BF16)
+        dqkv[:, ats[2]] = dv[...].astype(BF16)
+
+    count = C // HD
+
+    @pl.loop(0, count // 2)
+    def _(head):
+        attend_head(head)
+
+    for level in up.levels():
+        up.advance(adder, level)
+    for level in outer.levels():
+        outer.advance(adder, level)
+
+    @pl.loop(count // 2, count)
+    def _(head):
+        attend_head(head)
+
+    down.finish(adder)
+    loaded("rows")
+    loaded("weights")
+
+    def rows_tile(m, index):
+        at = pl.ds(pl.multiple_of(m * wide, wide), wide)
+        return dot(dqkv[pl.ds(index * R, R), :], wbuf[at, pl.ds(0, 2 * width)], NT)
+
+    def rows_put(m, value):
+        at = pl.ds(pl.multiple_of(m * wide, wide), wide)
+        rows[pl.ds(0, R), at] = (value + dfs[:, at]).astype(BF16)
+
+    for step in range(1, n):
+        act.reduce_step(step, rows_tile, rows_put)
+    for m in piece_order():
+        store(
+            6,
+            lambda i, m=m: dot(
+                abuf[:, pl.ds(m * wide, wide)],
+                dqkv[:, pl.ds(pl.multiple_of(i * half, half), half)],
+                TN,
+            ),
+            lambda i, m=m: grad_x.at[
+                i // 3, pl.ds(m * wide, wide), pl.ds(pl.multiple_of((i % 3) * half, half), half)
+            ],
+        )
+        inner.ready(m)
+    for e in range(2):
+        for index, part in enumerate((0, 2)):
+            at = pl.ds(e * width + part * half, half)
+            value = jnp.sum(dqkv[:, at].astype(F32), axis=0, keepdims=True)
+            to = pl.ds(index * half, half)
+            line = lax.broadcasted_iota(jnp.int32, (2 * T, half), 0)
+            small_q[:, to] = jnp.where(line == places[e], value, small_q[:, to])
+    act.reduce_step(0, rows_tile, rows_put)
+    act.reduce_end()
+    input_done = trade(rows.at[pl.ds(0, R), :], input_grad)
+
+    smalls = ((small_d, got_d), (small_q, got_q), (small_u, got_u))
+    rounds = [[k.along(step) for step in range(1, n)]] if n > 1 else []
+    rounds += [[k.mate()], [k.across()]]
+    mask = 1
+    while mask < planes:
+        rounds.append([k.plane(mask)])
+        mask *= 2
+    small_slot = k.slots(3 * (n + 1 + planes))
+    turn = [0]
+
+    def small_round():
+        if not rounds:
+            return
+        copies = []
+        for peer in rounds.pop(0):
+            group = []
+            for index, (mine, other) in enumerate(smalls):
+                copy = k.copy(small_slot + 3 * turn[0] + index, mine, other.at[turn[0]], peer)
+                copy.start()
+                group.append((copy, mine, other.at[turn[0]]))
+            turn[0] += 1
+            copies += group
+        for copy, mine, other in copies:
+            copy.wait()
+        for copy, mine, other in copies:
+            mine[...] += other[...]
+
+    small_round()
+    for level in inner.levels():
+        inner.advance(adder, level)
+    small_round()
+    up.finish(adder)
+    small_round()
+    outer.finish(adder)
+    while rounds:
+        small_round()
+    inner.finish(adder)
+    homes = [
+        local.start(work.home(0, k.c), work.last.at[0]) for work in (down, up, outer, inner)
+    ]
+    layer_done()
+    input_done()
+    for work in (down, up, outer, inner):
+        work.arrive()
+    for copy in homes:
+        copy.wait()
+    for copy in k.sent:
+        copy.wait_send()
+
+
+def backward(size, arrays):
+    R, D, L, T = size.rows, size.dim, size.length, size.tp
+    P_, n, wide, half, uhalf = size.planes, size.n, size.wide, size.half, size.uhalf
+    C, U, fine = size.heads, size.units, size.fine
+    width = 3 * half
+    bits = P_.bit_length() - 1
+    rounds = 2 + bits + n - 1
+    shape = jax.ShapeDtypeStruct
+    m = max(P_ - 1, 1)
+    outs = [
+        shape((R, D), BF16),
+        shape((R, D), BF16),
+        shape((P_, U, wide), BF16),
+        shape((2, D, uhalf), BF16),
+        shape((P_, C, wide), BF16),
+        shape((2, D, width), BF16),
+        shape((m, 2, uhalf, wide), BF16),
+        shape((m, 2, wide, uhalf), BF16),
+        shape((m, 2, half, wide), BF16),
+        shape((m, 2, wide, width), BF16),
+        shape((4, uhalf, fine), BF16),
+        shape((4, fine, uhalf), BF16),
+        shape((4, half, fine), BF16),
+        shape((4, fine, width), BF16),
+    ]
+    smalls = [
+        shape((P_, 8, wide), F32),
+        shape((2 * T, 2 * half), F32),
+        shape((2 * T, uhalf), F32),
+    ]
+    anywhere = pl.BlockSpec(memory_space=pl.ANY)
+    vmem = pl.BlockSpec(memory_space=pltpu.VMEM)
+    tall, broad = max(U, D), max(D, 2 * width)
+    slots = 2 * n + 2 * n * P_ + 4 * (2 * P_ + 1) + 2 * P_ + 3 * (n + 1 + P_)
+    far = max(n - 1, 1) * P_
+    tile = (max(min(512, U), wide, C), max(wide, min(512, uhalf), half))
+    scratch = [
+        pltpu.VMEM((L, D), BF16),
+        pltpu.VMEM((tall, broad), BF16),
+        pltpu.VMEM((D, U), BF16),
+        pltpu.VMEM((P_, C, wide), BF16),
+        pltpu.VMEM((L, max(U, D)), BF16),
+        pltpu.VMEM((L, U), BF16),
+        pltpu.VMEM((3, L, C), BF16),
+        pltpu.VMEM((L, 3 * C), BF16),
+        pltpu.VMEM((L, C), BF16),
+        pltpu.VMEM((L, C), BF16),
+        pltpu.VMEM((L, HD), F32),
+        pltpu.VMEM((P_, R, wide), BF16),
+        pltpu.VMEM((n * P_, R, wide), BF16),
+        pltpu.VMEM((far, R, wide), BF16),
+        pltpu.VMEM((far, R, wide), BF16),
+        pltpu.VMEM((R, D), F32),
+        pltpu.VMEM((L, HD), F32),
+        pltpu.VMEM((L, HD), F32),
+        pltpu.VMEM((2,) + tile, BF16),
+        pltpu.VMEM((2, bits + 1, wide, min(256, half, uhalf)), BF16),
+        pltpu.VMEM((2, bits + 1, min(256, half, uhalf), wide), BF16),
+        pltpu.VMEM((rounds, P_, 8, wide), F32),
+        pltpu.VMEM((rounds, 2 * T, 2 * half), F32),
+        pltpu.VMEM((rounds, 2 * T, uhalf), F32),
+        pltpu.VMEM((8, D), F32),
+        pltpu.VMEM((8, D), F32),
+        pltpu.SemaphoreType.DMA((slots,)),
+        pltpu.SemaphoreType.DMA((slots,)),
+        pltpu.SemaphoreType.DMA((32 + 3 * P_,)),
+        pltpu.SemaphoreType.DMA((2,)),
+        pltpu.SemaphoreType.DMA((2, bits + 1)),
+        pltpu.SemaphoreType.REGULAR,
+    ]
+    return pl.pallas_call(
+        functools.partial(backward_kernel, size),
+        out_shape=outs + smalls,
+        in_specs=[anywhere] * 13 + [vmem, vmem, anywhere, anywhere] + [vmem] * 4,
+        out_specs=[anywhere] * 14 + [vmem] * 3,
+        scratch_shapes=scratch,
+        compiler_params=pltpu.CompilerParams(
+            collective_id=1, has_side_effects=True, vmem_limit_bytes=VMEM
+        ),
+        name="backward",
     )(*arrays)
 
 
@@ -874,31 +1356,26 @@
     segments,
     cotangent,
 ):
-    lay = Layout(fsdp, tp)
-    length = segments.shape[1]
-    local = query_weight.shape[1] // HD
-    rows_own = inputs.shape[0]
-
-    def heads(table):
-        return table.reshape(length, local, HD)
-
     size = Sizes(fsdp, tp, inputs, query_weight, up_weight, segments)
-    residual_vectors = jnp.stack(
-        [output_bias, first_gain, first_shift, down_bias, second_gain, second_shift] + [output_bias] * 2
+    f, t = lax.axis_index("fsdp"), lax.axis_index("tp")
+    c = f % 2
+    residual = jnp.stack(
+        [output_bias, first_gain, first_shift, down_bias, second_gain, second_shift]
+        + [output_bias] * 2
     )
-    residual_vectors = residual_vectors.reshape(8, size.planes, size.wide).transpose(1, 0, 2)
+    residual = residual.reshape(8, size.planes, size.wide).transpose(1, 0, 2)
     role_bias = jnp.concatenate(
         [v.reshape(2, -1) for v in (query_bias, value_bias, up_bias)], axis=1
     )[:, None]
-    results = forward(
+    kept = forward(
         size,
         (
             inputs,
             cotangent,
-            segments.reshape(tp, 1, rows_own),
-            segments.reshape(length, 1),
+            segments.reshape(tp, 1, size.rows),
+            segments.reshape(size.length, 1),
             role_bias,
-            residual_vectors,
+            residual,
             query_weight,
             key_weight,
             value_weight,
@@ -907,117 +1384,48 @@
             down_weight,
         ),
     )
-    query_full, key_full, value_full, up_full = (
-        jnp.concatenate([results[i][0], results[i][1]], axis=1) for i in (0, 1, 2, 4)
-    )
-    output_full, down_full = (
-        results[i].transpose(1, 0, 2).reshape(results[i].shape[1], -1) for i in (3, 5)
-    )
-    rows_all, (query, keys, value), context, log_total, mid_all, pre, hidden = results[6:13]
-    first_normed, first_inv, final, d_second, sums = results[13:]
-    log_total = log_total[:, :local].T
-    layer_out = lay.relative(lay.trade(final))
-    down_bias_term, second_gain_term, second_shift_term = sums[0], sums[1], sums[2]
-    first_gain = lay.relative(first_gain)
-    gelu_back = jax.vjp(gelu_tanh, pre.astype(F32))[1]
-    labels = jnp.where(lay.c == lay.h, segments[0], lay.core(segments[0]))
-    label_parts = []
-    for step in range(lay.n):
-        for core in (lay.c, 1 - lay.c):
-            at = (core * lay.n + (lay.l + lay.n - step) % lay.n) * rows_own
-            label_parts.append(lax.dynamic_slice_in_dim(labels, at, rows_own))
-    labels = jnp.concatenate(label_parts)
-
-    def rows_at(table, step):
-        return table[2 * rows_own * step : 2 * rows_own * (step + 1)]
-
-    d_branch_all = lay.gather(d_second.astype(BF16))
-    d_hidden = against(d_branch_all, down_full)
-    d_pre = gelu_back(d_hidden)[0].astype(BF16)
-    up_bias_term = jnp.sum(d_pre.astype(F32), axis=0)
-    d_mid = lay.reduce(lambda step: against(rows_at(d_pre, step), up_full))
-    down_term = across(hidden, d_branch_all)
-    up_term = across(mid_all, d_pre)
-    down_grad = lay.collect(down_term, 1)
-    up_grad = lay.collect(up_term, 0)
-    d_first = d_mid + d_second
-    d_first_sum, first_gain_term, first_shift_term = norm_back(
-        d_first, first_normed, first_inv, first_gain
-    )
-    output_bias_term = jnp.sum(d_first_sum, axis=0)
-    d_attn_all = lay.gather(d_first_sum.astype(BF16))
-    d_context = against(d_attn_all, output_full).astype(BF16)
-    output_term = across(context, d_attn_all)
-    output_grad = lay.collect(output_term, 1)
-    d_query, d_key, d_value = (
-        v.reshape(length, local * HD)
-        for v in attend_back(
-            heads(query), heads(keys), heads(value), heads(d_context), log_total, labels
+    results = backward(size, tuple(kept) + (residual,))
+    layer_out, input_grad = results[:2]
+    last_d, last_u, last_o, last_x, small_d, small_q, small_u = results[10:]
+
+    def owned(last, axis):
+        mine = last[0].astype(F32) + last[2].astype(F32)
+        other = last[1].astype(F32) + last[3].astype(F32)
+        return jnp.where(
+            c == 0,
+            jnp.concatenate([mine, other], axis=axis),
+            jnp.concatenate([other, mine], axis=axis),
         )
-    )
-    query_bias_term = jnp.sum(d_query.astype(F32), axis=0)
-    value_bias_term = jnp.sum(d_value.astype(F32), axis=0)
-    d_rows = lay.reduce(
-        lambda step: against(rows_at(d_query, step), query_full)
-        + against(rows_at(d_key, step), key_full)
-        + against(rows_at(d_value, step), value_full)
-    )
-    input_grad = lay.relative(lay.trade((d_rows + d_first_sum).astype(BF16)))
-    query_grad = lay.collect(across(rows_all, d_query), 0)
-    key_grad = lay.collect(across(rows_all, d_key), 0)
-    value_grad = lay.collect(across(rows_all, d_value), 0)
-
-    def small(terms):
-        total = lax.psum(jnp.concatenate(terms), AXES)
-        result, at = [], 0
-        for term in terms:
-            result.append(total[at : at + term.shape[0]])
-            at += term.shape[0]
-        return result
-
-    f, t = lax.axis_index("fsdp"), lax.axis_index("tp")
-
-    def residual(vector):
-        size = vector.shape[0] // (fsdp * tp)
-        return lax.dynamic_slice_in_dim(vector, (f * tp + t) * size, size)
-
-    def split(vector):
-        size = vector.shape[0] // (fsdp * tp)
-        return lax.dynamic_slice_in_dim(vector, (t * fsdp + f) * size, size)[None]
-
-    early = small(
-        [
-            lay.relative(v)
-            for v in (
-                down_bias_term,
-                second_gain_term,
-                second_shift_term,
-                output_bias_term,
-                first_gain_term,
-                first_shift_term,
-            )
-        ]
-        + [lay.unrole(up_bias_term)]
-    )
-    late = small([lay.unrole(query_bias_term), lay.unrole(value_bias_term)])
+
+    half = size.half
+    inner = [owned(last_x[:, :, i * half : (i + 1) * half], 1) for i in range(3)]
+    small_d = small_d.transpose(1, 0, 2).reshape(8, size.dim)
+    residual_size = size.dim // (fsdp * tp)
+    ends = lax.dynamic_slice(small_d, (0, (f * tp + t) * residual_size), (8, residual_size))
+
+    def split(table):
+        row = lax.dynamic_slice_in_dim(table, 2 * t, 2).reshape(1, -1)
+        part = row.shape[1] // fsdp
+        return lax.dynamic_slice_in_dim(row, f * part, part, axis=1)
+
     return (
         layer_out,
         input_grad,
-        query_grad,
-        split(late[0]),
-        key_grad,
-        value_grad,
-        split(late[1]),
-        output_grad,
-        residual(early[3]),
-        residual(early[4]),
-        residual(early[5]),
-        up_grad,
-        split(early[6]),
-        down_grad,
-        residual(early[0]),
-        residual(early[1]),
-        residual(early[2]),
+        inner[0],
+        split(small_q[:, :half]),
+        inner[1],
+        inner[2],
+        split(small_q[:, half:]),
+        owned(last_o, 0),
+        ends[3],
+        ends[4],
+        ends[5],
+        owned(last_u, 1),
+        split(small_u),
+        owned(last_d, 0),
+        ends[0],
+        ends[1],
+        ends[2],
     )
 
 

time: 1010 us -> 779 us (0.77)
  Pallas kernels: 338 us -> 745 us
  waiting for transfers between devices: 218 us -> 0 us
  matrix products: 136 us -> 0 us
  local copies, waits for them, and re-layouts: 92.7 us -> 13.2 us
  other arithmetic: 88.2 us -> 8.83 us
  starting transfers between devices: 65.5 us -> 0 us
  blocking collectives: 41.1 us -> 0 us
  between operations: 15.7 us -> 1.22 us
    pallas_call x0 -> x1, Pallas kernels: none -> 401 us  [backward(): pl.pallas_call(functools.partial(backward_kernel, size), out_shape=outs +...]
    dot_general x21 -> x0, matrix products: 136 us -> none  [the longest x6 48.3 us: across(): lax.dot_general(left, right, (((0,), (0,)), ((), ())), preferred_element_...]
    psum x1 -> x0, waiting for transfers between devices: 121 us -> none  [small(): total = lax.psum(jnp.concatenate(terms), AXES)]
    ppermute x51 -> x0, waiting for transfers between devices: 96.6 us -> none  [move(): return lax.ppermute(value, AXES, pairs)]
    ppermute x51 -> x0, starting transfers between devices: 65.4 us -> none  [move(): return lax.ppermute(value, AXES, pairs)]
    convert_element_type x24 -> x0, other arithmetic: 41.4 us -> none  [the longest x12 15.7 us: collect(): both = self.plane(both, m).astype(F32)]
    psum x1 -> x0, blocking collectives: 41.1 us -> none  [small(): total = lax.psum(jnp.concatenate(terms), AXES)]
    concatenate x23 -> x0, other arithmetic: 20.3 us -> none  [the longest x12 12 us: collect(): both = jnp.concatenate([v.astype(BF16) for v in total[m]], axis=axis)]
  transfers between devices with their start and end apart: 52 -> 0, of which waited for: 15 -> 0; matrix products, arithmetic and copies ran while one was open for 26% -> 0% of each run, Pallas kernels for 0% -> 0%
where the time goes in v3:
time: 779 us; the launch traced here: 768 us
  Pallas kernels  745 us (96%)
  local copies, waits for them, and re-layouts  13.2 us (2%)
  other arithmetic  8.83 us (1%)
    pallas_call x1, Pallas kernels, backward(): pl.pallas_call(functools.partial(backward_kernel, size), out_shape=outs +...  401 us
    pallas_call x1, Pallas kernels, forward(): pl.pallas_call(functools.partial(forward_kernel, size), out_shape=whole +...  344 us

profile of v3, /device:TPU:1, one launch (start us, length us, event | category | flops | bytes accessed | tf_op | source)
XLA Modules:
  0.0 768.3 jit_solution(15919530435527314599)
XLA Ops:
  0.7 1.5 stack.29
  2.2 1.7 copy.35.refs_3_
  3.9 0.7 reshape.118
  4.6 0.7 reshape.116
  5.3 0.7 reshape.117
  6.0 0.6 broadcast_in_dim.3.refs_4_
  6.6 344.3 %forward.1 = (bf16[2,2048,256]{2,1,0:T(8,128)(2,1)}, bf16[2,2048,256]{2,1,0:T(8,128)(2,1)}, bf16[2,2048,256]{2,1,0:T(8,128)(2,1)}, bf16[4,512,512]{2,1,0:T(8,128...) custom-call(bf16[256,2048]{1,0:T(8,128)(2,1)} %refs_0_.1, ...), custom_call_target="tpu_custom_call" | custom-call | tf_op jit(solution)/shard_map/forward/pallas_call | solution.py:661
  350.9 400.8 %backward.1 = (bf16[256,2048]{1,0:T(8,128)(2,1)}, bf16[256,2048]{1,0:T(8,128)(2,1)}, bf16[4,2048,512]{2,1,0:T(8,128)(2,1)}, bf16[2,2048,1024]{2,1,0:T(8,128)(2,1...) custom-call(bf16[2,2048,256]{2,1,0:T(8,128)(2,1)} %get-tuple-element, ...), custom_call_target="tpu_custom_call" | custom-call | tf_op jit(solution)/shard_map/backward/pallas_call | solution.py:1324
  751.7 1.7 add_bitcast_fusion.1
  753.5 0.0 copy-start
  753.5 1.6 maximum_select_fusion.1
  755.0 0.8 copy-done
  755.8 0.4 add_bitcast_fusion.3
  756.2 0.0 copy-start.1
  756.2 0.0 copy-start.4
  756.2 1.6 maximum_select_fusion
  757.8 0.3 copy-done.1
  758.1 0.4 copy-done.4
  758.5 0.2 add_bitcast_fusion.5
  758.7 0.0 copy-start.5
  758.7 0.0 copy-start.3
  758.7 0.8 maximum_select_fusion.5
  759.6 0.8 maximum_select_fusion.4
  760.4 0.0 copy-start.2
  760.4 0.8 maximum_select_fusion.3
  761.2 0.0 copy-done.5
  761.2 0.6 constant_dynamic-slice_fusion.2
  761.8 0.6 constant_dynamic-slice_fusion.3
  762.4 0.8 maximum_select_fusion.2
  763.3 0.8 dynamic-slice_bitcast_fusion
  764.0 0.6 constant_dynamic-slice_fusion
  764.6 0.7 constant_dynamic-slice_fusion.1
  765.3 0.5 slice_bitcast_fusion
  765.9 0.0 copy-done.3
  765.9 1.0 copy.41
  766.9 0.0 copy-done.2
  766.9 1.0 copy.42
  (6 shorter events, 0.0 us)
Async XLA Ops:
  753.5 2.3 copy-start
  756.2 1.9 copy-start.1
  756.2 2.3 copy-start.4
  758.7 2.5 copy-start.5
  758.7 7.2 copy-start.3
  760.4 6.5 copy-start.2
